TPU v7x, 32 devices: a whole 2x2x4 slice. The times are simulated.
32 devices in a mesh: band: 4 (over x, core), crop: 8 (over z, y).
Axes of the slice: x: 2, y: 2, z: 4, core: 2. Of those that a mesh axis runs over, the one named last changes fastest.
Arguments:
- patches: bfloat16 [8, 1776, 768], P('crop', 'band'), may hold values from -6 to 6
- specials: bfloat16 [8, 5, 768], P('crop'), may hold values from -6 to 6
- patch_mask: int32 [8, 1776], P('crop', 'band'), may hold values from 0 to 1, as said below
- band_rows: int32 [4], replicated, may hold values from 1 to 12, as said below
- mask_token: float32 [768], replicated, may hold values from -5 to 5
- first_gain: float32 [768], replicated, may hold values from 0.5 to 1.5
- first_shift: float32 [768], replicated, may hold values from -3 to 3
- joint_weight: bfloat16 [768, 2304], replicated, may hold values from -0.21875 to 0.21875
- query_bias: float32 [768], replicated, may hold values from -3 to 3
- value_bias: float32 [768], replicated, may hold values from -3 to 3
- out_weight: bfloat16 [768, 768], replicated, may hold values from -4 to 4
- out_bias: float32 [768], replicated, may hold values from -3 to 3
- first_scale: float32 [768], replicated, may hold values from 0.25 to 1
- second_gain: float32 [768], replicated, may hold values from 0.5 to 1.5
- second_shift: float32 [768], replicated, may hold values from -3 to 3
- up_weight: bfloat16 [768, 3072], replicated, may hold values from -0.21875 to 0.21875
- up_bias: float32 [3072], replicated, may hold values from -3 to 3
- down_weight: bfloat16 [3072, 768], replicated, may hold values from -0.109375 to 0.109375
- down_bias: float32 [768], replicated, may hold values from -3 to 3
- second_scale: float32 [768], replicated, may hold values from 0.25 to 1
- cot_patches: bfloat16 [8, 1776, 768], P('crop', 'band'), may hold values from -6 to 6
- cot_specials: bfloat16 [8, 5, 768], P('crop'), may hold values from -6 to 6
Outputs:
- out_patches: bfloat16 [8, 1776, 768], P('crop', 'band')
- out_specials: bfloat16 [8, 5, 768], P('crop')
- grad_patches: bfloat16 [8, 1776, 768], P('crop', 'band')
- grad_specials: bfloat16 [8, 5, 768], P('crop')
- mask_token_grad: float32 [768], P('crop')
- first_gain_grad: float32 [768], P('crop')
- first_shift_grad: float32 [768], P('crop')
- joint_weight_grad: float32 [768, 2304], P('crop')
- query_bias_grad: float32 [768], P('crop')
- value_bias_grad: float32 [768], P('crop')
- out_weight_grad: float32 [768, 768], P('crop')
- out_bias_grad: float32 [768], P('crop')
- first_scale_grad: float32 [768], P('crop')
- second_gain_grad: float32 [768], P('crop')
- second_shift_grad: float32 [768], P('crop')
- up_weight_grad: float32 [768, 3072], P('crop')
- up_bias_grad: float32 [3072], P('crop')
- down_weight_grad: float32 [3072, 768], P('crop')
- down_bias_grad: float32 [768], P('crop')
- second_scale_grad: float32 [768], P('crop')
Inputs may be any that keep to these rules, and one draw needn't show every extreme that they name: `band_rows`: the bands' rows add up to 37, and one band holds exactly 12. `patch_mask`: masked patches form rectangular blocks.
All inputs are finite; a program needn't handle non-finite values.
Results may differ from a plain program's by a relative error of at most 0.028.
Values may be sent and summed in bfloat16 or wider, within the bound.
A program may use at most 192 MiB of HBM per device.

v0:
```python
from functools import partial

import jax
import jax.numpy as jnp
from jax import lax
from jax.experimental import pallas as pl
from jax.experimental.pallas import tpu as pltpu
from jax.sharding import PartitionSpec as P

HEAD = 64
GRID = 37
PAIR = 2 * HEAD
BANDS = 4
F32 = jnp.float32
BF16 = jnp.bfloat16
VMEM_LIMIT = 56 << 20


def round_up(value, unit):
    return (value + unit - 1) // unit * unit


def params(semantics=None):
    return pltpu.CompilerParams(vmem_limit_bytes=VMEM_LIMIT)


def dot(a, b):
    return jnp.dot(a, b, preferred_element_type=F32)


def dot_nt(a, b):
    return lax.dot_general(a, b, (((1,), (1,)), ((), ())), preferred_element_type=F32)


def dot_tn(a, b):
    return lax.dot_general(a, b, (((0,), (0,)), ((), ())), preferred_element_type=F32)


def normalize(rows):
    centred = rows - jnp.mean(rows, axis=-1, keepdims=True)
    spread = jnp.mean(centred * centred, axis=-1, keepdims=True)
    scale = lax.rsqrt(spread + 1e-06)
    return centred * scale, scale


def normalize_back(grad, hat, scale):
    return scale * (
        grad
        - jnp.mean(grad, axis=-1, keepdims=True)
        - hat * jnp.mean(grad * hat, axis=-1, keepdims=True)
    )


def column_sum(rows):
    return jnp.sum(rows, axis=0, keepdims=True)


def line(ref):
    return ref[...].reshape(1, -1)


def whole(shape):
    return pl.BlockSpec(shape, lambda *_: (0,) * len(shape))


VMEM = pl.BlockSpec(memory_space=pltpu.VMEM)
ANY = pl.BlockSpec(memory_space=pl.ANY)
SMEM = pl.BlockSpec(memory_space=pltpu.SMEM)


def own_special(specials, band, slot):
    row = jnp.zeros((1, specials.shape[1]), F32)
    for special in range(specials.shape[0]):
        if special // BANDS == slot:
            row = row + jnp.where(band == special % BANDS, specials[special : special + 1], 0.0)
    return row


def place_rows(ref, patch_rows, specials, band):
    slots = patch_rows.shape[0]
    rows = ref.shape[0]
    ref[0:slots, :] = patch_rows
    extra = [own_special(specials, band, slot) for slot in range(rows - slots)]
    ref[slots:rows, :] = jnp.concatenate(extra, axis=0)


def counted_rows(info_ref, relative, rows, slots, width):
    index = lax.broadcasted_iota(jnp.int32, (rows, width), 0)
    used = index < info_ref[relative]
    special = (index >= slots) & (index < slots + info_ref[BANDS + relative])
    return used | special


def stack_pair(rows):
    lane = lax.broadcasted_iota(jnp.int32, rows.shape, 1)
    zero = jnp.zeros_like(rows)
    return jnp.concatenate(
        [jnp.where(lane < HEAD, rows, zero), jnp.where(lane >= HEAD, rows, zero)], axis=0
    )


def unstack_pair(rows):
    half = rows.shape[0] // 2
    lane = lax.broadcasted_iota(jnp.int32, (half, rows.shape[1]), 1)
    return jnp.where(lane < HEAD, rows[:half], rows[half:])


def mask_column(mask):
    return jnp.broadcast_to(mask[...].astype(F32), (8, mask.shape[1])).T[:, :1] > 0


def first_kernel(info, mask, patches, specials, token, gain, shift, tokens, first):
    band = info[2 * BANDS]
    filled = jnp.where(mask_column(mask), line(token), patches[...].astype(F32))
    place_rows(tokens, filled, specials[...].astype(F32), band)
    hat, _ = normalize(tokens[...])
    first[...] = (hat * line(gain) + line(shift)).astype(BF16)


def project_kernel(slots, info, first, weight, query_bias, value_bias, queries, keys, values):
    relative = pl.program_id(0)
    rows, width = queries.shape
    counted = counted_rows(info, relative, rows, slots, width)
    low = first[...]

    @pl.when(relative == 0)
    def _():
        queries[...] = (dot(low, weight[:, :width]) + line(query_bias)).astype(BF16)

    keys[...] = jnp.where(counted, dot(low, weight[:, width : 2 * width]), 0.0).astype(BF16)
    values[...] = jnp.where(
        counted, dot(low, weight[:, 2 * width :]) + line(value_bias), 0.0
    ).astype(BF16)


def attend_kernel(slots, info, queries, keys, values, attended, totals, weights):
    rows = queries.shape[0]
    factor = HEAD ** (-0.5)
    stacked = stack_pair((queries[...].astype(F32) * factor).astype(BF16))
    scores = dot_nt(stacked, keys[...])
    low = jnp.exp(scores).astype(BF16)
    weights[0] = low
    ones = jnp.concatenate(
        [
            counted_rows(info, r, rows, slots, PAIR).astype(F32).astype(BF16)
            for r in range(BANDS)
        ],
        axis=0,
    )
    summed = dot(low, jnp.concatenate([values[...], ones], axis=1))
    total = unstack_pair(summed[:, PAIR:])
    attended[...] = unstack_pair(summed[:, :PAIR]) / total
    totals[...] = total


def middle_kernel(
    slots,
    info,
    attended,
    tokens,
    weight,
    bias,
    first_scale,
    gain,
    shift,
    second_scale,
    cot_patches,
    cot_specials,
    branch,
    middle,
    second,
    incoming,
    down_in,
    down_bias_grad,
):
    rows = tokens.shape[0]
    band = info[2 * BANDS]
    side = dot(attended[...].astype(BF16), weight[...]) + line(bias)
    branch[...] = side
    mid = tokens[...] + line(first_scale) * side
    middle[...] = mid
    hat, _ = normalize(mid)
    second[...] = (hat * line(gain) + line(shift)).astype(BF16)
    counted = counted_rows(info, 0, slots, slots, tokens.shape[1])
    given = jnp.where(counted, cot_patches[...].astype(F32), 0.0)
    place_rows(incoming, given, cot_specials[...].astype(F32), band)
    low = (incoming[...] * line(second_scale)).astype(BF16)
    down_in[...] = low
    down_bias_grad[...] = column_sum(low.astype(F32))


def gelu_and_slope(x):
    phi = 0.5 + 0.5 * lax.erf(x * 0.7071067811865476)
    density = jnp.exp(-0.5 * x * x) * 0.3989422804014327
    return x * phi, phi + x * density


def mlp_kernel(
    second, down_in, up, up_bias, down, branch_two, second_grad, up_grad, up_bias_grad, down_grad
):
    step = pl.program_id(0)
    low = second[...]
    grad = down_in[...]
    hidden = dot(low, up[...]) + up_bias[...]
    active, slope = gelu_and_slope(hidden)
    active = active.astype(BF16)
    hidden_in = (slope * dot_nt(grad, down[...])).astype(BF16)

    @pl.when(step == 0)
    def _():
        branch_two[...] = jnp.zeros_like(branch_two)
        second_grad[...] = jnp.zeros_like(second_grad)

    branch_two[...] += dot(active, down[...])
    second_grad[...] += dot_nt(hidden_in, up[...])
    up_grad[...] = dot_tn(low, hidden_in).astype(BF16)
    down_grad[...] = dot_tn(active, grad).astype(BF16)
    up_bias_grad[...] = column_sum(hidden_in.astype(F32))


def middle_back_kernel(
    slots,
    info,
    middle,
    branch,
    branch_two,
    second_grad,
    incoming,
    attended,
    weight,
    down_bias,
    second_scale,
    gain,
    first_scale,
    out_patches,
    out_specials,
    middle_grad,
    attended_grad,
    weight_grad,
    vectors,
):
    rows = middle.shape[0]
    mid = middle[...]
    given = incoming[...]
    two = branch_two[...] + line(down_bias)
    output = mid + line(second_scale) * two
    counted = counted_rows(info, 0, slots, slots, mid.shape[1])
    out_patches[...] = jnp.where(counted, output[:slots], 0.0).astype(BF16)
    out_specials[...] = output[slots:]
    hat, scale = normalize(mid)
    grad = second_grad[...]
    back = given + normalize_back(grad * line(gain), hat, scale)
    middle_grad[...] = back
    out_in = (back * line(first_scale)).astype(BF16)
    attended_grad[...] = dot_nt(out_in, weight[...])
    weight_grad[...] = dot_tn(attended[...].astype(BF16), out_in).astype(BF16)
    vectors[...] = jnp.concatenate(
        [
            column_sum(given * two),
            column_sum(grad * hat),
            column_sum(grad),
            column_sum(back * branch[...]),
            column_sum(out_in.astype(F32)),
            jnp.zeros((3, mid.shape[1]), F32),
        ],
        axis=0,
    )


def attend_back_kernel(
    slots,
    info,
    weights,
    queries,
    keys,
    values,
    attended,
    totals,
    attended_grad,
    query_grad,
    key_grad,
    value_grad,
):
    rows = queries.shape[0]
    factor = HEAD ** (-0.5)
    stacked = stack_pair((queries[...].astype(F32) * factor).astype(BF16))
    inverse = 1.0 / totals[...]
    scaled = attended_grad[...] * inverse
    returned = stack_pair(scaled.astype(BF16))
    product = scaled * attended[...]
    slope = jnp.sum(stack_pair(product), axis=1, keepdims=True)
    stacked_t = stacked.astype(F32).T.astype(BF16)
    returned_t = returned.astype(F32).T.astype(BF16)
    total = jnp.zeros((2 * rows, PAIR), F32)
    for block in range(BANDS):
        span = slice(block * rows, (block + 1) * rows)
        counted = counted_rows(info, block, rows, slots, PAIR)
        low = weights[0, :, span]
        moved = dot_nt(returned, values[span, :])
        scores = (low.astype(F32) * (moved - slope)).astype(BF16)
        total = total + dot(scores, keys[span, :])
        key_part = dot(stacked_t, scores).T
        value_part = dot(returned_t, low).T
        key_grad[span, :] = jnp.where(counted, key_part, 0.0).astype(BF16)
        value_grad[span, :] = jnp.where(counted, value_part, 0.0).astype(BF16)
    query_grad[...] = (unstack_pair(total) * factor).astype(BF16)


def joint_grad_kernel(firsts, query_grad, key_grad, value_grad, weight, weight_grad, first_grad):
    rows = query_grad.shape[0]
    width = query_grad.shape[1]
    low = firsts[...]
    weight_grad[:, :width] = dot_tn(low[:rows], query_grad[...]).astype(BF16)
    weight_grad[:, width : 2 * width] = dot_tn(low, key_grad[...]).astype(BF16)
    weight_grad[:, 2 * width :] = dot_tn(low, value_grad[...]).astype(BF16)
    for block in range(BANDS):
        span = slice(block * rows, (block + 1) * rows)
        part = dot_nt(key_grad[span, :], weight[:, width : 2 * width])
        part = part + dot_nt(value_grad[span, :], weight[:, 2 * width :])
        if block == 0:
            part = part + dot_nt(query_grad[...], weight[:, :width])
        first_grad[span, :] = part.astype(BF16)


def first_back_kernel(
    slots,
    first_grad,
    tokens,
    middle_grad,
    mask,
    gain,
    query_grad,
    value_grad,
    grad_patches,
    grad_specials,
    vectors,
):
    grad = first_grad[...]
    hat, scale = normalize(tokens[...])
    token_grad = middle_grad[...] + normalize_back(grad * line(gain), hat, scale)
    masked = mask_column(mask)
    patch_grad = token_grad[:slots]
    grad_patches[...] = jnp.where(masked, 0.0, patch_grad).astype(BF16)
    grad_specials[...] = token_grad[slots:]
    vectors[...] = jnp.concatenate(
        [
            column_sum(jnp.where(masked, patch_grad, 0.0)),
            column_sum(grad * hat),
            column_sum(grad),
            column_sum(query_grad[...].astype(F32)),
            column_sum(value_grad[...].astype(F32)),
            jnp.zeros((3, grad.shape[1]), F32),
        ],
        axis=0,
    )


def swap(x, axis, distance):
    size = lax.axis_size(axis)
    return lax.ppermute(x, axis, [(i, i ^ distance) for i in range(size)])


def halve(x, axis, distance):
    bit = (lax.axis_index(axis) // distance) % 2
    sent = lax.dynamic_index_in_dim(x, 1 - bit, 0, keepdims=False)
    kept = lax.dynamic_index_in_dim(x, bit, 0, keepdims=False)
    got = swap(sent, axis, distance)
    return (kept.astype(F32) + got.astype(F32)).astype(BF16)


def reduce_weight(partial_sum):
    rows, columns = partial_sum.shape
    crops = lax.axis_size("crop")
    half = columns // 2
    x = jnp.stack([partial_sum[:, :half], partial_sum[:, half:]])
    x = halve(x, "band", 1)
    distance = 1
    held = x.reshape((crops, rows // crops, half))
    order = []
    while distance < crops:
        order.append(distance)
        distance *= 2
    for distance in order:
        count = held.shape[0]
        held = held.reshape((count // 2, 2) + held.shape[1:])
        held = jnp.moveaxis(held, 1, 0)
        held = halve(held, "crop", distance)
    held = held.reshape((rows // crops, half))
    other = swap(held, "band", 2)
    full = (held.astype(F32) + other.astype(F32)).astype(BF16)
    mate = swap(full, "band", 1)
    bit = lax.axis_index("band") % 2
    low = jnp.where(bit == 0, full, mate).astype(F32)
    high = jnp.where(bit == 0, mate, full).astype(F32)
    return jnp.concatenate([low, high], axis=1)


def gather_blocks(x):
    near = swap(x, "band", 1)
    far = swap(x, "band", 2)
    diagonal = swap(far, "band", 1)
    return jnp.concatenate([x, near, far, diagonal], axis=0)


def scatter_blocks(x):
    rows = x.shape[0] // BANDS
    got = swap(jnp.concatenate([x[rows : 2 * rows], x[3 * rows :]], axis=0), "band", 1)
    own = x[:rows].astype(F32) + got[:rows].astype(F32)
    far = (x[2 * rows : 3 * rows].astype(F32) + got[rows:].astype(F32)).astype(BF16)
    return own + swap(far, "band", 2).astype(F32)


def reduce_general(
    up, down, out, joint, vectors, more, down_bias, up_bias, out_own, grad_own, special_count
):
    crops = lax.axis_size("crop")
    width = down.shape[1]
    owned = -(-special_count // BANDS)
    both = jnp.concatenate([out_own[:owned], grad_own[:owned]], axis=1).astype(BF16)
    both = lax.all_gather(both, "band", axis=0, tiled=False)
    both = jnp.transpose(both, (1, 0, 2)).reshape(owned * BANDS, 2 * width)[:special_count]
    plain = jnp.concatenate([vectors[:5], more[:5], down_bias], axis=0)
    plain = jnp.transpose(plain.reshape(11, crops, -1), (1, 0, 2)).reshape(crops, -1)
    packed = jnp.concatenate([plain, up_bias.reshape(crops, -1)], axis=1)
    packed = lax.psum_scatter(packed, "crop", scatter_dimension=0, tiled=False)
    packed = lax.psum(packed, "band")
    part = width // crops
    return (
        reduce_weight(up),
        reduce_weight(down),
        reduce_weight(out),
        reduce_weight(joint),
        [packed[i * part : (i + 1) * part] for i in range(11)],
        packed[11 * part :],
        both[None, :, :width],
        both[None, :, width:],
    )


MESH = pl.DeviceIdType.MESH
PLACES = ("core", "x", "diagonal", "y", "near", "far")


class Place:
    def __init__(self):
        band, crop = lax.axis_index("band"), lax.axis_index("crop")
        self.band = band
        self.core, self.x = lax.rem(band, 2), lax.div(band, 2)
        self.y, self.near, self.far = lax.rem(crop, 2), lax.rem(lax.div(crop, 2), 2), lax.div(crop, 4)
        core_step, x_step = 1 - 2 * self.core, 2 - 4 * self.x
        self.device = {
            "core": (band + core_step, crop),
            "x": (band + x_step, crop),
            "diagonal": (band + core_step + x_step, crop),
            "y": (band, crop + 1 - 2 * self.y),
            "near": (band, crop + 2 - 4 * self.near),
            "far": (band, crop + 4 - 8 * self.far),
        }

    def greet(self, names):
        barrier = pltpu.get_barrier_semaphore()
        for name in names:
            pl.semaphore_signal(barrier, inc=1, device_id=self.device[name], device_id_type=MESH)
        pl.semaphore_wait(barrier, len(names))


class Sender:
    def __init__(self, place, send_sems, recv_sems):
        self.place, self.send_sems, self.recv_sems = place, send_sems, recv_sems
        self.copies = {}

    def send(self, key, source, target, name):
        index = len(self.copies)
        copy = pltpu.make_async_remote_copy(
            src_ref=source,
            dst_ref=target,
            send_sem=self.send_sems.at[index],
            recv_sem=self.recv_sems.at[index],
            device_id=self.place.device[name],
            device_id_type=MESH,
        )
        copy.start()
        self.copies[key] = copy

    def arrived(self, key):
        self.copies[key].wait_recv()

    def finish(self):
        for copy in self.copies.values():
            copy.wait_send()


def chunk_list(hidden_parts):
    chunks = []
    for part in range(hidden_parts):
        chunks += [("down", part), ("up", part)]
    return chunks + [("out", 0), ("joint", 0), ("joint", 1), ("joint", 2)]


def chunk_scratch(count, rows, columns):
    unit = (rows, columns)
    return [
        pltpu.VMEM((count, 2, 2, 2, 2) + unit, BF16),
        pltpu.VMEM((count, 2, 2, 2, 2) + unit, BF16),
        pltpu.VMEM((count, 2, 2, 2) + unit, BF16),
        pltpu.VMEM((count, 2, 2) + unit, BF16),
        pltpu.VMEM((count, 2) + unit, BF16),
        pltpu.VMEM((count, 2) + unit, BF16),
    ]


class ChunkSums:
    def __init__(self, place, sender, buffers, total):
        self.place, self.sender, self.total = place, sender, total
        self.own, self.got, self.got_a, self.got_b, self.got_c, self.got_d = buffers

    def steps(self, n):
        return 7 if n % 2 == 0 else 6

    def step(self, n, stage):
        (self.even if n % 2 == 0 else self.odd)(n, stage)

    def even(self, n, stage):
        p, s, own = self.place, self.sender, self.own
        if stage == 0:
            own[n] = own[n] + self.got[n]
            s.send((n, 1), own.at[n, 1 - p.x], self.got_a.at[n], "x")
        elif stage == 1:
            s.arrived((n, 1))
            own[n, p.x] = own[n, p.x] + self.got_a[n]
            s.send((n, 2), own.at[n, p.x, :, :, 1 - p.y], self.got_b.at[n], "y")
        elif stage == 2:
            s.arrived((n, 2))
            own[n, p.x, :, :, p.y] = own[n, p.x, :, :, p.y] + self.got_b[n]
            s.send((n, 3), own.at[n, p.x, :, 1 - p.near, p.y], self.got_c.at[n], "near")
        elif stage == 3:
            s.arrived((n, 3))
            own[n, p.x, :, p.near, p.y] = own[n, p.x, :, p.near, p.y] + self.got_c[n]
            s.send((n, 4), own.at[n, p.x, 1 - p.far, p.near, p.y], self.got_d.at[n, 0], "far")
        elif stage == 4:
            s.arrived((n, 4))
            self.total[n, p.core, p.x] = own[n, p.x, p.far, p.near, p.y] + self.got_d[n, 0]
            place = self.total.at[n, p.core, p.x]
            s.send((n, 5), place, place, "x")
        elif stage == 5:
            s.arrived((n, 5))
            place = self.total.at[n, p.core]
            s.send((n, 6), place, place, "core")
        else:
            s.arrived((n, 6))

    def odd(self, n, stage):
        p, s, own = self.place, self.sender, self.own
        if stage == 0:
            own[n] = own[n] + self.got[n]
            s.send((n, 1), own.at[n, :, :, 1 - p.y], self.got_a.at[n], "y")
        elif stage == 1:
            s.arrived((n, 1))
            own[n, :, :, p.y] = own[n, :, :, p.y] + self.got_a[n]
            s.send((n, 2), own.at[n, :, 1 - p.near, p.y], self.got_b.at[n], "near")
        elif stage == 2:
            s.arrived((n, 2))
            own[n, :, p.near, p.y] = own[n, :, p.near, p.y] + self.got_b[n]
            s.send((n, 3), own.at[n, 1 - p.far, p.near, p.y], self.got_c.at[n], "far")
        elif stage == 3:
            s.arrived((n, 3))
            own[n, p.far, p.near, p.y] = own[n, p.far, p.near, p.y] + self.got_c[n]
            s.send((n, 4), own.at[n, p.far, p.near, p.y], self.got_d.at[n], "x")
        elif stage == 4:
            s.arrived((n, 4))
            self.total[n, p.core] = own[n, p.far, p.near, p.y] + self.got_d[n]
            place = self.total.at[n, p.core]
            s.send((n, 5), place, place, "core")
        else:
            s.arrived((n, 5))


class VectorSums:
    def __init__(self, place, sender, buffers, total):
        self.place, self.sender, self.total = place, sender, total
        self.own, self.got, self.got_y, self.got_near = buffers

    def step(self, stage):
        p, s, own = self.place, self.sender, self.own
        if stage == 0:
            s.send("v0", own.at[0], self.got.at[0], "core")
        elif stage == 1:
            s.arrived("v0")
            own[1] = own[0] + self.got[0]
            s.send("v1", own.at[1], self.got.at[1], "x")
        elif stage == 2:
            s.arrived("v1")
            own[2] = own[1] + self.got[1]
            s.send("v2", own.at[2, :, :, 1 - p.y], self.got_y, "y")
        elif stage == 3:
            s.arrived("v2")
            own[2, :, :, p.y] = own[2, :, :, p.y] + self.got_y[...]
            s.send("v3", own.at[2, :, 1 - p.near, p.y], self.got_near.at[0:2], "near")
        elif stage == 4:
            s.arrived("v3")
            own[2, :, p.near, p.y] = own[2, :, p.near, p.y] + self.got_near[0:2]
            s.send("v4", own.at[2, 1 - p.far, p.near, p.y], self.got_near.at[2], "far")
        else:
            s.arrived("v4")
            self.total[...] = own[2, p.far, p.near, p.y] + self.got_near[2]


def pack_vectors(own, vectors, more, down_bias, up_bias, part):
    for crop in range(8):
        span = slice(crop * part, (crop + 1) * part)
        wide = 4 * crop * part
        rows = [vectors[0:5, span], more[0:5, span], down_bias[0:1, span]]
        rows += [up_bias[0:1, wide + j * part : wide + (j + 1) * part] for j in range(4)]
        own[0, crop // 4, crop // 2 % 2, crop % 2, 0:15, 0:part] = jnp.concatenate(rows, axis=0)


def vector_scratch():
    return [
        pltpu.VMEM((3, 2, 2, 2, 16, 128), F32),
        pltpu.VMEM((2, 2, 2, 2, 16, 128), F32),
        pltpu.VMEM((2, 2, 16, 128), F32),
        pltpu.VMEM((3, 16, 128), F32),
    ]


def weight_source(refs, chunk, columns, half, x_half):
    name, part = chunk
    ref = refs[name]
    if name == "down":
        span = pl.ds(pl.multiple_of(columns * half, 128), columns)
        if x_half is None:
            return ref.at[:, :, :, part, :, :, span]
        return ref.at[:, :, :, part, x_half, :, span]
    span = pl.ds(pl.multiple_of(2 * columns * part + columns * half, 128), columns)
    if x_half is None:
        return ref.at[:, :, :, :, :, span]
    return ref.at[:, :, :, x_half, :, span]


def reduce_kernel(
    chunks,
    up,
    down,
    out,
    joint,
    vectors,
    more,
    down_bias,
    up_bias,
    out_own,
    grad_own,
    total,
    vector_total,
    specials,
    *scratch,
):
    buffers, vector_buffers = scratch[:6], scratch[6:10]
    send_sems, recv_sems, load_sems = scratch[10:]
    count = len(chunks)
    columns = total.shape[4]
    part = 2 * total.shape[3]
    place = Place()
    sender = Sender(place, send_sems, recv_sems)
    sums = ChunkSums(place, sender, buffers, total)
    vector_sums = VectorSums(place, sender, vector_buffers, vector_total)
    refs = dict(up=up, down=down, out=out, joint=joint)
    loads = []
    for n, chunk in enumerate(chunks):
        pieces = [0, 1] if n % 2 == 0 else [None]
        copies = []
        for i, piece in enumerate(pieces):
            target = sums.own.at[n] if piece is None else sums.own.at[n, piece]
            source = weight_source(refs, chunk, columns, place.core, piece)
            copy = pltpu.make_async_copy(source, target, load_sems.at[n, i])
            copy.start()
            copies.append(copy)
        loads.append(copies)
    pack_vectors(vector_sums.own, vectors, more, down_bias, up_bias, part)
    mine = jnp.concatenate([out_own[0:4], grad_own[0:4]], axis=0)
    specials[place.band] = mine
    place.greet(PLACES)
    vector_sums.step(0)
    here = specials.at[place.band]
    for name in ("core", "x", "diagonal"):
        sender.send(("special", name), here, here, name)
    for n, chunk in enumerate(chunks):
        for piece in [0, 1] if n % 2 == 0 else [None]:
            target = sums.got.at[n] if piece is None else sums.got.at[n, piece]
            source = weight_source(refs, chunk, columns, 1 - place.core, piece)
            sender.send((n, 0, piece), source, target, "core")
    events = []
    for n in range(count):
        for stage in range(sums.steps(n)):
            events.append((n // 2 + stage, stage, n))
    for stage in range(1, 6):
        events.append((stage, 0, count + stage))
    for _, stage, n in sorted(events):
        if n >= count:
            vector_sums.step(n - count)
            continue
        if stage == 0:
            for copy in loads[n]:
                copy.wait()
            for piece in [0, 1] if n % 2 == 0 else [None]:
                sender.arrived((n, 0, piece))
        sums.step(n, stage)
    for name in ("core", "x", "diagonal"):
        sender.arrived(("special", name))
    sender.finish()


def finish_kernel(
    chunks,
    special_count,
    total,
    vector_total,
    specials,
    up,
    down,
    out,
    joint,
    up_bias,
    out_specials,
    grad_specials,
    *vectors,
):
    _, _, _, rows, columns = total.shape
    refs = dict(up=up, down=down, out=out, joint=joint)
    for n, (name, part) in enumerate(chunks):
        for core in range(2):
            for x in range(2):
                row, column = x * rows, core * columns
                if name == "down":
                    row += 2 * rows * part
                else:
                    column += 2 * columns * part
                value = total[n, core, x].astype(F32)
                refs[name][row : row + rows, column : column + columns] = value
    part = vectors[0].shape[0]
    for i, vector in enumerate(vectors):
        vector[...] = vector_total[i, 0:part]
    up_bias[...] = jnp.concatenate([vector_total[i : i + 1, 0:part] for i in range(11, 15)], axis=1)[0]
    for first, target in ((0, out_specials), (4, grad_specials)):
        picked = [
            specials[s % BANDS, first + s // BANDS : first + s // BANDS + 1]
            for s in range(special_count)
        ]
        target[0] = jnp.concatenate(picked, axis=0).astype(BF16)


def reduce_all(
    up, down, out, joint, vectors, more, down_bias, up_bias, out_own, grad_own, special_count
):
    width, hidden_width = up.shape
    chunks = chunk_list(hidden_width // width)
    part = width // 8
    rows, columns = part // 2, width // 2
    count = len(chunks)
    shaped = jax.ShapeDtypeStruct
    copies = 10 * count
    total, vector_total, specials = pl.pallas_call(
        partial(reduce_kernel, chunks),
        out_shape=[
            shaped((count, 2, 2, rows, columns), BF16),
            shaped((16, 128), F32),
            shaped((BANDS, 8, width), F32),
        ],
        in_specs=[ANY] * 4 + [VMEM] * 6,
        out_specs=[VMEM] * 3,
        scratch_shapes=chunk_scratch(count, rows, columns)
        + vector_scratch()
        + [
            pltpu.SemaphoreType.DMA((copies,)),
            pltpu.SemaphoreType.DMA((copies,)),
            pltpu.SemaphoreType.DMA((count, 2)),
        ],
        compiler_params=pltpu.CompilerParams(
            vmem_limit_bytes=VMEM_LIMIT, collective_id=0, has_side_effects=True
        ),
        name="reduce_all",
    )(
        up.reshape(2, 2, 2, 2, rows, hidden_width),
        down.reshape(2, 2, 2, hidden_width // width, 2, rows, width),
        out.reshape(2, 2, 2, 2, rows, width),
        joint.reshape(2, 2, 2, 2, rows, 3 * width),
        vectors,
        more,
        down_bias,
        up_bias,
        out_own,
        grad_own,
    )
    special = shaped((1, special_count, width), BF16)
    results = pl.pallas_call(
        partial(finish_kernel, chunks, special_count),
        out_shape=[
            shaped((part, hidden_width), F32),
            shaped((hidden_width // 8, width), F32),
            shaped((part, width), F32),
            shaped((part, 3 * width), F32),
            shaped((hidden_width // 8,), F32),
            special,
            special,
        ]
        + [shaped((part,), F32)] * 11,
        in_specs=[VMEM] * 3,
        out_specs=[VMEM] * 18,
        compiler_params=params(),
        name="finish",
    )(total, vector_total, specials)
    up, down, out, joint, up_bias, out_specials, grad_specials = results[:7]
    return up, down, out, joint, results[7:], up_bias, out_specials, grad_specials


def body(
    patches,
    specials,
    patch_mask,
    band_rows,
    mask_token,
    first_gain,
    first_shift,
    joint_weight,
    query_bias,
    value_bias,
    out_weight,
    out_bias,
    first_scale,
    second_gain,
    second_shift,
    up_weight,
    up_bias,
    down_weight,
    down_bias,
    second_scale,
    cot_patches,
    cot_specials,
):
    slots, width = patches.shape[1:]
    special_count = specials.shape[1]
    hidden_width = up_weight.shape[1]
    owned = -(-special_count // BANDS)
    rows = round_up(slots + owned, 16)
    pad = rows - slots
    every = BANDS * rows
    pairs = width // PAIR
    band = lax.axis_index("band")
    relatives = [band ^ r for r in range(BANDS)]
    info = jnp.stack(
        [band_rows[b] * GRID for b in relatives]
        + [(special_count - b + BANDS - 1) // BANDS for b in relatives]
        + [band]
    ).astype(jnp.int32)
    mask = patch_mask
    patches, specials = patches[0], specials[0]
    cot_patches, cot_specials = cot_patches[0], cot_specials[0]
    shaped = jax.ShapeDtypeStruct

    tokens, first = pl.pallas_call(
        first_kernel,
        out_shape=[shaped((rows, width), F32), shaped((rows, width), BF16)],
        in_specs=[SMEM] + [VMEM] * 6,
        compiler_params=params(),
        name="first",
    )(info, mask, patches, specials, mask_token, first_gain, first_shift)

    firsts = gather_blocks(first)

    block = pl.BlockSpec((rows, width), lambda i: (i, 0))
    queries, keys, values = pl.pallas_call(
        partial(project_kernel, slots),
        grid=(BANDS,),
        out_shape=[
            shaped((rows, width), BF16),
            shaped((every, width), BF16),
            shaped((every, width), BF16),
        ],
        in_specs=[SMEM, block, whole((width, 3 * width)), VMEM, VMEM],
        out_specs=[whole((rows, width)), block, block],
        compiler_params=params(),
        name="project",
    )(info, firsts, joint_weight, query_bias, value_bias)

    own_pair = pl.BlockSpec((rows, PAIR), lambda i: (0, i))
    all_pair = pl.BlockSpec((every, PAIR), lambda i: (0, i))
    kept = pl.BlockSpec((1, 2 * rows, every), lambda i: (i, 0, 0))
    attended, totals, weights = pl.pallas_call(
        partial(attend_kernel, slots),
        grid=(pairs,),
        out_shape=[
            shaped((rows, width), F32),
            shaped((rows, width), F32),
            shaped((pairs, 2 * rows, every), BF16),
        ],
        in_specs=[SMEM, own_pair, all_pair, all_pair],
        out_specs=[own_pair, own_pair, kept],
        compiler_params=params(),
        name="attend",
    )(info, queries, keys, values)

    branch, middle, second, incoming, down_in, down_bias_grad = pl.pallas_call(
        partial(middle_kernel, slots),
        out_shape=[
            shaped((rows, width), F32),
            shaped((rows, width), F32),
            shaped((rows, width), BF16),
            shaped((rows, width), F32),
            shaped((rows, width), BF16),
            shaped((1, width), F32),
        ],
        in_specs=[SMEM] + [VMEM] * 10,
        out_specs=[VMEM] * 6,
        compiler_params=params(),
        name="middle",
    )(
        info,
        attended,
        tokens,
        out_weight,
        out_bias,
        first_scale,
        second_gain,
        second_shift,
        second_scale,
        cot_patches,
        cot_specials,
    )

    steps = 6
    chunk = hidden_width // steps
    branch_two, second_grad, up_grad, up_bias_grad, down_grad = pl.pallas_call(
        mlp_kernel,
        grid=(steps,),
        out_shape=[
            shaped((rows, width), F32),
            shaped((rows, width), F32),
            shaped((width, hidden_width), BF16),
            shaped((1, hidden_width), F32),
            shaped((hidden_width, width), BF16),
        ],
        in_specs=[
            whole((rows, width)),
            whole((rows, width)),
            pl.BlockSpec((width, chunk), lambda i: (0, i)),
            pl.BlockSpec((1, chunk), lambda i: (0, i)),
            pl.BlockSpec((chunk, width), lambda i: (i, 0)),
        ],
        out_specs=[
            whole((rows, width)),
            whole((rows, width)),
            pl.BlockSpec((width, chunk), lambda i: (0, i)),
            pl.BlockSpec((1, chunk), lambda i: (0, i)),
            pl.BlockSpec((chunk, width), lambda i: (i, 0)),
        ],
        compiler_params=params(),
        name="mlp",
    )(second, down_in, up_weight, up_bias.reshape(1, -1), down_weight)

    out_patches, out_own, middle_grad, attended_grad, out_weight_grad, vectors = pl.pallas_call(
        partial(middle_back_kernel, slots),
        out_shape=[
            shaped((slots, width), BF16),
            shaped((pad, width), F32),
            shaped((rows, width), F32),
            shaped((rows, width), F32),
            shaped((width, width), BF16),
            shaped((8, width), F32),
        ],
        in_specs=[SMEM] + [VMEM] * 11,
        out_specs=[VMEM] * 6,
        compiler_params=params(),
        name="middle_back",
    )(
        info,
        middle,
        branch,
        branch_two,
        second_grad,
        incoming,
        attended,
        out_weight,
        down_bias,
        second_scale,
        second_gain,
        first_scale,
    )

    query_grad, key_grad, value_grad = pl.pallas_call(
        partial(attend_back_kernel, slots),
        grid=(pairs,),
        out_shape=[
            shaped((rows, width), BF16),
            shaped((every, width), BF16),
            shaped((every, width), BF16),
        ],
        in_specs=[SMEM, kept, own_pair, all_pair, all_pair, own_pair, own_pair, own_pair],
        out_specs=[own_pair, all_pair, all_pair],
        compiler_params=params(),
        name="attend_back",
    )(info, weights, queries, keys, values, attended, totals, attended_grad)

    joint_weight_grad, first_part = pl.pallas_call(
        joint_grad_kernel,
        out_shape=[shaped((width, 3 * width), BF16), shaped((every, width), BF16)],
        in_specs=[VMEM] * 5,
        out_specs=[VMEM] * 2,
        compiler_params=params(),
        name="joint_grad",
    )(firsts, query_grad, key_grad, value_grad, joint_weight)

    first_grad = scatter_blocks(first_part)

    grad_patches, grad_own, more_vectors = pl.pallas_call(
        partial(first_back_kernel, slots),
        out_shape=[
            shaped((slots, width), BF16),
            shaped((pad, width), F32),
            shaped((8, width), F32),
        ],
        in_specs=[VMEM] * 7,
        out_specs=[VMEM] * 3,
        compiler_params=params(),
        name="first_back",
    )(first_grad, tokens, middle_grad, mask, first_gain, query_grad, value_grad)

    if lax.axis_size("crop") == 8:
        finished = reduce_all(
            up_grad,
            down_grad,
            out_weight_grad,
            joint_weight_grad,
            vectors,
            more_vectors,
            down_bias_grad,
            up_bias_grad,
            out_own,
            grad_own,
            special_count,
        )
    else:
        finished = reduce_general(
            up_grad,
            down_grad,
            out_weight_grad,
            joint_weight_grad,
            vectors,
            more_vectors,
            down_bias_grad,
            up_bias_grad,
            out_own,
            grad_own,
            special_count,
        )
    up, down, out, joint, rows_of, up_bias_sum, out_specials, grad_specials = finished
    return (
        out_patches[None],
        out_specials,
        grad_patches[None],
        grad_specials,
        rows_of[5],
        rows_of[6],
        rows_of[7],
        joint,
        rows_of[8],
        rows_of[9],
        out,
        rows_of[4],
        rows_of[3],
        rows_of[1],
        rows_of[2],
        up,
        up_bias_sum,
        down,
        rows_of[10],
        rows_of[0],
    )


def solution(mesh):
    split = P("crop", "band", None)
    special = P("crop", None, None)
    in_specs = (
        (split, special, P("crop", "band")) + (P(),) * 17 + (split, special)
    )
    line, matrix = P("crop"), P("crop", None)
    out_specs = (
        split,
        special,
        split,
        special,
        line,
        line,
        line,
        matrix,
        line,
        line,
        matrix,
        line,
        line,
        line,
        line,
        matrix,
        line,
        matrix,
        line,
        line,
    )
    return jax.shard_map(body, mesh=mesh, in_specs=in_specs, out_specs=out_specs, check_vma=False)
```

profile of v0, /device:TPU:1, one launch (start us, length us, event | category | flops | bytes accessed | tf_op | source)
XLA Modules:
  0.0 251.8 jit_solution(10678370289075615114)
XLA Ops:
  0.7 1.4 fusion.1
  4.8 0.6 stack.27.info
  5.4 2.7 %first.1 = (f32[448,768]{1,0:T(8,128)}, bf16[448,768]{1,0:T(8,128)(2,1)}) custom-call(s32[9]{0:T(128)} %stack.27.info, s32[1,444]{1,0:T(1,128)} %mask.3, bf16[444,768]{1,0:T(8,128)(2,1)} %bitcast.21, bf16[5,768]{1,0:T(8,128)(2,1)} %bitcast.24, f32[768]{0:T(1024)} %token_.1, f32[768]{0:T(1024)} %gain.7, f32[768]{0:T(1024)} %shift.2), custom_call_target="tpu_custom_call" | custom-call | tf_op jit(solution)/shard_map/first/pallas_call | solution.py:859
  8.1 2.0 collective-permute-start.1
  10.1 1.0 collective-permute-start
  11.1 14.4 %collective-permute-done.1 = bf16[448,768]{1,0:T(8,128)(2,1)S(1)} collective-permute-done((bf16[448,768]{1,0:T(8,128)(2,1)}, bf16[448,768]{1,0:T(8,128)(2,1)S(1)}, u32[]{:S(2)}, u32[]{:S(2)}) %collective-permute-start.1) | collective-permute-done | bytes 688160 | tf_op jit(solution)/shard_map/ppermute | solution.py:360
  25.5 1.2 collective-permute-start.2
  26.7 1.1 constant_dynamic-update-slice_fusion.3
  27.9 0.0 collective-permute-done
  28.0 0.5 collective-permute-done.2
  28.6 0.0 copy-start
  28.6 1.6 copy-done
  30.1 9.1 %project.1 = (bf16[448,768]{1,0:T(8,128)(2,1)}, bf16[1792,768]{1,0:T(8,128)(2,1)}, bf16[1792,768]{1,0:T(8,128)(2,1)}) custom-call(s32[9]{0:T(128)} %stack.27.info, bf16[1792,768]{1,0:T(8,128)(2,1)} %copy-done, bf16[768,2304]{1,0:T(8,128)(2,1)} %weight.7, f32[768]{0:T(1024)} %query_bias.1, f32[768]{0:T(1024)} %value_bias.1), custom_call_target="tpu_custom_call" | custom-call | tf_op jit(solution)/shard_map/project/pallas_call | solution.py:870
  39.3 15.3 %attend.1 = (f32[448,768]{1,0:T(8,128)}, f32[448,768]{1,0:T(8,128)}, bf16[6,896,1792]{2,1,0:T(8,128)(2,1)}) custom-call(s32[9]{0:T(128)} %stack.27.info, bf16[448,768]{1,0:T(8,128)(2,1)} %get-tuple-element.75.queries, bf16[1792,768]{1,0:T(8,128)(2,1)} %get-tuple-element.76.keys, bf16[1792,768]{1,0:T(8,128)(2,1)} %get-tuple-element.77.values), custom_call_target="tpu_custom_call" | custom-call | tf_op jit(solution)/shard_map/attend/pallas_call | solution.py:887
  54.6 5.6 %middle.1 = (f32[448,768]{1,0:T(8,128)}, f32[448,768]{1,0:T(8,128)}, bf16[448,768]{1,0:T(8,128)(2,1)}, f32[448,768]{1,0:T(8,128)}, bf16[448,768]{1,0:T(8,128)(2,1)}, /*index=5*/f32[1,768]{1,0:T(1,128)}) custom-call(s32[9]{0:T(128)} %stack.27.info, f32[448,768]{1,0:T(8,128)} %get-tuple-element.78.attended, f32[448,768]{1,0:T(8,128)} %get-tuple-element.79.tokens, ...), custom_call_target="tpu_custom_call" | custom-call | tf_op jit(solution)/shard_map/middle/pallas_call | solution.py:901
  60.1 18.9 %mlp.1 = (f32[448,768]{1,0:T(8,128)}, f32[448,768]{1,0:T(8,128)}, bf16[768,3072]{1,0:T(8,128)(2,1)}, f32[1,3072]{1,0:T(1,128)}, bf16[3072,768]{1,0:T(8,128)(2,1)}) custom-call(bf16[448,768]{1,0:T(8,128)(2,1)} %get-tuple-element.82.second, bf16[448,768]{1,0:T(8,128)(2,1)} %get-tuple-element.83.down_in, bf16[768,3072]{1,0:T(8,128)(2,1)} %up.1, ...), custom_call_target="tpu_custom_call" | custom-call | tf_op jit(solution)/shard_map/mlp/pallas_call | solution.py:931
  79.0 8.0 %middle_back.1 = (bf16[444,768]{1,0:T(8,128)(2,1)}, f32[4,768]{1,0:T(4,128)}, f32[448,768]{1,0:T(8,128)}, f32[448,768]{1,0:T(8,128)}, bf16[768,768]{1,0:T(8,128)(2,1)}, /*index=5*/f32[8,768]{1,0:T(8,128)}) custom-call(s32[9]{0:T(128)} %stack.27.info, f32[448,768]{1,0:T(8,128)} %get-tuple-element.80.middle, f32[448,768]{1,0:T(8,128)} %get-tuple-element.81.branch, ...), custom_call_target="tpu_custom_call" | custom-call | tf_op jit(solution)/shard_map/middle_back/pallas_call | solution.py:959
  87.0 30.9 %attend_back.1 = (bf16[448,768]{1,0:T(8,128)(2,1)}, bf16[1792,768]{1,0:T(8,128)(2,1)}, bf16[1792,768]{1,0:T(8,128)(2,1)}) custom-call(s32[9]{0:T(128)} %stack.27.info, bf16[6,896,1792]{2,1,0:T(8,128)(2,1)} %get-tuple-element.91.weights, bf16[448,768]{1,0:T(8,128)(2,1)} %get-tuple-element.75.queries, bf16[1792,768]{1,0:T(8,128)(2,1)} %get-tuple-element.76.keys, ...), custom_call_target="tpu_custom_call" | custom-call | tf_op jit(solution)/shard_map/attend_back/pallas_call | solution.py:988
  117.9 16.0 %joint_grad.1 = (bf16[768,2304]{1,0:T(8,128)(2,1)}, bf16[1792,768]{1,0:T(8,128)(2,1)}) custom-call(bf16[1792,768]{1,0:T(8,128)(2,1)} %copy-done, bf16[448,768]{1,0:T(8,128)(2,1)} %get-tuple-element.94.query_grad, bf16[1792,768]{1,0:T(8,128)(2,1)} %get-tuple-element.95.key_grad, bf16[1792,768]{1,0:T(8,128)(2,1)} %get-tuple-element.96.value_grad, ...), custom_call_target="tpu_custom_call" | custom-call | tf_op jit(solution)/shard_map/joint_grad/pallas_call | solution.py:1002
  133.9 1.4 fusion
  135.3 0.0 copy-start.1
  135.3 0.1 pad_maximum_fusion
  135.4 0.4 collective-permute-start.3
  135.9 2.8 %collective-permute-done.3 = bf16[896,768]{1,0:T(8,128)(2,1)S(1)} collective-permute-done((bf16[896,768]{1,0:T(8,128)(2,1)S(1)}, bf16[896,768]{1,0:T(8,128)(2,1)S(1)}, u32[]{:S(2)}, u32[]{:S(2)}) %collective-permute-start.3) | collective-permute-done | bytes 1376288 | tf_op jit(solution)/shard_map/ppermute | solution.py:360
  138.6 0.0 copy-done.1
  138.6 0.2 add_convert_fusion
  138.8 1.5 collective-permute-start.4
  140.4 15.2 %collective-permute-done.4 = bf16[448,768]{1,0:T(8,128)(2,1)S(1)} collective-permute-done((bf16[448,768]{1,0:T(8,128)(2,1)S(1)}, bf16[448,768]{1,0:T(8,128)(2,1)S(1)}, u32[]{:S(2)}, u32[]{:S(2)}) %collective-permute-start.4) | collective-permute-done | bytes 688160 | tf_op jit(solution)/shard_map/ppermute | solution.py:360
  155.6 1.4 convert_add_fusion.first_grad
  156.9 5.7 %first_back.1 = (bf16[444,768]{1,0:T(8,128)(2,1)}, f32[4,768]{1,0:T(4,128)}, f32[8,768]{1,0:T(8,128)}) custom-call(f32[448,768]{1,0:T(8,128)} %convert_add_fusion.first_grad, f32[448,768]{1,0:T(8,128)} %get-tuple-element.79.tokens, f32[448,768]{1,0:T(8,128)} %get-tuple-element.100.middle_grad, s32[1,444]{1,0:T(1,128)} %mask.3, f32[768]{0:T(1024)} %gain.7, ...), custom_call_target="tpu_custom_call" | custom-call | tf_op jit(solution)/shard_map/first_back/pallas_call | solution.py:1013
  162.7 85.6 %reduce_all.1 = (bf16[12,2,2,48,384]{4,3,2,1,0:T(8,128)(2,1)}, f32[16,128]{1,0:T(8,128)}, f32[4,8,768]{2,1,0:T(8,128)}) custom-call(bf16[2,2,2,2,48,3072]{5,4,3,2,1,0:T(8,128)(2,1)} %bitcast.16, bf16[2,2,2,4,2,48,768]{6,5,4,3,2,1,0:T(8,128)(2,1)} %bitcast.17, bf16[2,2,2,2,48,768]{5,4,3,2,1,0:T(8,128)(2,1)} %bitcast.19, ...), custom_call_target="tpu_custom_call" | custom-call | tf_op jit(solution)/shard_map/reduce_all/pallas_call | solution.py:761
  248.2 3.4 %finish.1 = (f32[96,3072]{1,0:T(8,128)}, f32[384,768]{1,0:T(8,128)}, f32[96,768]{1,0:T(8,128)}, f32[96,2304]{1,0:T(8,128)}, f32[384]{0:T(512)}, /*index=5*/bf16[...) custom-call(bf16[12,2,2,48,384]{4,3,2,1,0:T(8,128)(2,1)} %get-tuple-, ...), custom_call_target="tpu_custom_call" | custom-call | tf_op jit(solution)/shard_map/finish/pallas_call | solution.py:794
  (3 shorter events, 0.1 us)
Async XLA Ops:
  8.1 17.4 %collective-permute-start.1 = (bf16[448,768]{1,0:T(8,128)(2,1)}, bf16[448,768]{1,0:T(8,128)(2,1)S(1)}, u32[]{:S(2)}, u32[]{:S(2)}) collective-permute-start(bf16[448,768]{1,0:T(8,128)(2,1)} %get-tuple-element.74), channel_id=1, source_target_pairs={{0,16},{8,24},{16,0},{24,8},{1,17},{9,25},{17,1},{25,9},{2,18},{10... | collective-permute-start | bytes 2064392 | tf_op jit(solution)/shard_map/ppermute | solution.py:360
  10.1 17.7 %collective-permute-start = (bf16[448,768]{1,0:T(8,128)(2,1)}, bf16[448,768]{1,0:T(8,128)(2,1)S(1)}, u32[]{:S(2)}, u32[]{:S(2)}) collective-permute-start(bf16[448,768]{1,0:T(8,128)(2,1)} %get-tuple-element.74), channel_id=1, source_target_pairs={{0,8},{8,0},{16,24},{24,16},{1,9},{9,1},{17,25},{25,17},{2,10},{10... | collective-permute-start | bytes 2064392 | tf_op jit(solution)/shard_map/ppermute | solution.py:360
  25.5 3.0 %collective-permute-start.2 = (bf16[448,768]{1,0:T(8,128)(2,1)S(1)}, bf16[448,768]{1,0:T(8,128)(2,1)S(1)}, u32[]{:S(2)}, u32[]{:S(2)}) collective-permute-start(bf16[448,768]{1,0:T(8,128)(2,1)S(1)} %collective-permute-done.1), channel_id=1, source_target_pairs={{0,8},{8,0},{16,24},{24,16},{1,9},{9,1},{17,25},{25,17},{2,10},{10... | collective-permute-start | bytes 2064392 | tf_op jit(solution)/shard_map/ppermute | solution.py:360
  28.6 1.6 copy-start
  135.3 3.3 %copy-start.1 = (bf16[1792,768]{1,0:T(8,128)(2,1)S(1)}, bf16[1792,768]{1,0:T(8,128)(2,1)}, u32[]{:S(2)}) copy-start(bf16[1792,768]{1,0:T(8,128)(2,1)} %get-tuple-element.99) | copy-start | bytes 8257540
  135.4 3.2 %collective-permute-start.3 = (bf16[896,768]{1,0:T(8,128)(2,1)S(1)}, bf16[896,768]{1,0:T(8,128)(2,1)S(1)}, u32[]{:S(2)}, u32[]{:S(2)}) collective-permute-start(bf16[896,768]{1,0:T(8,128)(2,1)S(1)} %pad_maximum_fusion), channel_id=1, source_target_pairs={{0,8},{8,0},{16,24},{24,16},{1,9},{9,1},{17,25},{25,17},{2,10},{10... | collective-permute-start | bytes 4128776 | tf_op jit(solution)/shard_map/ppermute | solution.py:360
  138.8 16.7 %collective-permute-start.4 = (bf16[448,768]{1,0:T(8,128)(2,1)S(1)}, bf16[448,768]{1,0:T(8,128)(2,1)S(1)}, u32[]{:S(2)}, u32[]{:S(2)}) collective-permute-start(bf16[448,768]{1,0:T(8,128)(2,1)S(1)} %add_convert_fusion), channel_id=1, source_target_pairs={{0,16},{8,24},{16,0},{24,8},{1,17},{9,25},{17,1},{25,9},{2,18},{10... | collective-permute-start | bytes 2064392 | tf_op jit(solution)/shard_map/ppermute | solution.py:360
where the time goes:
time: 252 us
  Pallas kernels  201 us (80%)
  waiting for transfers between devices  32.9 us (13%)
  local copies, waits for them, and re-layouts  6.27 us (2%)
  starting transfers between devices  6.18 us (2%)
  between operations  3.59 us (1%)
    pallas_call x1, Pallas kernels, reduce_all(): pl.pallas_call(partial(reduce_kernel, chunks), out_shape=[shaped((count,...  85.6 us
    ppermute x5, waiting for transfers between devices, swap(): return lax.ppermute(x, axis, [(i, i ^ distance) for i in range(size)])  32.9 us
    pallas_call x1, Pallas kernels, body(): pl.pallas_call(partial(attend_back_kernel, slots), grid=(pairs,), out_sha...  30.9 us
    pallas_call x1, Pallas kernels, body(): pl.pallas_call(mlp_kernel, grid=(steps,), out_shape=[shaped((rows, width)...  18.9 us
    pallas_call x1, Pallas kernels, body(): pl.pallas_call(joint_grad_kernel, out_shape=[shaped((width, 3 * width), B...  16 us
    pallas_call x1, Pallas kernels, body(): pl.pallas_call(partial(attend_kernel, slots), grid=(pairs,), out_shape=[s...  15.3 us
    pallas_call x1, Pallas kernels, body(): pl.pallas_call(partial(project_kernel, slots), grid=(BANDS,), out_shape=[...  9.12 us
    pallas_call x1, Pallas kernels, body(): pl.pallas_call(partial(middle_back_kernel, slots), out_shape=[shaped((slo...  7.95 us
  transfers between devices with their start and end apart: 5, of which 4 were waited for; matrix products, arithmetic and copies ran while one was open for 0% of the time, Pallas kernels for 0%

commit v1 on v0

v1 whole, which is shorter than its diff:
```python
from functools import partial

import jax
import jax.numpy as jnp
from jax import lax
from jax.experimental import pallas as pl
from jax.experimental.pallas import tpu as pltpu
from jax.sharding import PartitionSpec as P

HEAD = 64
GRID = 37
PAIR = 2 * HEAD
BANDS = 4
KEY_PART = 256
F32 = jnp.float32
BF16 = jnp.bfloat16
VMEM_LIMIT = 60 << 20


def round_up(value, unit):
    return (value + unit - 1) // unit * unit


def params(semantics=None):
    return pltpu.CompilerParams(vmem_limit_bytes=VMEM_LIMIT)


def dot(a, b):
    return jnp.dot(a, b, preferred_element_type=F32)


def dot_nt(a, b):
    return lax.dot_general(a, b, (((1,), (1,)), ((), ())), preferred_element_type=F32)


def dot_tn(a, b):
    return lax.dot_general(a, b, (((0,), (0,)), ((), ())), preferred_element_type=F32)


def normalize(rows):
    centred = rows - jnp.mean(rows, axis=-1, keepdims=True)
    spread = jnp.mean(centred * centred, axis=-1, keepdims=True)
    scale = lax.rsqrt(spread + 1e-06)
    return centred * scale, scale


def normalize_back(grad, hat, scale):
    return scale * (
        grad
        - jnp.mean(grad, axis=-1, keepdims=True)
        - hat * jnp.mean(grad * hat, axis=-1, keepdims=True)
    )


def column_sum(rows):
    return jnp.sum(rows, axis=0, keepdims=True)


def line(ref):
    return ref[...].reshape(1, -1)


def whole(shape):
    return pl.BlockSpec(shape, lambda *_: (0,) * len(shape))


VMEM = pl.BlockSpec(memory_space=pltpu.VMEM)
ANY = pl.BlockSpec(memory_space=pl.ANY)
SMEM = pl.BlockSpec(memory_space=pltpu.SMEM)


def own_special(specials, band, slot):
    row = jnp.zeros((1, specials.shape[1]), F32)
    for special in range(specials.shape[0]):
        if special // BANDS == slot:
            row = row + jnp.where(band == special % BANDS, specials[special : special + 1], 0.0)
    return row


def place_rows(ref, patch_rows, specials, band):
    slots = patch_rows.shape[0]
    rows = ref.shape[0]
    ref[0:slots, :] = patch_rows
    extra = [own_special(specials, band, slot) for slot in range(rows - slots)]
    ref[slots:rows, :] = jnp.concatenate(extra, axis=0)


def counted_rows(info_ref, relative, rows, slots, width):
    index = lax.broadcasted_iota(jnp.int32, (rows, width), 0)
    used = index < info_ref[relative]
    special = (index >= slots) & (index < slots + info_ref[BANDS + relative])
    return used | special


def stack_pair(rows):
    lane = lax.broadcasted_iota(jnp.int32, rows.shape, 1)
    zero = jnp.zeros_like(rows)
    return jnp.concatenate(
        [jnp.where(lane < HEAD, rows, zero), jnp.where(lane >= HEAD, rows, zero)], axis=0
    )


def unstack_pair(rows):
    half = rows.shape[0] // 2
    lane = lax.broadcasted_iota(jnp.int32, (half, rows.shape[1]), 1)
    return jnp.where(lane < HEAD, rows[:half], rows[half:])


def mask_column(mask):
    return jnp.broadcast_to(mask[...].astype(F32), (8, mask.shape[1])).T[:, :1] > 0


def first_kernel(slots, info, mask, patches, specials, token, gain, shift, tokens, first):
    band = info[2 * BANDS]
    filled = jnp.where(mask_column(mask), line(token), patches[...].astype(F32))
    place_rows(tokens, filled, specials[...].astype(F32), band)
    hat, _ = normalize(tokens[...])
    counted = counted_rows(info, 0, tokens.shape[0], slots, tokens.shape[1])
    first[...] = jnp.where(counted, hat * line(gain) + line(shift), 0.0).astype(BF16)


def project_kernel(slots, info, first, weight, query_bias, value_bias, queries, keys, values):
    relative = pl.program_id(0)
    rows, width = queries.shape
    counted = counted_rows(info, relative, rows, slots, width)
    low = first[...]

    @pl.when(relative == 0)
    def _():
        queries[...] = (dot(low, weight[:, :width]) + line(query_bias)).astype(BF16)

    keys[...] = dot(low, weight[:, width : 2 * width]).astype(BF16)
    values[...] = jnp.where(
        counted, dot(low, weight[:, 2 * width :]) + line(value_bias), 0.0
    ).astype(BF16)


def attend_kernel(slots, info, queries, keys, values, attended, totals, weights):
    rows = queries.shape[0]
    factor = HEAD ** (-0.5)
    stacked = stack_pair((queries[...].astype(F32) * factor).astype(BF16))
    scores = dot_nt(stacked, keys[...])
    low = jnp.exp(scores).astype(BF16)
    weights[0] = low
    ones = jnp.concatenate(
        [
            counted_rows(info, r, rows, slots, PAIR).astype(F32).astype(BF16)
            for r in range(BANDS)
        ],
        axis=0,
    )
    summed = dot(low, jnp.concatenate([values[...], ones], axis=1))
    total = unstack_pair(summed[:, PAIR:])
    attended[...] = unstack_pair(summed[:, :PAIR]) / total
    totals[...] = total


def middle_kernel(
    slots,
    info,
    attended,
    tokens,
    weight,
    bias,
    first_scale,
    gain,
    shift,
    second_scale,
    cot_patches,
    cot_specials,
    branch,
    middle,
    second,
    incoming,
    down_in,
    down_keep,
    down_send,
    down_bias_grad,
):
    rows = tokens.shape[0]
    band = info[2 * BANDS]
    side = dot(attended[...].astype(BF16), weight[...]) + line(bias)
    branch[...] = side
    mid = tokens[...] + line(first_scale) * side
    middle[...] = mid
    hat, _ = normalize(mid)
    second[...] = (hat * line(gain) + line(shift)).astype(BF16)
    counted = counted_rows(info, 0, slots, slots, tokens.shape[1])
    given = jnp.where(counted, cot_patches[...].astype(F32), 0.0)
    place_rows(incoming, given, cot_specials[...].astype(F32), band)
    low = (incoming[...] * line(second_scale)).astype(BF16)
    down_in[...] = low
    keep, send = own_half(low, band)
    down_keep[...] = keep
    down_send[...] = send
    down_bias_grad[...] = column_sum(low.astype(F32))


def own_half(rows, band):
    half = rows.shape[1] // 2
    first = lax.rem(band, 2) == 0
    low, high = rows[:, :half], rows[:, half:]
    return jnp.where(first, low, high), jnp.where(first, high, low)


def gelu_and_slope(x):
    phi = 0.5 + 0.5 * lax.erf(x * 0.7071067811865476)
    density = jnp.exp(-0.5 * x * x) * 0.3989422804014327
    return x * phi, phi + x * density


def mlp_kernel(
    info,
    second,
    down_in,
    down_keep,
    down_send,
    up,
    up_bias,
    down,
    branch_two,
    second_grad,
    up_grad_keep,
    up_grad_send,
    up_bias_grad,
    down_grad_keep,
    down_grad_send,
):
    step = pl.program_id(0)
    low = second[...]
    hidden = dot(low, up[...]) + up_bias[...]
    active, slope = gelu_and_slope(hidden)
    active = active.astype(BF16)
    hidden_in = (slope * dot_nt(down_in[...], down[...])).astype(BF16)

    @pl.when(step == 0)
    def _():
        branch_two[...] = jnp.zeros_like(branch_two)
        second_grad[...] = jnp.zeros_like(second_grad)

    branch_two[...] += dot(active, down[...])
    second_grad[...] += dot_nt(hidden_in, up[...])
    keep, send = own_half(hidden_in, info[2 * BANDS])
    up_grad_send[...] = dot_tn(low, send).astype(BF16)
    up_grad_keep[...] = dot_tn(low, keep).astype(BF16)
    down_grad_send[...] = dot_tn(active, down_send[...]).astype(BF16)
    down_grad_keep[...] = dot_tn(active, down_keep[...]).astype(BF16)
    up_bias_grad[...] = column_sum(hidden_in.astype(F32))


def middle_back_kernel(
    slots,
    info,
    middle,
    branch,
    branch_two,
    second_grad,
    incoming,
    attended,
    weight,
    down_bias,
    second_scale,
    gain,
    first_scale,
    out_patches,
    out_specials,
    middle_grad,
    attended_grad,
    out_keep,
    out_send,
    vectors,
):
    rows = middle.shape[0]
    mid = middle[...]
    given = incoming[...]
    two = branch_two[...] + line(down_bias)
    output = mid + line(second_scale) * two
    counted = counted_rows(info, 0, slots, slots, mid.shape[1])
    out_patches[...] = jnp.where(counted, output[:slots], 0.0).astype(BF16)
    out_specials[...] = output[slots:]
    hat, scale = normalize(mid)
    grad = second_grad[...]
    back = given + normalize_back(grad * line(gain), hat, scale)
    middle_grad[...] = back
    out_in = (back * line(first_scale)).astype(BF16)
    attended_grad[...] = dot_nt(out_in, weight[...])
    keep, send = own_half(out_in, info[2 * BANDS])
    low = attended[...].astype(BF16)
    out_keep[...] = dot_tn(low, keep).astype(BF16)
    out_send[...] = dot_tn(low, send).astype(BF16)
    vectors[...] = jnp.concatenate(
        [
            column_sum(given * two),
            column_sum(grad * hat),
            column_sum(grad),
            column_sum(back * branch[...]),
            column_sum(out_in.astype(F32)),
            jnp.zeros((3, mid.shape[1]), F32),
        ],
        axis=0,
    )


def attend_back_pair(weights, queries, keys, values, attended, totals, attended_grad, outs, between):
    query_grad, key_grad, value_grad = outs
    rows = queries.shape[0]
    every = keys.shape[0]
    factor = HEAD ** (-0.5)
    stacked = stack_pair((queries[...].astype(F32) * factor).astype(BF16))
    scaled = attended_grad[...] / totals[...]
    returned = stack_pair(scaled.astype(BF16))
    slope = jnp.sum(stack_pair(scaled * attended[...]), axis=1, keepdims=True)
    stacked_t = stacked.astype(F32).T.astype(BF16)
    returned_t = returned.astype(F32).T.astype(BF16)
    total = jnp.zeros((2 * rows, PAIR), F32)
    for part in range(every // KEY_PART):
        span = slice(part * KEY_PART, (part + 1) * KEY_PART)
        low = weights[0, :, span]
        moved = dot_nt(returned, values[span, :])
        scores = (low.astype(F32) * (moved - slope)).astype(BF16)
        total = total + dot(scores, keys[span, :])
        key_grad[span, :] = dot(stacked_t, scores).T.astype(BF16)
        value_grad[span, :] = dot(returned_t, low).T.astype(BF16)
        between(part)
    query_grad[...] = (unstack_pair(total) * factor).astype(BF16)


def first_part(block, rows, query_grad, key_grad, value_grad, weight):
    width = weight.shape[0]
    span = slice(block * rows, (block + 1) * rows)
    part = jnp.zeros((rows, width), F32)
    for pair in range(0, width // PAIR, 2):
        for offset, grad in ((width, key_grad), (2 * width, value_grad), (0, query_grad)):
            if offset == 0 and block > 0:
                continue
            at = slice(0, rows) if offset == 0 else span
            low = jnp.concatenate([grad[pair, at, :], grad[pair + 1, at, :]], axis=1)
            columns = slice(offset + pair * PAIR, offset + (pair + 2) * PAIR)
            part = part + dot_nt(low, weight[:, columns])
    return part


def joint_columns(firsts, grad):
    low = jnp.concatenate([grad[pair] for pair in range(grad.shape[0])], axis=1)
    return dot_tn(firsts, low).astype(BF16)


def first_back(slots, info, grad, tokens, middle_grad, mask, gain):
    rows, width = tokens.shape
    grad = jnp.where(counted_rows(info, 0, rows, slots, width), grad, 0.0)
    hat, scale = normalize(tokens[...])
    token_grad = middle_grad[...] + normalize_back(grad * line(gain), hat, scale)
    masked = mask_column(mask)
    patch_grad = token_grad[:slots]
    patches = jnp.where(masked, 0.0, patch_grad).astype(BF16)
    vectors = [
        column_sum(jnp.where(masked, patch_grad, 0.0)),
        column_sum(grad * hat),
        column_sum(grad),
    ]
    return patches, token_grad[slots:], vectors


def bias_sums(info, slots, rows, query_grad, value_grad):
    ones = [
        counted_rows(info, block, rows, slots, PAIR).astype(F32).astype(BF16)
        for block in range(BANDS)
    ]
    ones = jnp.concatenate(ones, axis=0)
    pairs = range(query_grad.shape[0])
    queries = [column_sum(query_grad[pair].astype(F32)) for pair in pairs]
    values = [dot_tn(ones, value_grad[pair])[0:1] for pair in pairs]
    both = [jnp.concatenate(queries, axis=1), jnp.concatenate(values, axis=1)]
    return jnp.concatenate(both + [jnp.zeros((6, both[0].shape[1]), F32)], axis=0)


def swap(x, axis, distance):
    size = lax.axis_size(axis)
    return lax.ppermute(x, axis, [(i, i ^ distance) for i in range(size)])


def halve(x, axis, distance):
    bit = (lax.axis_index(axis) // distance) % 2
    sent = lax.dynamic_index_in_dim(x, 1 - bit, 0, keepdims=False)
    kept = lax.dynamic_index_in_dim(x, bit, 0, keepdims=False)
    got = swap(sent, axis, distance)
    return (kept.astype(F32) + got.astype(F32)).astype(BF16)


def reduce_half(kept, got, columns):
    held = (kept.astype(F32) + got.astype(F32)).astype(BF16)
    rows, half = held.shape
    crops = lax.axis_size("crop")
    held = held.reshape((crops, rows // crops, half))
    distance = 1
    while distance < crops:
        count = held.shape[0]
        held = jnp.moveaxis(held.reshape((count // 2, 2) + held.shape[1:]), 1, 0)
        held = halve(held, "crop", distance)
        distance *= 2
    held = held.reshape((rows // crops, half))
    other = swap(held, "band", 2)
    full = (held.astype(F32) + other.astype(F32)).astype(BF16)
    mate = swap(full, "band", 1)
    bit = lax.axis_index("band") % 2
    low = jnp.where(bit == 0, full, mate).astype(F32).reshape(rows // crops, -1, columns)
    high = jnp.where(bit == 0, mate, full).astype(F32).reshape(rows // crops, -1, columns)
    return jnp.stack([low, high], axis=2).reshape(rows // crops, 2 * half)


def gather_blocks(x):
    near = swap(x, "band", 1)
    far = swap(x, "band", 2)
    diagonal = swap(far, "band", 1)
    return jnp.concatenate([x, near, far, diagonal], axis=0)


def scatter_blocks(x):
    rows = x.shape[0] // BANDS
    got = swap(jnp.concatenate([x[rows : 2 * rows], x[3 * rows :]], axis=0), "band", 1)
    own = x[:rows].astype(F32) + got[:rows].astype(F32)
    far = (x[2 * rows : 3 * rows].astype(F32) + got[rows:].astype(F32)).astype(BF16)
    return own + swap(far, "band", 2).astype(F32)


def reduce_small(vectors, more, down_bias, up_bias, out_own, grad_own, special_count):
    crops = lax.axis_size("crop")
    width = vectors.shape[1]
    owned = -(-special_count // BANDS)
    both = jnp.concatenate([out_own[:owned], grad_own[:owned]], axis=1).astype(BF16)
    both = lax.all_gather(both, "band", axis=0, tiled=False)
    both = jnp.transpose(both, (1, 0, 2)).reshape(owned * BANDS, 2 * width)[:special_count]
    plain = jnp.concatenate([vectors[:5], more[:5], down_bias], axis=0)
    plain = jnp.transpose(plain.reshape(11, crops, -1), (1, 0, 2)).reshape(crops, -1)
    packed = jnp.concatenate([plain, up_bias.reshape(crops, -1)], axis=1)
    packed = lax.psum_scatter(packed, "crop", scatter_dimension=0, tiled=False)
    packed = lax.psum(packed, "band")
    part = width // crops
    rows = [packed[i * part : (i + 1) * part] for i in range(11)]
    return rows, packed[11 * part :], both[None, :, :width], both[None, :, width:]


def attend_back_kernel(
    weights, queries, keys, values, attended, totals, attended_grad, query_grad, key_grad, value_grad
):
    outs = (query_grad.at[0], key_grad.at[0], value_grad.at[0])
    inputs = (weights, queries, keys, values, attended, totals, attended_grad)
    attend_back_pair(*inputs, outs, lambda part: None)


def joint_back_kernel(
    slots, info, firsts, query_grad, key_grad, value_grad, weight, joint_keep, joint_send, first_grad, sums
):
    rows, width = query_grad.shape[1], weight.shape[0]
    for block in range(BANDS):
        part = first_part(block, rows, query_grad, key_grad, value_grad, weight)
        first_grad[block * rows : (block + 1) * rows, :] = part.astype(BF16)
    half = width // 2
    for part, grad in enumerate((query_grad, key_grad, value_grad)):
        low = firsts[0:rows, :] if part == 0 else firsts[...]
        keep, send = own_half(joint_columns(low, grad), info[2 * BANDS])
        joint_keep[:, part * half : (part + 1) * half] = keep
        joint_send[:, part * half : (part + 1) * half] = send
    sums[...] = bias_sums(info, slots, rows, query_grad, value_grad)


def first_back_kernel(
    slots, info, first_grad, tokens, middle_grad, mask, gain, sums, patches, specials, vectors
):
    grads, special_grad, rows = first_back(
        slots, info, first_grad[...], tokens, middle_grad, mask, gain
    )
    patches[...] = grads
    specials[...] = special_grad
    vectors[...] = jnp.concatenate(rows + [sums[0:5]], axis=0)


def backward_general(given, slots, special_count):
    g = given
    rows, width = g["tokens"].shape
    every = BANDS * rows
    pairs = width // PAIR
    shaped = jax.ShapeDtypeStruct
    own_pair = pl.BlockSpec((rows, PAIR), lambda i: (0, i))
    all_pair = pl.BlockSpec((every, PAIR), lambda i: (0, i))
    grads = pl.pallas_call(
        attend_back_kernel,
        grid=(pairs,),
        out_shape=[
            shaped((pairs, rows, PAIR), BF16),
            shaped((pairs, every, PAIR), BF16),
            shaped((pairs, every, PAIR), BF16),
        ],
        in_specs=[
            pl.BlockSpec((1, 2 * rows, every), lambda i: (i, 0, 0)),
            own_pair,
            all_pair,
            all_pair,
            own_pair,
            own_pair,
            own_pair,
        ],
        out_specs=[
            pl.BlockSpec((1, rows, PAIR), lambda i: (i, 0, 0)),
            pl.BlockSpec((1, every, PAIR), lambda i: (i, 0, 0)),
            pl.BlockSpec((1, every, PAIR), lambda i: (i, 0, 0)),
        ],
        compiler_params=params(),
        name="attend_back",
    )(
        g["weights"],
        g["queries"],
        g["keys"],
        g["values"],
        g["attended"],
        g["totals"],
        g["attended_grad"],
    )
    half = width // 2
    joint_keep, joint_send, parts, sums = pl.pallas_call(
        partial(joint_back_kernel, slots),
        out_shape=[
            shaped((width, 3 * half), BF16),
            shaped((width, 3 * half), BF16),
            shaped((every, width), BF16),
            shaped((8, width), F32),
        ],
        in_specs=[SMEM] + [VMEM] * 5,
        out_specs=[VMEM] * 4,
        compiler_params=params(),
        name="joint_back",
    )(g["info"], g["firsts"], *grads, g["joint_weight"])
    grad_patches, grad_own, more = pl.pallas_call(
        partial(first_back_kernel, slots),
        out_shape=[
            shaped((slots, width), BF16),
            shaped((rows - slots, width), F32),
            shaped((8, width), F32),
        ],
        in_specs=[SMEM] + [VMEM] * 6,
        out_specs=[VMEM] * 3,
        compiler_params=params(),
        name="first_back",
    )(
        g["info"],
        scatter_blocks(parts),
        g["tokens"],
        g["middle_grad"],
        g["mask"],
        g["first_gain"],
        sums,
    )
    small = reduce_small(
        g["vectors"],
        more,
        g["down_bias_grad"],
        g["up_bias_grad"],
        g["out_own"],
        grad_own,
        special_count,
    )
    matrices = (
        reduce_half(g["up_keep"], g["up_got"], half),
        reduce_half(g["down_keep"], g["down_got"], half),
        reduce_half(g["out_keep"], swap(g["out_send"], "band", 1), half),
        reduce_half(joint_keep, swap(joint_send, "band", 1), half),
    )
    return (grad_patches,) + matrices + small


MESH = pl.DeviceIdType.MESH
CROPS = 8
X_FIRST = (0, 2, 4, 6, 10)
NEIGHBOURS = ("core", "x", "diagonal")
PLACES = NEIGHBOURS + tuple(range(1, CROPS))


class Place:
    def __init__(self):
        band, crop = lax.axis_index("band"), lax.axis_index("crop")
        self.band = band
        self.core, self.x = lax.rem(band, 2), lax.div(band, 2)
        self.y, self.near, self.far = lax.rem(crop, 2), lax.rem(lax.div(crop, 2), 2), lax.div(crop, 4)
        core_step, x_step = 1 - 2 * self.core, 2 - 4 * self.x
        self.device = {
            "core": (band + core_step, crop),
            "x": (band + x_step, crop),
            "diagonal": (band + core_step + x_step, crop),
            "y": (band, crop + 1 - 2 * self.y),
            "near": (band, crop + 2 - 4 * self.near),
            "far": (band, crop + 4 - 8 * self.far),
        }
        self.crop = crop
        for step in range(1, CROPS):
            self.device[step] = (band, lax.rem(crop + step, CROPS))

    def greet(self, names):
        barrier = pltpu.get_barrier_semaphore()
        for name in names:
            pl.semaphore_signal(barrier, inc=1, device_id=self.device[name], device_id_type=MESH)
        pl.semaphore_wait(barrier, len(names))


class Sender:
    def __init__(self, place, send_sems, recv_sems):
        self.place, self.send_sems, self.recv_sems = place, send_sems, recv_sems
        self.routes = {}

    def add(self, key, source, target, name):
        self.routes[key] = (len(self.routes), source, target, name)

    def copy(self, key):
        index, source, target, name = self.routes[key]
        return pltpu.make_async_remote_copy(
            src_ref=source,
            dst_ref=target,
            send_sem=self.send_sems.at[index],
            recv_sem=self.recv_sems.at[index],
            device_id=self.place.device[name],
            device_id_type=MESH,
        )

    def send(self, key):
        self.copy(key).start()

    def arrived(self, key):
        self.copy(key).wait_recv()

    def finish(self):
        for key in self.routes:
            self.copy(key).wait_send()


def chunk_list(hidden_parts):
    chunks = []
    for part in range(hidden_parts):
        chunks += [("down", part), ("up", part)]
    return chunks + [("out", 0), ("joint", 0), ("joint", 1), ("joint", 2)]


def chunk_scratch(count, rows, columns):
    unit = (rows, columns)
    return [
        pltpu.VMEM((count, 2, 2, 2, 2) + unit, BF16),
        pltpu.VMEM((count, 2, 2, 2) + unit, BF16),
        pltpu.VMEM((count, 2, 2) + unit, BF16),
        pltpu.VMEM((count, 2) + unit, BF16),
        pltpu.VMEM((count, 2) + unit, BF16),
    ]


class ChunkSums:
    def __init__(self, place, sender, buffers, total, count):
        p, self.sender = place, sender
        own, got_a, got_b, got_c, got_d = buffers
        self.table = {}
        for n in range(count):
            if x_first(n):
                half = total.at[n, p.core, p.x]
                rows = [
                    (None, None, own.at[n, 1 - p.x], got_a.at[n], "x"),
                    (own.at[n, p.x], got_a.at[n], own.at[n, p.x, :, :, 1 - p.y], got_b.at[n], "y"),
                    (
                        own.at[n, p.x, :, :, p.y],
                        got_b.at[n],
                        own.at[n, p.x, :, 1 - p.near, p.y],
                        got_c.at[n],
                        "near",
                    ),
                    (
                        own.at[n, p.x, :, p.near, p.y],
                        got_c.at[n],
                        own.at[n, p.x, 1 - p.far, p.near, p.y],
                        got_d.at[n, 0],
                        "far",
                    ),
                    (own.at[n, p.x, p.far, p.near, p.y], got_d.at[n, 0], half, half, "x"),
                    (None, None, total.at[n, p.core], total.at[n, p.core], "core"),
                ]
                last = half
            else:
                half = total.at[n, p.core]
                rows = [
                    (None, None, own.at[n, :, :, 1 - p.y], got_a.at[n], "y"),
                    (
                        own.at[n, :, :, p.y],
                        got_a.at[n],
                        own.at[n, :, 1 - p.near, p.y],
                        got_b.at[n],
                        "near",
                    ),
                    (
                        own.at[n, :, p.near, p.y],
                        got_b.at[n],
                        own.at[n, 1 - p.far, p.near, p.y],
                        got_c.at[n],
                        "far",
                    ),
                    (
                        own.at[n, p.far, p.near, p.y],
                        got_c.at[n],
                        own.at[n, p.far, p.near, p.y],
                        got_d.at[n],
                        "x",
                    ),
                    (own.at[n, p.far, p.near, p.y], got_d.at[n], half, half, "core"),
                ]
                last = half
            self.table[n] = rows
            for stage, (_, _, source, target, name) in enumerate(rows):
                sender.add((n, stage + 1), source, target, name)
            self.table[n, "last"] = last

    def steps(self, n):
        return len(self.table[n]) + 1

    def step(self, n, stage):
        if stage > 0:
            self.sender.arrived((n, stage))
        if stage == len(self.table[n]):
            return
        into, got, source, target, _ = self.table[n][stage]
        if into is not None:
            place = self.table[n, "last"] if source is target else into
            place[...] = into[...] + got[...]
        self.sender.send((n, stage + 1))


class VectorSums:
    def __init__(self, place, sender, buffers, total):
        self.place, self.sender, self.total = place, sender, total
        self.own, self.got, self.parts = buffers
        for step in range(1, CROPS):
            source = self.own.at[lax.rem(place.crop + step, CROPS)]
            sender.add(("vector", step), source, self.got.at[place.crop], step)
        here = self.parts.at[place.band]
        for name in NEIGHBOURS:
            sender.add(("parts", name), here, here, name)

    def spread(self):
        for step in range(1, CROPS):
            self.sender.send(("vector", step))

    def share(self):
        p = self.place
        self.got[p.crop] = self.own[p.crop]
        for step in range(1, CROPS):
            self.sender.arrived(("vector", step))
        self.parts[p.band] = jnp.sum(self.got[...], axis=0)
        for name in NEIGHBOURS:
            self.sender.send(("parts", name))

    def close(self):
        for name in NEIGHBOURS:
            self.sender.arrived(("parts", name))
        self.total[...] = jnp.sum(self.parts[...], axis=0)


def pack_vectors(own, rows, up_bias, part):
    for crop in range(CROPS):
        span = slice(crop * part, (crop + 1) * part)
        wide = 4 * crop * part
        wider = [up_bias[0:1, wide + j * part : wide + (j + 1) * part] for j in range(4)]
        own[crop, 0:15, 0:part] = jnp.concatenate([rows[:, span]] + wider, axis=0)


def vector_scratch():
    return [
        pltpu.VMEM((CROPS, 16, 128), F32),
        pltpu.VMEM((CROPS, 16, 128), F32),
        pltpu.VMEM((BANDS, 16, 128), F32),
    ]


def x_first(n):
    return n in X_FIRST


def halves_of(n):
    return (0, 1) if x_first(n) else (None,)


def part_of(ref, name, part, columns, x_half):
    at = slice(None) if x_half is None else x_half
    if name == "down":
        return ref.at[:, :, :, part, at]
    return ref.at[:, :, :, at, :, pl.ds(part * columns, columns)]


def piece(ref, x_half):
    return ref if x_half is None else ref.at[x_half]


PACE = 8.0
LAGS = (0.0, 13.0, 17.0, 20.5, 23.0, 25.5, 28.0)
SLOT = 0.65


def backward_kernel(
    chunks,
    slots,
    pairs,
    info,
    weights,
    queries,
    keys,
    values,
    attended,
    totals,
    attended_grad,
    mask,
    gain,
    vectors,
    down_bias,
    up_bias,
    out_own,
    up_keep,
    up_got,
    down_keep,
    down_got,
    out_keep,
    out_send,
    firsts_in,
    weight_in,
    tokens_in,
    middle_grad_in,
    grad_patches,
    total_out,
    vector_total,
    specials_out,
    *scratch,
):
    buffers, vector_buffers = scratch[:5], scratch[5:8]
    (
        total,
        out_got,
        joint_got,
        joint_sent,
        loaded,
        query_grad,
        key_grad,
        value_grad,
        firsts,
        weight,
        tokens,
        middle_grad,
        parts,
        got_parts,
        got_far,
        specials,
        send_sems,
        recv_sems,
        load_sems,
        whole_sems,
    ) = scratch[8:]
    step = pl.program_id(0)
    count = len(chunks)
    columns = total.shape[4]
    rows, width = tokens.shape
    place = Place()
    sender = Sender(place, send_sems, recv_sems)
    sums = ChunkSums(place, sender, buffers, total, count)
    vector_sums = VectorSums(place, sender, vector_buffers, vector_total)
    own = buffers[0]
    keeps = dict(up=up_keep, down=down_keep, out=out_keep)
    gots = dict(up=up_got, down=down_got)

    def own_loads(n):
        name, part = chunks[n]
        return [
            pltpu.make_async_copy(
                part_of(keeps[name], name, part, columns, h), piece(own.at[n], h), load_sems.at[n, 0, i]
            )
            for i, h in enumerate(halves_of(n))
        ]

    def got_loads(n):
        name, part = chunks[n]
        return [
            pltpu.make_async_copy(
                part_of(gots[name], name, part, columns, h), piece(loaded.at[n % 2], h), load_sems.at[n, 1, i]
            )
            for i, h in enumerate(halves_of(n))
        ]

    def whole_loads():
        pairs_of = ((weight_in, weight), (firsts_in, firsts), (tokens_in, tokens), (middle_grad_in, middle_grad))
        return [
            pltpu.make_async_copy(a, b, whole_sems.at[i]) for i, (a, b) in enumerate(pairs_of)
        ]

    early = [n for n, (name, _) in enumerate(chunks) if name != "joint"]
    mlp = [n for n in early if chunks[n][0] != "out"]
    out_chunk = early[-1]
    late = [n for n, (name, _) in enumerate(chunks) if name == "joint"]

    for h in halves_of(out_chunk):
        source = part_of(out_send, "out", 0, columns, h)
        sender.add((out_chunk, 0, h), source, piece(out_got, h), "core")
    for n in late:
        sender.add((n, 0), joint_sent.at[n - late[0]], joint_got.at[n - late[0]], "core")
    for index in range(2):
        sender.add(("first", index), parts.at[index], got_parts.at[index], "core")
    sender.add("far", parts.at[2], got_far, "x")
    for name in NEIGHBOURS:
        sender.add(("special", name), specials.at[place.band], specials.at[place.band], name)

    def begin():
        for n in early:
            for copy in own_loads(n):
                copy.start()
        for n in mlp[:2]:
            for copy in got_loads(n):
                copy.start()
        place.greet(PLACES)
        for h in halves_of(out_chunk):
            sender.send((out_chunk, 0, h))

    def early_stage(n, stage):
        if stage == 0:
            for copy in own_loads(n):
                copy.wait()
            if n in mlp:
                for copy in got_loads(n):
                    copy.wait()
                own[n] = own[n] + loaded[n % 2]
                if n + 2 in mlp:
                    for copy in got_loads(n + 2):
                        copy.start()
            else:
                for h in halves_of(n):
                    sender.arrived((n, 0, h))
                own[n] = own[n] + out_got[...]
        sums.step(n, stage)

    def late_stage(n, stage):
        if stage == 0:
            sender.arrived((n, 0))
            own[n] = own[n] + joint_got[n - late[0]]
        sums.step(n, stage)

    events = []
    for n in early:
        for stage in range(sums.steps(n)):
            events.append((PACE * (n // 2) + LAGS[stage] + 0.3 * (n % 2), stage, n))
    events.sort()

    @pl.when(step == 0)
    def _():
        begin()

    slots_per_pair = BANDS * rows // KEY_PART
    plan = {}
    rest = list(events)
    for index in range(pairs * slots_per_pair):
        due = [e for e in rest if e[0] <= SLOT * (index + 1)]
        rest = rest[len(due) :]
        if due:
            plan[index] = due

    def slot(part):
        for pair in range(pairs):
            index = pair * slots_per_pair + part
            if index not in plan:
                continue

            @pl.when(step == pair)
            def _():
                for _, stage, n in plan[index]:
                    early_stage(n, stage)

    @pl.when(step < pairs)
    def _():
        pair = jnp.minimum(step, pairs - 1)
        outs = (query_grad.at[pair], key_grad.at[pair], value_grad.at[pair])
        inputs = (weights, queries, keys, values, attended, totals, attended_grad)
        attend_back_pair(*inputs, outs, slot)

    @pl.when(step == 1)
    def _():
        for copy in whole_loads():
            copy.start()

    @pl.when(step == pairs)
    def _():
        waiting = list(rest)

        def catch_up(time):
            while waiting and waiting[0][0] <= time:
                _, stage, n = waiting.pop(0)
                early_stage(n, stage)

        now = SLOT * pairs * slots_per_pair
        for copy in whole_loads():
            copy.wait()
        grads = (query_grad, key_grad, value_grad)
        for index, block in enumerate((1, 3)):
            parts[index] = first_part(block, rows, *grads, weight).astype(BF16)
            sender.send(("first", index))
            now += 1.2
            catch_up(now)
        parts[2] = first_part(2, rows, *grads, weight).astype(BF16)
        sender.arrived(("first", 1))
        parts[2] = parts[2] + got_parts[1]
        sender.send("far")
        now += 1.2
        catch_up(now)
        for n in (late[1], late[2], late[0]):
            part = chunks[n][1]
            low = firsts[0:rows, :] if part == 0 else firsts[...]
            keep, send = own_half(joint_columns(low, grads[part]), place.band)
            shape = (2, 2, 2, 2, width // CROPS // 2, columns)
            keep, send = keep.reshape(shape), send.reshape(shape)
            for h in halves_of(n):
                picked = send if h is None else send[:, :, :, h]
                kept = keep if h is None else keep[:, :, :, h]
                if h is None:
                    joint_sent[n - late[0]] = picked
                    own[n] = kept
                else:
                    joint_sent[n - late[0], h] = picked
                    own[n, h] = kept
            sender.send((n, 0))
            now += 2.5
            catch_up(now)
        first_grad = first_part(0, rows, *grads, weight)
        biases = bias_sums(info, slots, rows, query_grad, value_grad)
        for n in (late[1], late[2], late[0]):
            late_stage(n, 0)
        now += 2.5
        catch_up(now)
        start = now
        for n in late:
            for stage in range(1, sums.steps(n)):
                lag = start + 6.0 + 3.0 * stage + (3.0 if n == late[2] else 0.0)
                waiting.append((lag, stage, n))
        waiting.sort()

        def finish_until(time):
            while waiting and waiting[0][0] <= time:
                _, stage, n = waiting.pop(0)
                (late_stage if n in late else early_stage)(n, stage)

        finish_until(start + FIRST_LAG)
        sender.arrived(("first", 0))
        sender.arrived("far")
        first_grad = first_grad + got_parts[0].astype(F32) + got_far[...].astype(F32)
        patches, special_grad, rows_of = first_back(
            slots, info, first_grad, tokens, middle_grad, mask, gain
        )
        grad_patches[...] = patches
        specials[place.band] = jnp.concatenate([out_own[0:4], special_grad[0:4]], axis=0)
        for name in NEIGHBOURS:
            sender.send(("special", name))
        packed = jnp.concatenate([vectors[0:5]] + rows_of + [biases[0:2], down_bias[...]], axis=0)
        pack_vectors(vector_sums.own, packed, up_bias, width // CROPS)
        vector_sums.spread()
        finish_until(start + FIRST_LAG + 8.0)
        vector_sums.share()
        finish_until(start + FIRST_LAG + 12.0)
        vector_sums.close()
        finish_until(1e9)
        for name in NEIGHBOURS:
            sender.arrived(("special", name))
        specials_out[...] = specials[...]
        sender.finish()
        copy = pltpu.make_async_copy(total, total_out, whole_sems.at[4])
        copy.start()
        copy.wait()


FIRST_LAG = 8.0


def finish_kernel(
    chunks,
    special_count,
    total,
    vector_total,
    specials,
    up,
    down,
    out,
    joint,
    up_bias,
    out_specials,
    grad_specials,
    *vectors,
):
    _, _, _, rows, columns = total.shape
    refs = dict(up=up, down=down, out=out, joint=joint)
    for n, (name, part) in enumerate(chunks):
        for core in range(2):
            for x in range(2):
                row, column = x * rows, core * columns
                if name == "down":
                    row += 2 * rows * part
                else:
                    column += 2 * columns * part
                value = total[n, core, x].astype(F32)
                refs[name][row : row + rows, column : column + columns] = value
    part = vectors[0].shape[0]
    for i, vector in enumerate(vectors):
        vector[...] = vector_total[i, 0:part]
    up_bias[...] = jnp.concatenate([vector_total[i : i + 1, 0:part] for i in range(11, 15)], axis=1)[0]
    for first, target in ((0, out_specials), (4, grad_specials)):
        picked = [
            specials[s % BANDS, first + s // BANDS : first + s // BANDS + 1]
            for s in range(special_count)
        ]
        target[0] = jnp.concatenate(picked, axis=0).astype(BF16)


def backward_fused(given, slots, special_count):
    g = given
    rows, width = g["tokens"].shape
    hidden_width = g["up_bias_grad"].shape[1]
    every = BANDS * rows
    pairs = width // PAIR
    chunks = chunk_list(hidden_width // width)
    count = len(chunks)
    part = width // CROPS
    unit_rows, columns = part // 2, width // 2
    unit = (2, 2, 2, 2, unit_rows, columns)
    hidden_parts = hidden_width // width
    shaped = jax.ShapeDtypeStruct
    last = pairs - 1
    own_pair = pl.BlockSpec((rows, PAIR), lambda i: (0, jnp.minimum(i, last)))
    all_pair = pl.BlockSpec((every, PAIR), lambda i: (0, jnp.minimum(i, last)))
    kept = pl.BlockSpec((1, 2 * rows, every), lambda i: (jnp.minimum(i, last), 0, 0))
    up_shape = (2, 2, 2, 2, unit_rows, hidden_parts * columns)
    down_shape = (2, 2, 2, hidden_parts, 2, unit_rows, columns)
    grad_patches, total, vector_total, specials = pl.pallas_call(
        partial(backward_kernel, chunks, slots, pairs),
        grid=(pairs + 1,),
        out_shape=[
            shaped((slots, width), BF16),
            shaped((count, 2, 2, unit_rows, columns), BF16),
            shaped((16, 128), F32),
            shaped((BANDS, 8, width), F32),
        ],
        in_specs=[SMEM, kept, own_pair, all_pair, all_pair, own_pair, own_pair, own_pair]
        + [VMEM] * 6
        + [ANY] * 10,
        out_specs=[VMEM, ANY, VMEM, VMEM],
        scratch_shapes=chunk_scratch(count, unit_rows, columns)
        + vector_scratch()
        + [
            pltpu.VMEM((count, 2, 2, unit_rows, columns), BF16),
            pltpu.VMEM(unit, BF16),
            pltpu.VMEM((3,) + unit, BF16),
            pltpu.VMEM((3,) + unit, BF16),
            pltpu.VMEM((2,) + unit, BF16),
            pltpu.VMEM((pairs, rows, PAIR), BF16),
            pltpu.VMEM((pairs, every, PAIR), BF16),
            pltpu.VMEM((pairs, every, PAIR), BF16),
            pltpu.VMEM((every, width), BF16),
            pltpu.VMEM((width, 3 * width), BF16),
            pltpu.VMEM((rows, width), F32),
            pltpu.VMEM((rows, width), F32),
            pltpu.VMEM((3, rows, width), BF16),
            pltpu.VMEM((2, rows, width), BF16),
            pltpu.VMEM((rows, width), BF16),
            pltpu.VMEM((BANDS, 8, width), F32),
            pltpu.SemaphoreType.DMA((10 * count,)),
            pltpu.SemaphoreType.DMA((10 * count,)),
            pltpu.SemaphoreType.DMA((count, 2, 2)),
            pltpu.SemaphoreType.DMA((5,)),
        ],
        compiler_params=pltpu.CompilerParams(
            vmem_limit_bytes=VMEM_LIMIT, collective_id=0, has_side_effects=True
        ),
        name="backward",
    )(
        g["info"],
        g["weights"],
        g["queries"],
        g["keys"],
        g["values"],
        g["attended"],
        g["totals"],
        g["attended_grad"],
        g["mask"],
        g["first_gain"],
        g["vectors"],
        g["down_bias_grad"],
        g["up_bias_grad"],
        g["out_own"],
        g["up_keep"].reshape(up_shape),
        g["up_got"].reshape(up_shape),
        g["down_keep"].reshape(down_shape),
        g["down_got"].reshape(down_shape),
        g["out_keep"].reshape(unit),
        g["out_send"].reshape(unit),
        g["firsts"],
        g["joint_weight"],
        g["tokens"],
        g["middle_grad"],
    )
    special = shaped((1, special_count, width), BF16)
    results = pl.pallas_call(
        partial(finish_kernel, chunks, special_count),
        out_shape=[
            shaped((part, hidden_width), F32),
            shaped((hidden_width // CROPS, width), F32),
            shaped((part, width), F32),
            shaped((part, 3 * width), F32),
            shaped((hidden_width // CROPS,), F32),
            special,
            special,
        ]
        + [shaped((part,), F32)] * 11,
        in_specs=[VMEM] * 3,
        out_specs=[VMEM] * 18,
        compiler_params=params(),
        name="finish",
    )(total, vector_total, specials)
    up, down, out, joint, up_bias, out_specials, grad_specials = results[:7]
    return grad_patches, up, down, out, joint, results[7:], up_bias, out_specials, grad_specials


def body(
    patches,
    specials,
    patch_mask,
    band_rows,
    mask_token,
    first_gain,
    first_shift,
    joint_weight,
    query_bias,
    value_bias,
    out_weight,
    out_bias,
    first_scale,
    second_gain,
    second_shift,
    up_weight,
    up_bias,
    down_weight,
    down_bias,
    second_scale,
    cot_patches,
    cot_specials,
):
    slots, width = patches.shape[1:]
    special_count = specials.shape[1]
    hidden_width = up_weight.shape[1]
    owned = -(-special_count // BANDS)
    rows = round_up(slots + owned, 16)
    pad = rows - slots
    every = BANDS * rows
    pairs = width // PAIR
    band = lax.axis_index("band")
    relatives = [band ^ r for r in range(BANDS)]
    info = jnp.stack(
        [band_rows[b] * GRID for b in relatives]
        + [(special_count - b + BANDS - 1) // BANDS for b in relatives]
        + [band]
    ).astype(jnp.int32)
    mask = patch_mask
    patches, specials = patches[0], specials[0]
    cot_patches, cot_specials = cot_patches[0], cot_specials[0]
    shaped = jax.ShapeDtypeStruct

    tokens, first = pl.pallas_call(
        partial(first_kernel, slots),
        out_shape=[shaped((rows, width), F32), shaped((rows, width), BF16)],
        in_specs=[SMEM] + [VMEM] * 6,
        compiler_params=params(),
        name="first",
    )(info, mask, patches, specials, mask_token, first_gain, first_shift)

    firsts = gather_blocks(first)

    block = pl.BlockSpec((rows, width), lambda i: (i, 0))
    queries, keys, values = pl.pallas_call(
        partial(project_kernel, slots),
        grid=(BANDS,),
        out_shape=[
            shaped((rows, width), BF16),
            shaped((every, width), BF16),
            shaped((every, width), BF16),
        ],
        in_specs=[SMEM, block, whole((width, 3 * width)), VMEM, VMEM],
        out_specs=[whole((rows, width)), block, block],
        compiler_params=params(),
        name="project",
    )(info, firsts, joint_weight, query_bias, value_bias)

    own_pair = pl.BlockSpec((rows, PAIR), lambda i: (0, i))
    all_pair = pl.BlockSpec((every, PAIR), lambda i: (0, i))
    kept = pl.BlockSpec((1, 2 * rows, every), lambda i: (i, 0, 0))
    attended, totals, weights = pl.pallas_call(
        partial(attend_kernel, slots),
        grid=(pairs,),
        out_shape=[
            shaped((rows, width), F32),
            shaped((rows, width), F32),
            shaped((pairs, 2 * rows, every), BF16),
        ],
        in_specs=[SMEM, own_pair, all_pair, all_pair],
        out_specs=[own_pair, own_pair, kept],
        compiler_params=params(),
        name="attend",
    )(info, queries, keys, values)

    branch, middle, second, incoming, down_in, down_keep, down_send, down_bias_grad = pl.pallas_call(
        partial(middle_kernel, slots),
        out_shape=[
            shaped((rows, width), F32),
            shaped((rows, width), F32),
            shaped((rows, width), BF16),
            shaped((rows, width), F32),
            shaped((rows, width), BF16),
            shaped((rows, width // 2), BF16),
            shaped((rows, width // 2), BF16),
            shaped((1, width), F32),
        ],
        in_specs=[SMEM] + [VMEM] * 10,
        out_specs=[VMEM] * 8,
        compiler_params=params(),
        name="middle",
    )(
        info,
        attended,
        tokens,
        out_weight,
        out_bias,
        first_scale,
        second_gain,
        second_shift,
        second_scale,
        cot_patches,
        cot_specials,
    )

    steps = hidden_width // width
    half = width // 2
    (
        branch_two,
        second_grad,
        up_keep,
        up_send,
        up_bias_grad,
        down_grad_keep,
        down_grad_send,
    ) = pl.pallas_call(
        mlp_kernel,
        grid=(steps,),
        out_shape=[
            shaped((rows, width), F32),
            shaped((rows, width), F32),
            shaped((width, hidden_width // 2), BF16),
            shaped((width, hidden_width // 2), BF16),
            shaped((1, hidden_width), F32),
            shaped((hidden_width, half), BF16),
            shaped((hidden_width, half), BF16),
        ],
        in_specs=[
            SMEM,
            whole((rows, width)),
            whole((rows, width)),
            whole((rows, half)),
            whole((rows, half)),
            pl.BlockSpec((width, width), lambda i: (0, i)),
            pl.BlockSpec((1, width), lambda i: (0, i)),
            pl.BlockSpec((width, width), lambda i: (i, 0)),
        ],
        out_specs=[
            whole((rows, width)),
            whole((rows, width)),
            pl.BlockSpec((width, half), lambda i: (0, i)),
            pl.BlockSpec((width, half), lambda i: (0, i)),
            pl.BlockSpec((1, width), lambda i: (0, i)),
            pl.BlockSpec((width, half), lambda i: (i, 0)),
            pl.BlockSpec((width, half), lambda i: (i, 0)),
        ],
        compiler_params=params(),
        name="mlp",
    )(info, second, down_in, down_keep, down_send, up_weight, up_bias.reshape(1, -1), down_weight)
    up_got = swap(up_send, "band", 1)
    down_got = swap(down_grad_send, "band", 1)

    out_patches, out_own, middle_grad, attended_grad, out_keep, out_send, vectors = pl.pallas_call(
        partial(middle_back_kernel, slots),
        out_shape=[
            shaped((slots, width), BF16),
            shaped((pad, width), F32),
            shaped((rows, width), F32),
            shaped((rows, width), F32),
            shaped((width, half), BF16),
            shaped((width, half), BF16),
            shaped((8, width), F32),
        ],
        in_specs=[SMEM] + [VMEM] * 11,
        out_specs=[VMEM] * 7,
        compiler_params=params(),
        name="middle_back",
    )(
        info,
        middle,
        branch,
        branch_two,
        second_grad,
        incoming,
        attended,
        out_weight,
        down_bias,
        second_scale,
        second_gain,
        first_scale,
    )

    given = dict(
        info=info,
        weights=weights,
        queries=queries,
        keys=keys,
        values=values,
        attended=attended,
        totals=totals,
        attended_grad=attended_grad,
        mask=mask,
        first_gain=first_gain,
        vectors=vectors,
        down_bias_grad=down_bias_grad,
        up_bias_grad=up_bias_grad,
        out_own=out_own,
        up_keep=up_keep,
        up_got=up_got,
        down_keep=down_grad_keep,
        down_got=down_got,
        out_keep=out_keep,
        out_send=out_send,
        firsts=firsts,
        joint_weight=joint_weight,
        tokens=tokens,
        middle_grad=middle_grad,
    )
    backward = backward_fused if lax.axis_size("crop") == CROPS else backward_general
    (
        grad_patches,
        up,
        down,
        out,
        joint,
        rows_of,
        up_bias_sum,
        out_specials,
        grad_specials,
    ) = backward(given, slots, special_count)
    return (
        out_patches[None],
        out_specials,
        grad_patches[None],
        grad_specials,
        rows_of[5],
        rows_of[6],
        rows_of[7],
        joint,
        rows_of[8],
        rows_of[9],
        out,
        rows_of[4],
        rows_of[3],
        rows_of[1],
        rows_of[2],
        up,
        up_bias_sum,
        down,
        rows_of[10],
        rows_of[0],
    )


def solution(mesh):
    split = P("crop", "band", None)
    special = P("crop", None, None)
    in_specs = (
        (split, special, P("crop", "band")) + (P(),) * 17 + (split, special)
    )
    line, matrix = P("crop"), P("crop", None)
    out_specs = (
        split,
        special,
        split,
        special,
        line,
        line,
        line,
        matrix,
        line,
        line,
        matrix,
        line,
        line,
        line,
        line,
        matrix,
        line,
        matrix,
        line,
        line,
    )
    return jax.shard_map(body, mesh=mesh, in_specs=in_specs, out_specs=out_specs, check_vma=False)
```

time: 252 us -> 211 us (0.84)
  Pallas kernels: 201 us -> 180 us
  waiting for transfers between devices: 32.9 us -> 14.9 us
    pallas_call x6 -> x3, Pallas kernels: 144 us -> 122 us  [the longest x1 115 us: backward_fused(): pl.pallas_call(partial(backward_kernel, chunks, slots, pairs), grid=(pair...]
    ppermute x5, waiting for transfers between devices: 32.9 us -> 14.9 us  [swap(): return lax.ppermute(x, axis, [(i, i ^ distance) for i in range(size)])]
  transfers between devices with their start and end apart: 5 -> 5, of which waited for: 4 -> 2; matrix products, arithmetic and copies ran while one was open for 0% -> 1% of each run, Pallas kernels for 0% -> 4%
where the time goes in v1:
time: 211 us; the launch traced here: 210 us
  Pallas kernels  180 us (85%)
  waiting for transfers between devices  14.9 us (7%)
  local copies, waits for them, and re-layouts  7.1 us (3%)
  starting transfers between devices  4.8 us (2%)
  between operations  3.45 us (2%)
    pallas_call x1, Pallas kernels, backward_fused(): pl.pallas_call(partial(backward_kernel, chunks, slots, pairs), grid=(pair...  115 us
    pallas_call x1, Pallas kernels, body(): pl.pallas_call(mlp_kernel, grid=(steps,), out_shape=[shaped((rows, width)...  20.3 us
    pallas_call x1, Pallas kernels, body(): pl.pallas_call(partial(attend_kernel, slots), grid=(pairs,), out_shape=[s...  15.3 us
    ppermute x5, waiting for transfers between devices, swap(): return lax.ppermute(x, axis, [(i, i ^ distance) for i in range(size)])  14.9 us
    pallas_call x1, Pallas kernels, body(): pl.pallas_call(partial(project_kernel, slots), grid=(BANDS,), out_shape=[...  9.15 us
    pallas_call x1, Pallas kernels, body(): pl.pallas_call(partial(middle_back_kernel, slots), out_shape=[shaped((slo...  7.93 us
    pallas_call x1, Pallas kernels, body(): pl.pallas_call(partial(middle_kernel, slots), out_shape=[shaped((rows, wi...  5.77 us
    unnamed x10, local copies, waits for them, and re-layouts  5.04 us
  transfers between devices with their start and end apart: 5, of which 2 were waited for; matrix products, arithmetic and copies ran while one was open for 1% of the time, Pallas kernels for 4%

profile of v1, /device:TPU:1, one launch (start us, length us, event | category | flops | bytes accessed | tf_op | source)
XLA Modules:
  0.0 210.4 jit_solution(15582204751439870884)
XLA Ops:
  0.7 1.4 fusion
  4.8 0.6 stack.27.info
  5.4 2.7 %first.1 = (f32[448,768]{1,0:T(8,128)}, bf16[448,768]{1,0:T(8,128)(2,1)}) custom-call(s32[9]{0:T(128)} %stack.27.info, s32[1,444]{1,0:T(1,128)} %mask.3, bf16[444,768]{1,0:T(8,128)(2,1)} %bitcast.22, bf16[5,768]{1,0:T(8,128)(2,1)} %bitcast.28, f32[768]{0:T(1024)} %token_.1, f32[768]{0:T(1024)} %gain.7, f32[768]{0:T(1024)} %shift.2), custom_call_target="tpu_custom_call" | custom-call | tf_op jit(solution)/shard_map/first/pallas_call | solution.py:1266
  8.1 2.0 collective-permute-start.1
  10.1 1.0 collective-permute-start
  11.1 14.4 %collective-permute-done.1 = bf16[448,768]{1,0:T(8,128)(2,1)S(1)} collective-permute-done((bf16[448,768]{1,0:T(8,128)(2,1)}, bf16[448,768]{1,0:T(8,128)(2,1)S(1)}, u32[]{:S(2)}, u32[]{:S(2)}) %collective-permute-start.1) | collective-permute-done | bytes 688160 | tf_op jit(solution)/shard_map/ppermute | solution.py:379
  25.5 1.2 collective-permute-start.2
  26.7 1.1 constant_dynamic-update-slice_fusion.3
  27.9 0.0 collective-permute-done
  28.0 0.5 collective-permute-done.2
  28.6 0.0 copy-start
  28.6 1.6 copy-done
  30.1 9.1 %project.1 = (bf16[448,768]{1,0:T(8,128)(2,1)}, bf16[1792,768]{1,0:T(8,128)(2,1)}, bf16[1792,768]{1,0:T(8,128)(2,1)}) custom-call(s32[9]{0:T(128)} %stack.27.info, bf16[1792,768]{1,0:T(8,128)(2,1)} %copy-done, bf16[768,2304]{1,0:T(8,128)(2,1)} %weight_in.1, f32[768]{0:T(1024)} %query_bias.1, f32[768]{0:T(1024)} %value_bias.1), custom_call_target="tpu_custom_call" | custom-call | tf_op jit(solution)/shard_map/project/pallas_call | solution.py:1277
  39.3 15.3 %attend.1 = (f32[448,768]{1,0:T(8,128)}, f32[448,768]{1,0:T(8,128)}, bf16[6,896,1792]{2,1,0:T(8,128)(2,1)}) custom-call(s32[9]{0:T(128)} %stack.27.info, bf16[448,768]{1,0:T(8,128)(2,1)} %get-tuple-element.73.queries, bf16[1792,768]{1,0:T(8,128)(2,1)} %get-tuple-element.74.keys, bf16[1792,768]{1,0:T(8,128)(2,1)} %get-tuple-element.75.values), custom_call_target="tpu_custom_call" | custom-call | tf_op jit(solution)/shard_map/attend/pallas_call | solution.py:1294
  54.6 5.8 %middle.1 = (f32[448,768]{1,0:T(8,128)}, f32[448,768]{1,0:T(8,128)}, bf16[448,768]{1,0:T(8,128)(2,1)}, f32[448,768]{1,0:T(8,128)}, bf16[448,768]{1,0:T(8,128)(2,...) custom-call(s32[9]{0:T(128)} %stack.27.info, f32[448,768]{1,0:T(8,128)} %get-tuple-element.76.attended, ...), custom_call_target="tpu_custom_call" | custom-call | tf_op jit(solution)/shard_map/middle/pallas_call | solution.py:1308
  60.4 20.3 %mlp.1 = (f32[448,768]{1,0:T(8,128)}, f32[448,768]{1,0:T(8,128)}, bf16[768,1536]{1,0:T(8,128)(2,1)}, bf16[768,1536]{1,0:T(8,128)(2,1)}, f32[1,3072]{1,0:T(1,128)...) custom-call(s32[9]{0:T(128)} %stack.27.info, bf16[448,768]{1,0:T(8,128)(2,1)} %get-tuple-element.80.second, ...), custom_call_target="tpu_custom_call" | custom-call | tf_op jit(solution)/shard_map/mlp/pallas_call | solution.py:1348
  80.7 0.4 collective-permute-start.3
  81.1 0.1 collective-permute-start.4
  81.2 7.9 %middle_back.1 = (bf16[444,768]{1,0:T(8,128)(2,1)}, f32[4,768]{1,0:T(4,128)}, f32[448,768]{1,0:T(8,128)}, f32[448,768]{1,0:T(8,128)}, bf16[768,384]{1,0:T(8,128)...) custom-call(s32[9]{0:T(128)} %stack.27.info, f32[448,768]{1,0:T(8,128)} %get-tuple-element.78.middle, ...), custom_call_target="tpu_custom_call" | custom-call | tf_op jit(solution)/shard_map/middle_back/pallas_call | solution.py:1385
  89.2 0.0 collective-permute-done.3
  89.2 0.0 copy-start.1
  89.2 0.0 collective-permute-done.4
  89.2 1.4 copy-done.1
  90.6 115.4 %backward.1 = (bf16[444,768]{1,0:T(8,128)(2,1)}, bf16[12,2,2,48,384]{4,3,2,1,0:T(8,128)(2,1)}, f32[16,128]{1,0:T(8,128)}, f32[4,8,768]{2,1,0:T(8,128)}) custom-call(s32[9]{0:T(128)} %stack.27.info, bf16[6,896,1792]{2,1,0:T(8,128)(2,1)} %get-tuple-element.88.weights, bf16[448,768]{1,0:T(8,128)(2,1)} %get-tuple-element.73.queries, ...), custom_call_target="tpu_custom_call" | custom-call | tf_op jit(solution)/shard_map/backward/pallas_call | solution.py:1133
  206.0 0.0 copy-start.2
  206.0 3.5 %finish.1 = (f32[96,3072]{1,0:T(8,128)}, f32[384,768]{1,0:T(8,128)}, f32[96,768]{1,0:T(8,128)}, f32[96,2304]{1,0:T(8,128)}, f32[384]{0:T(512)}, /*index=5*/bf16[...) custom-call(bf16[12,2,2,48,384]{4,3,2,1,0:T(8,128)(2,1)} %get-tuple-, ...), custom_call_target="tpu_custom_call" | custom-call | tf_op jit(solution)/shard_map/finish/pallas_call | solution.py:1201
  209.5 0.0 copy-done.2
  209.5 0.8 copy.46
  (3 shorter events, 0.1 us)
Async XLA Ops:
  8.1 17.4 %collective-permute-start.1 = (bf16[448,768]{1,0:T(8,128)(2,1)}, bf16[448,768]{1,0:T(8,128)(2,1)S(1)}, u32[]{:S(2)}, u32[]{:S(2)}) collective-permute-start(bf16[448,768]{1,0:T(8,128)(2,1)} %get-tuple-element.72), channel_id=1, source_target_pairs={{0,16},{8,24},{16,0},{24,8},{1,17},{9,25},{17,1},{25,9},{2,18},{10... | collective-permute-start | bytes 2064392 | tf_op jit(solution)/shard_map/ppermute | solution.py:379
  10.1 17.7 %collective-permute-start = (bf16[448,768]{1,0:T(8,128)(2,1)}, bf16[448,768]{1,0:T(8,128)(2,1)S(1)}, u32[]{:S(2)}, u32[]{:S(2)}) collective-permute-start(bf16[448,768]{1,0:T(8,128)(2,1)} %get-tuple-element.72), channel_id=1, source_target_pairs={{0,8},{8,0},{16,24},{24,16},{1,9},{9,1},{17,25},{25,17},{2,10},{10... | collective-permute-start | bytes 2064392 | tf_op jit(solution)/shard_map/ppermute | solution.py:379
  25.5 3.0 %collective-permute-start.2 = (bf16[448,768]{1,0:T(8,128)(2,1)S(1)}, bf16[448,768]{1,0:T(8,128)(2,1)S(1)}, u32[]{:S(2)}, u32[]{:S(2)}) collective-permute-start(bf16[448,768]{1,0:T(8,128)(2,1)S(1)} %collective-permute-done.1), channel_id=1, source_target_pairs={{0,8},{8,0},{16,24},{24,16},{1,9},{9,1},{17,25},{25,17},{2,10},{10... | collective-permute-start | bytes 2064392 | tf_op jit(solution)/shard_map/ppermute | solution.py:379
  28.6 1.6 copy-start
  80.7 8.5 %collective-permute-start.3 = (bf16[768,1536]{1,0:T(8,128)(2,1)}, bf16[768,1536]{1,0:T(8,128)(2,1)S(1)}, u32[]{:S(2)}, u32[]{:S(2)}) collective-permute-start(bf16[768,1536]{1,0:T(8,128)(2,1)} %get-tuple-element.96), channel_id=1, source_target_pairs={{0,8},{8,0},{16,24},{24,16},{1,9},{9,1},{17,25},{25,17},{2,10},{10... | collective-permute-start | bytes 7077896 | tf_op jit(solution)/shard_map/ppermute | solution.py:379
  81.1 8.1 %collective-permute-start.4 = (bf16[3072,384]{1,0:T(8,128)(2,1)}, bf16[3072,384]{1,0:T(8,128)(2,1)}, u32[]{:S(2)}, u32[]{:S(2)}) collective-permute-start(bf16[3072,384]{1,0:T(8,128)(2,1)} %get-tuple-element.98), channel_id=1, source_target_pairs={{0,8},{8,0},{16,24},{24,16},{1,9},{9,1},{17,25},{25,17},{2,10},{10... | collective-permute-start | bytes 7077896 | tf_op jit(solution)/shard_map/ppermute | solution.py:379
  89.2 1.4 copy-start.1
  206.0 3.5 %copy-start.2 = (bf16[444,768]{1,0:T(8,128)(2,1)S(1)}, bf16[444,768]{1,0:T(8,128)(2,1)}, u32[]{:S(2)}) copy-start(bf16[444,768]{1,0:T(8,128)(2,1)} %get-tuple-element.106) | copy-start | bytes 2045956

commit v2 on v1

--- a/solution.py
+++ b/solution.py
@@ -119,40 +119,169 @@
     first[...] = jnp.where(counted, hat * line(gain) + line(shift), 0.0).astype(BF16)
 
 
+def split_pairs(ref, rows, value):
+    for pair in range(ref.shape[0]):
+        ref[pair, rows, :] = value[:, pair * PAIR : (pair + 1) * PAIR].astype(BF16)
+
+
+def project_keys(low, weight, value_bias, counted, keys, values, rows):
+    width = weight.shape[0]
+    split_pairs(keys, rows, dot(low, weight[:, width : 2 * width]))
+    value = dot(low, weight[:, 2 * width :]) + line(value_bias)
+    split_pairs(values, rows, jnp.where(counted, value, 0.0))
+
+
+def attend_pair(queries, keys, values, ones):
+    factor = HEAD ** (-0.5)
+    stacked = stack_pair((queries.astype(F32) * factor).astype(BF16))
+    low = jnp.exp(dot_nt(stacked, keys)).astype(BF16)
+    summed = dot(low, jnp.concatenate([values, ones], axis=1))
+    return low, unstack_pair(summed[:, :PAIR]), unstack_pair(summed[:, PAIR:])
+
+
 def project_kernel(slots, info, first, weight, query_bias, value_bias, queries, keys, values):
     relative = pl.program_id(0)
-    rows, width = queries.shape
+    rows, width = first.shape
     counted = counted_rows(info, relative, rows, slots, width)
     low = first[...]
 
     @pl.when(relative == 0)
     def _():
-        queries[...] = (dot(low, weight[:, :width]) + line(query_bias)).astype(BF16)
-
-    keys[...] = dot(low, weight[:, width : 2 * width]).astype(BF16)
-    values[...] = jnp.where(
-        counted, dot(low, weight[:, 2 * width :]) + line(value_bias), 0.0
-    ).astype(BF16)
-
-
-def attend_kernel(slots, info, queries, keys, values, attended, totals, weights):
-    rows = queries.shape[0]
-    factor = HEAD ** (-0.5)
-    stacked = stack_pair((queries[...].astype(F32) * factor).astype(BF16))
-    scores = dot_nt(stacked, keys[...])
-    low = jnp.exp(scores).astype(BF16)
+        split_pairs(queries, slice(None), dot(low, weight[:, :width]) + line(query_bias))
+
+    project_keys(low, weight, value_bias, counted, keys, values, slice(None))
+
+
+def attend_kernel(
+    slots, info, queries, keys, values, firsts, attended, totals, weights, firsts_t
+):
+    rows = queries.shape[1]
+    ones = [
+        counted_rows(info, r, rows, slots, PAIR).astype(F32).astype(BF16) for r in range(BANDS)
+    ]
+    low, summed, total = attend_pair(
+        queries[0], keys[0], values[0], jnp.concatenate(ones, axis=0)
+    )
     weights[0] = low
-    ones = jnp.concatenate(
-        [
-            counted_rows(info, r, rows, slots, PAIR).astype(F32).astype(BF16)
-            for r in range(BANDS)
-        ],
-        axis=0,
+    firsts_t[...] = firsts[...].astype(F32).T.astype(BF16)
+    attended[...] = summed / total
+    totals[...] = total
+
+
+def forward_kernel(
+    slots,
+    pairs,
+    info,
+    mask,
+    patches,
+    specials,
+    token,
+    gain,
+    shift,
+    query_bias,
+    value_bias,
+    weight_in,
+    tokens_out,
+    queries_out,
+    keys_out,
+    values_out,
+    attended,
+    totals,
+    weights,
+    firsts_t,
+    tokens,
+    firsts,
+    queries,
+    keys,
+    values,
+    ones,
+    sums,
+    counts,
+    weight,
+    send_sems,
+    recv_sems,
+    sems,
+):
+    step = pl.program_id(0)
+    rows, width = tokens.shape
+    half_rows = 2 * rows
+    place = Place()
+    sender = Sender(place, send_sems, recv_sems)
+    sender.add("near", firsts.at[0], firsts.at[1], "core")
+    sender.add("far", firsts.at[0], firsts.at[2], "x")
+    sender.add("diagonal", firsts.at[2], firsts.at[3], "core")
+    weight_load = lambda: pltpu.make_async_copy(weight_in, weight, sems.at[0])
+    stores = lambda: [
+        pltpu.make_async_copy(a, b, sems.at[i])
+        for i, (a, b) in enumerate(
+            ((tokens, tokens_out), (queries, queries_out), (keys, keys_out), (values, values_out)), 1
+        )
+    ]
+
+    def block_keys(block):
+        counted = counted_rows(info, block, rows, slots, width)
+        span = pl.ds(block * rows, rows)
+        project_keys(firsts[block], weight, value_bias, counted, keys, values, span)
+
+    @pl.when(step == 0)
+    def _():
+        weight_load().start()
+        filled = jnp.where(mask_column(mask), line(token), patches[...].astype(F32))
+        place_rows(tokens, filled, specials[...].astype(F32), place.band)
+        hat, _ = normalize(tokens[...])
+        counted = counted_rows(info, 0, rows, slots, width)
+        firsts[0] = jnp.where(counted, hat * line(gain) + line(shift), 0.0).astype(BF16)
+        place.greet(("core", "x"))
+        sender.send("near")
+        sender.send("far")
+        for block in range(BANDS):
+            used = counted_rows(info, block, rows, slots, PAIR)
+            ones[block * rows : (block + 1) * rows, :] = used.astype(F32).astype(BF16)
+        weight_load().wait()
+        split_pairs(queries, slice(None), dot(firsts[0], weight[:, :width]) + line(query_bias))
+        block_keys(0)
+        sender.arrived("near")
+        block_keys(1)
+
+    @pl.when(step == pairs)
+    def _():
+        sender.arrived("far")
+        sender.send("diagonal")
+        block_keys(2)
+        sender.arrived("diagonal")
+        block_keys(3)
+        for copy in stores():
+            copy.start()
+
+    far_half = step >= pairs
+    pair = jnp.where(far_half, step - pairs, step)
+    first_row = pl.multiple_of(jnp.where(far_half, half_rows, 0), half_rows)
+    span = pl.ds(first_row, half_rows)
+    low, summed, total = attend_pair(
+        queries[pair], keys[pair, span], values[pair, span], ones[span, :]
     )
-    summed = dot(low, jnp.concatenate([values[...], ones], axis=1))
-    total = unstack_pair(summed[:, PAIR:])
-    attended[...] = unstack_pair(summed[:, :PAIR]) / total
-    totals[...] = total
+    weights[0] = low
+    first_block = jnp.where(far_half, 2, 0)
+    lane = pl.ds(pl.multiple_of(pair * PAIR, PAIR), PAIR)
+    columns = [firsts[first_block + i, :, lane] for i in range(2)]
+    firsts_t[...] = jnp.concatenate(columns, axis=0).astype(F32).T.astype(BF16)
+
+    @pl.when(step < pairs)
+    def _():
+        sums[pair] = summed
+        counts[pair] = total
+
+    @pl.when(far_half)
+    def _():
+        whole_total = counts[pair] + total
+        attended[...] = (sums[pair] + summed) / whole_total
+        totals[...] = whole_total
+
+    @pl.when(step == 2 * pairs - 1)
+    def _():
+        sender.finish()
+        for copy in stores():
+            copy.wait()
 
 
 def middle_kernel(
@@ -302,9 +431,9 @@
 
 
 def attend_back_pair(weights, queries, keys, values, attended, totals, attended_grad, outs, between):
-    query_grad, key_grad, value_grad = outs
+    key_grad, value_grad = outs
+    queries, keys, values = queries.at[0], keys.at[0], values.at[0]
     rows = queries.shape[0]
-    every = keys.shape[0]
     factor = HEAD ** (-0.5)
     stacked = stack_pair((queries[...].astype(F32) * factor).astype(BF16))
     scaled = attended_grad[...] / totals[...]
@@ -313,8 +442,10 @@
     stacked_t = stacked.astype(F32).T.astype(BF16)
     returned_t = returned.astype(F32).T.astype(BF16)
     total = jnp.zeros((2 * rows, PAIR), F32)
-    for part in range(every // KEY_PART):
-        span = slice(part * KEY_PART, (part + 1) * KEY_PART)
+    start = 0
+    for part, size in enumerate(key_parts(keys.shape[0])):
+        span = slice(start, start + size)
+        start += size
         low = weights[0, :, span]
         moved = dot_nt(returned, values[span, :])
         scores = (low.astype(F32) * (moved - slope)).astype(BF16)
@@ -322,7 +453,14 @@
         key_grad[span, :] = dot(stacked_t, scores).T.astype(BF16)
         value_grad[span, :] = dot(returned_t, low).T.astype(BF16)
         between(part)
-    query_grad[...] = (unstack_pair(total) * factor).astype(BF16)
+    return unstack_pair(total) * factor
+
+
+def key_parts(count):
+    parts = [KEY_PART] * (count // KEY_PART)
+    if count % KEY_PART:
+        parts[-1] += count % KEY_PART
+    return parts
 
 
 def first_part(block, rows, query_grad, key_grad, value_grad, weight):
@@ -340,9 +478,20 @@
     return part
 
 
-def joint_columns(firsts, grad):
-    low = jnp.concatenate([grad[pair] for pair in range(grad.shape[0])], axis=1)
-    return dot_tn(firsts, low).astype(BF16)
+def own_pair_first(part, band):
+    core = lax.rem(band, 2)
+    return 2 * part + core, 2 * part + 1 - core
+
+
+def joint_columns(firsts_t, query_grad, key_grad, value_grad, pairs):
+    rows = query_grad.shape[1]
+    queries = dot(firsts_t[:, :rows], jnp.concatenate([query_grad[p] for p in pairs], axis=1))
+    results = []
+    for index, p in enumerate(pairs):
+        others = dot(firsts_t[...], jnp.concatenate([key_grad[p], value_grad[p]], axis=1))
+        own = queries[:, index * PAIR : (index + 1) * PAIR]
+        results.append(jnp.concatenate([own, others], axis=1).astype(BF16))
+    return results
 
 
 def first_back(slots, info, grad, tokens, middle_grad, mask, gain):
@@ -443,24 +592,25 @@
 def attend_back_kernel(
     weights, queries, keys, values, attended, totals, attended_grad, query_grad, key_grad, value_grad
 ):
-    outs = (query_grad.at[0], key_grad.at[0], value_grad.at[0])
     inputs = (weights, queries, keys, values, attended, totals, attended_grad)
-    attend_back_pair(*inputs, outs, lambda part: None)
+    part = attend_back_pair(*inputs, (key_grad.at[0], value_grad.at[0]), lambda part: None)
+    query_grad[0] = part.astype(BF16)
 
 
 def joint_back_kernel(
-    slots, info, firsts, query_grad, key_grad, value_grad, weight, joint_keep, joint_send, first_grad, sums
+    slots, info, firsts_t, query_grad, key_grad, value_grad, weight, joint_keep, joint_send, first_grad, sums
 ):
     rows, width = query_grad.shape[1], weight.shape[0]
     for block in range(BANDS):
         part = first_part(block, rows, query_grad, key_grad, value_grad, weight)
         first_grad[block * rows : (block + 1) * rows, :] = part.astype(BF16)
-    half = width // 2
-    for part, grad in enumerate((query_grad, key_grad, value_grad)):
-        low = firsts[0:rows, :] if part == 0 else firsts[...]
-        keep, send = own_half(joint_columns(low, grad), info[2 * BANDS])
-        joint_keep[:, part * half : (part + 1) * half] = keep
-        joint_send[:, part * half : (part + 1) * half] = send
+    third = 3 * PAIR
+    for part in range(query_grad.shape[0] // 2):
+        keep, send = joint_columns(
+            firsts_t, query_grad, key_grad, value_grad, own_pair_first(part, info[2 * BANDS])
+        )
+        joint_keep[:, part * third : (part + 1) * third] = keep
+        joint_send[:, part * third : (part + 1) * third] = send
     sums[...] = bias_sums(info, slots, rows, query_grad, value_grad)
 
 
@@ -475,6 +625,12 @@
     vectors[...] = jnp.concatenate(rows + [sums[0:5]], axis=0)
 
 
+def joint_order(x):
+    rows, columns = x.shape
+    x = x.reshape(rows, columns // (3 * PAIR), 3, PAIR)
+    return jnp.transpose(x, (0, 2, 1, 3)).reshape(rows, columns)
+
+
 def backward_general(given, slots, special_count):
     g = given
     rows, width = g["tokens"].shape
@@ -482,7 +638,6 @@
     pairs = width // PAIR
     shaped = jax.ShapeDtypeStruct
     own_pair = pl.BlockSpec((rows, PAIR), lambda i: (0, i))
-    all_pair = pl.BlockSpec((every, PAIR), lambda i: (0, i))
     grads = pl.pallas_call(
         attend_back_kernel,
         grid=(pairs,),
@@ -493,9 +648,9 @@
         ],
         in_specs=[
             pl.BlockSpec((1, 2 * rows, every), lambda i: (i, 0, 0)),
-            own_pair,
-            all_pair,
-            all_pair,
+            pl.BlockSpec((1, rows, PAIR), lambda i: (i, 0, 0)),
+            pl.BlockSpec((1, every, PAIR), lambda i: (i, 0, 0)),
+            pl.BlockSpec((1, every, PAIR), lambda i: (i, 0, 0)),
             own_pair,
             own_pair,
             own_pair,
@@ -529,7 +684,7 @@
         out_specs=[VMEM] * 4,
         compiler_params=params(),
         name="joint_back",
-    )(g["info"], g["firsts"], *grads, g["joint_weight"])
+    )(g["info"], g["firsts_t"], *grads, g["joint_weight"])
     grad_patches, grad_own, more = pl.pallas_call(
         partial(first_back_kernel, slots),
         out_shape=[
@@ -563,14 +718,14 @@
         reduce_half(g["up_keep"], g["up_got"], half),
         reduce_half(g["down_keep"], g["down_got"], half),
         reduce_half(g["out_keep"], swap(g["out_send"], "band", 1), half),
-        reduce_half(joint_keep, swap(joint_send, "band", 1), half),
+        joint_order(reduce_half(joint_keep, swap(joint_send, "band", 1), half)),
     )
     return (grad_patches,) + matrices + small
 
 
 MESH = pl.DeviceIdType.MESH
 CROPS = 8
-X_FIRST = (0, 2, 4, 6, 10)
+X_FIRST = (0, 1, 3, 4, 9, 10)
 NEIGHBOURS = ("core", "x", "diagonal")
 PLACES = NEIGHBOURS + tuple(range(1, CROPS))
 
@@ -791,9 +946,21 @@
     return ref if x_half is None else ref.at[x_half]
 
 
-PACE = 8.0
-LAGS = (0.0, 13.0, 17.0, 20.5, 23.0, 25.5, 28.0)
-SLOT = 0.65
+PLAN = (
+    (0, 0, 0), (0, 1, 0), (0, 2, 0), (0, 3, 0), (0, 5, 0), (0, 6, 0),
+    (7, 4, 0), (7, 7, 0), (9, 0, 1), (9, 2, 1), (16, 2, 2), (16, 1, 1),
+    (16, 5, 1), (18, 8, 0), (19, 2, 3), (19, 3, 1), (19, 6, 1), (22, 5, 2),
+    (24, 2, 4), (24, 6, 2), (24, 4, 1), (24, 7, 1), (26, 5, 3), (26, 0, 2),
+    (26, 9, 0), (27, 2, 5), (29, 6, 3), (29, 1, 2), (30, 7, 2), (32, 0, 3),
+    (33, 1, 3), (33, 8, 1), (33, 10, 0), (36, 7, 3), (36, 3, 2), (37, 0, 4),
+    (38, 4, 2), (38, 11, 0), (39, 8, 2), (40, 1, 4), (40, 5, 4), (40, 6, 4),
+    (40, 3, 3), (40, 4, 3), (40, 9, 1), (45, 8, 3), (45, 11, 1), (47, 5, 5),
+    (48, 3, 4), (49, 6, 5), (50, 10, 1), (51, 4, 4), (52, 9, 2), (53, 7, 4),
+    (54, 0, 5), (55, 1, 5), (56, 11, 2), (57, 7, 5), (58, 10, 2), (59, 8, 4),
+    (60, 9, 3), (61, 0, 6), (62, 3, 5), (63, 1, 6), (64, 4, 5), (65, 8, 5),
+    (66, 11, 3), (67, 3, 6), (68, 4, 6), (69, 10, 3), (70, 11, 4), (71, 9, 4),
+    (72, 10, 4), (73, 9, 5), (74, 11, 5), (75, 10, 5), (76, 9, 6), (77, 10, 6),
+)
 
 
 def backward_kernel(
@@ -837,10 +1004,11 @@
         joint_got,
         joint_sent,
         loaded,
+        query_sum,
         query_grad,
         key_grad,
         value_grad,
-        firsts,
+        firsts_t,
         weight,
         tokens,
         middle_grad,
@@ -878,19 +1046,19 @@
         name, part = chunks[n]
         return [
             pltpu.make_async_copy(
-                part_of(gots[name], name, part, columns, h), piece(loaded.at[n % 2], h), load_sems.at[n, 1, i]
+                part_of(gots[name], name, part, columns, h), piece(loaded.at[mlp.index(n) % 2], h), load_sems.at[n, 1, i]
             )
             for i, h in enumerate(halves_of(n))
         ]
 
     def whole_loads():
-        pairs_of = ((weight_in, weight), (firsts_in, firsts), (tokens_in, tokens), (middle_grad_in, middle_grad))
+        pairs_of = ((weight_in, weight), (firsts_in, firsts_t), (tokens_in, tokens), (middle_grad_in, middle_grad))
         return [
             pltpu.make_async_copy(a, b, whole_sems.at[i]) for i, (a, b) in enumerate(pairs_of)
         ]
 
     early = [n for n, (name, _) in enumerate(chunks) if name != "joint"]
-    mlp = [n for n in early if chunks[n][0] != "out"]
+    mlp = [n for _, n, stage in PLAN if stage == 0 and chunks[n][0] in gots]
     out_chunk = early[-1]
     late = [n for n, (name, _) in enumerate(chunks) if name == "joint"]
 
@@ -923,9 +1091,10 @@
             if n in mlp:
                 for copy in got_loads(n):
                     copy.wait()
-                own[n] = own[n] + loaded[n % 2]
-                if n + 2 in mlp:
-                    for copy in got_loads(n + 2):
+                index = mlp.index(n)
+                own[n] = own[n] + loaded[index % 2]
+                if index + 2 < len(mlp):
+                    for copy in got_loads(mlp[index + 2]):
                         copy.start()
             else:
                 for h in halves_of(n):
@@ -939,42 +1108,48 @@
             own[n] = own[n] + joint_got[n - late[0]]
         sums.step(n, stage)
 
-    events = []
-    for n in early:
-        for stage in range(sums.steps(n)):
-            events.append((PACE * (n // 2) + LAGS[stage] + 0.3 * (n % 2), stage, n))
-    events.sort()
+    def stage_of(n, stage):
+        (late_stage if n in late else early_stage)(n, stage)
+
+    def exchanges(slot):
+        for place_of, n, stage in PLAN:
+            if place_of == slot:
+                stage_of(n, stage)
+
+    def occupied(slot):
+        return any(place_of == slot for place_of, _, _ in PLAN)
+
+    def joint_chunk(part):
+        n = late[part]
+        picked = joint_columns(firsts_t, *grads, own_pair_first(part, place.band))
+        shape = (2, 2, 2, 2, width // CROPS // 2, columns)
+        for value, target in zip(picked, (own.at[n], joint_sent.at[part])):
+            value = value.reshape(shape)
+            for h in halves_of(n):
+                if h is None:
+                    target[...] = value
+                else:
+                    target[h] = value[:, :, :, h]
+        sender.send((n, 0))
+
+    half_rows = 2 * rows
+    per_step = len(key_parts(half_rows))
+
+    def between(part):
+        for index in range(2 * pairs):
+            if occupied(index * per_step + part):
+
+                @pl.when(step == index)
+                def _():
+                    exchanges(index * per_step + part)
+
+    grads = (query_grad, key_grad, value_grad)
+    last = 2 * pairs
+    after = last * per_step
 
     @pl.when(step == 0)
     def _():
         begin()
-
-    slots_per_pair = BANDS * rows // KEY_PART
-    plan = {}
-    rest = list(events)
-    for index in range(pairs * slots_per_pair):
-        due = [e for e in rest if e[0] <= SLOT * (index + 1)]
-        rest = rest[len(due) :]
-        if due:
-            plan[index] = due
-
-    def slot(part):
-        for pair in range(pairs):
-            index = pair * slots_per_pair + part
-            if index not in plan:
-                continue
-
-            @pl.when(step == pair)
-            def _():
-                for _, stage, n in plan[index]:
-                    early_stage(n, stage)
-
-    @pl.when(step < pairs)
-    def _():
-        pair = jnp.minimum(step, pairs - 1)
-        outs = (query_grad.at[pair], key_grad.at[pair], value_grad.at[pair])
-        inputs = (weights, queries, keys, values, attended, totals, attended_grad)
-        attend_back_pair(*inputs, outs, slot)
 
     @pl.when(step == 1)
     def _():
@@ -983,68 +1158,56 @@
 
     @pl.when(step == pairs)
     def _():
-        waiting = list(rest)
-
-        def catch_up(time):
-            while waiting and waiting[0][0] <= time:
-                _, stage, n = waiting.pop(0)
-                early_stage(n, stage)
-
-        now = SLOT * pairs * slots_per_pair
         for copy in whole_loads():
             copy.wait()
-        grads = (query_grad, key_grad, value_grad)
-        for index, block in enumerate((1, 3)):
-            parts[index] = first_part(block, rows, *grads, weight).astype(BF16)
-            sender.send(("first", index))
-            now += 1.2
-            catch_up(now)
+        parts[1] = first_part(3, rows, *grads, weight).astype(BF16)
+        sender.send(("first", 1))
         parts[2] = first_part(2, rows, *grads, weight).astype(BF16)
+
+    @pl.when(step == pairs + 1)
+    def _():
         sender.arrived(("first", 1))
         parts[2] = parts[2] + got_parts[1]
         sender.send("far")
-        now += 1.2
-        catch_up(now)
-        for n in (late[1], late[2], late[0]):
-            part = chunks[n][1]
-            low = firsts[0:rows, :] if part == 0 else firsts[...]
-            keep, send = own_half(joint_columns(low, grads[part]), place.band)
-            shape = (2, 2, 2, 2, width // CROPS // 2, columns)
-            keep, send = keep.reshape(shape), send.reshape(shape)
-            for h in halves_of(n):
-                picked = send if h is None else send[:, :, :, h]
-                kept = keep if h is None else keep[:, :, :, h]
-                if h is None:
-                    joint_sent[n - late[0]] = picked
-                    own[n] = kept
-                else:
-                    joint_sent[n - late[0], h] = picked
-                    own[n, h] = kept
-            sender.send((n, 0))
-            now += 2.5
-            catch_up(now)
+
+    for part in range(2):
+
+        @pl.when(step == pairs + 2 * part + 2)
+        def _():
+            joint_chunk(part)
+
+    @pl.when(step < last)
+    def _():
+        far_half = step < pairs
+        pair = jnp.where(far_half, step, jnp.minimum(step - pairs, pairs - 1))
+        first_row = pl.multiple_of(jnp.where(far_half, half_rows, 0), half_rows)
+        span = pl.ds(first_row, half_rows)
+        outs = (key_grad.at[pair, span], value_grad.at[pair, span])
+        inputs = (weights, queries, keys, values, attended, totals, attended_grad)
+        part = attend_back_pair(*inputs, outs, between)
+
+        @pl.when(far_half)
+        def _():
+            query_sum[pair] = part
+
+        @pl.when(step >= pairs)
+        def _():
+            query_grad[pair] = (query_sum[pair] + part).astype(BF16)
+
+    @pl.when(step == last)
+    def _():
+        joint_chunk(2)
+        exchanges(after)
+        parts[0] = first_part(1, rows, *grads, weight).astype(BF16)
+        sender.send(("first", 0))
+        exchanges(after + 1)
         first_grad = first_part(0, rows, *grads, weight)
+        exchanges(after + 2)
         biases = bias_sums(info, slots, rows, query_grad, value_grad)
-        for n in (late[1], late[2], late[0]):
-            late_stage(n, 0)
-        now += 2.5
-        catch_up(now)
-        start = now
-        for n in late:
-            for stage in range(1, sums.steps(n)):
-                lag = start + 6.0 + 3.0 * stage + (3.0 if n == late[2] else 0.0)
-                waiting.append((lag, stage, n))
-        waiting.sort()
-
-        def finish_until(time):
-            while waiting and waiting[0][0] <= time:
-                _, stage, n = waiting.pop(0)
-                (late_stage if n in late else early_stage)(n, stage)
-
-        finish_until(start + FIRST_LAG)
         sender.arrived(("first", 0))
         sender.arrived("far")
         first_grad = first_grad + got_parts[0].astype(F32) + got_far[...].astype(F32)
+        exchanges(after + 3)
         patches, special_grad, rows_of = first_back(
             slots, info, first_grad, tokens, middle_grad, mask, gain
         )
@@ -1055,11 +1218,12 @@
         packed = jnp.concatenate([vectors[0:5]] + rows_of + [biases[0:2], down_bias[...]], axis=0)
         pack_vectors(vector_sums.own, packed, up_bias, width // CROPS)
         vector_sums.spread()
-        finish_until(start + FIRST_LAG + 8.0)
-        vector_sums.share()
-        finish_until(start + FIRST_LAG + 12.0)
-        vector_sums.close()
-        finish_until(1e9)
+        for slot in range(after + 4, max(entry[0] for entry in PLAN) + 1):
+            exchanges(slot)
+            if slot == after + 7:
+                vector_sums.share()
+            if slot == after + 15:
+                vector_sums.close()
         for name in NEIGHBOURS:
             sender.arrived(("special", name))
         specials_out[...] = specials[...]
@@ -1067,9 +1231,6 @@
         copy = pltpu.make_async_copy(total, total_out, whole_sems.at[4])
         copy.start()
         copy.wait()
-
-
-FIRST_LAG = 8.0
 
 
 def finish_kernel(
@@ -1098,6 +1259,12 @@
                 else:
                     column += 2 * columns * part
                 value = total[n, core, x].astype(F32)
+                if name == "joint":
+                    for third in range(3):
+                        column = third * 2 * columns + (2 * part + core) * PAIR
+                        piece_of = value[:, third * PAIR : (third + 1) * PAIR]
+                        joint[row : row + rows, column : column + PAIR] = piece_of
+                    continue
                 refs[name][row : row + rows, column : column + columns] = value
     part = vectors[0].shape[0]
     for i, vector in enumerate(vectors):
@@ -1124,22 +1291,25 @@
     unit = (2, 2, 2, 2, unit_rows, columns)
     hidden_parts = hidden_width // width
     shaped = jax.ShapeDtypeStruct
-    last = pairs - 1
-    own_pair = pl.BlockSpec((rows, PAIR), lambda i: (0, jnp.minimum(i, last)))
-    all_pair = pl.BlockSpec((every, PAIR), lambda i: (0, jnp.minimum(i, last)))
-    kept = pl.BlockSpec((1, 2 * rows, every), lambda i: (jnp.minimum(i, last), 0, 0))
+    last = 2 * pairs - 1
+    far_first = lambda i: 1 - jnp.minimum(i, last) // pairs
+    pair_of = lambda i: jnp.minimum(i, last) % pairs
+    own_pair = pl.BlockSpec((rows, PAIR), lambda i: (0, pair_of(i)))
+    own_heads = pl.BlockSpec((1, rows, PAIR), lambda i: (pair_of(i), 0, 0))
+    half_heads = pl.BlockSpec((1, 2 * rows, PAIR), lambda i: (pair_of(i), far_first(i), 0))
+    kept = pl.BlockSpec((1, 2 * rows, 2 * rows), lambda i: (pair_of(i), 0, far_first(i)))
     up_shape = (2, 2, 2, 2, unit_rows, hidden_parts * columns)
     down_shape = (2, 2, 2, hidden_parts, 2, unit_rows, columns)
     grad_patches, total, vector_total, specials = pl.pallas_call(
         partial(backward_kernel, chunks, slots, pairs),
-        grid=(pairs + 1,),
+        grid=(2 * pairs + 1,),
         out_shape=[
             shaped((slots, width), BF16),
             shaped((count, 2, 2, unit_rows, columns), BF16),
             shaped((16, 128), F32),
             shaped((BANDS, 8, width), F32),
         ],
-        in_specs=[SMEM, kept, own_pair, all_pair, all_pair, own_pair, own_pair, own_pair]
+        in_specs=[SMEM, kept, own_heads, half_heads, half_heads, own_pair, own_pair, own_pair]
         + [VMEM] * 6
         + [ANY] * 10,
         out_specs=[VMEM, ANY, VMEM, VMEM],
@@ -1151,10 +1321,11 @@
             pltpu.VMEM((3,) + unit, BF16),
             pltpu.VMEM((3,) + unit, BF16),
             pltpu.VMEM((2,) + unit, BF16),
+            pltpu.VMEM((pairs, rows, PAIR), F32),
             pltpu.VMEM((pairs, rows, PAIR), BF16),
             pltpu.VMEM((pairs, every, PAIR), BF16),
             pltpu.VMEM((pairs, every, PAIR), BF16),
-            pltpu.VMEM((every, width), BF16),
+            pltpu.VMEM((width, every), BF16),
             pltpu.VMEM((width, 3 * width), BF16),
             pltpu.VMEM((rows, width), F32),
             pltpu.VMEM((rows, width), F32),
@@ -1192,7 +1363,7 @@
         g["down_got"].reshape(down_shape),
         g["out_keep"].reshape(unit),
         g["out_send"].reshape(unit),
-        g["firsts"],
+        g["firsts_t"],
         g["joint_weight"],
         g["tokens"],
         g["middle_grad"],
@@ -1217,6 +1388,116 @@
     )(total, vector_total, specials)
     up, down, out, joint, up_bias, out_specials, grad_specials = results[:7]
     return grad_patches, up, down, out, joint, results[7:], up_bias, out_specials, grad_specials
+
+
+def forward_fused(
+    info, mask, patches, specials, token, gain, shift, weight, query_bias, value_bias, rows
+):
+    slots, width = patches.shape
+    every, pairs = BANDS * rows, width // PAIR
+    shaped = jax.ShapeDtypeStruct
+    half_of = lambda i: i // pairs
+    pair_of = lambda i: i % pairs
+    final_pair = pl.BlockSpec((rows, PAIR), lambda i: (0, jnp.maximum(i - pairs, 0)))
+    outs = pl.pallas_call(
+        partial(forward_kernel, slots, pairs),
+        grid=(2 * pairs,),
+        out_shape=[
+            shaped((rows, width), F32),
+            shaped((pairs, rows, PAIR), BF16),
+            shaped((pairs, every, PAIR), BF16),
+            shaped((pairs, every, PAIR), BF16),
+            shaped((rows, width), F32),
+            shaped((rows, width), F32),
+            shaped((pairs, 2 * rows, every), BF16),
+            shaped((width, every), BF16),
+        ],
+        in_specs=[SMEM] + [VMEM] * 8 + [ANY],
+        out_specs=[
+            ANY,
+            ANY,
+            ANY,
+            ANY,
+            final_pair,
+            final_pair,
+            pl.BlockSpec((1, 2 * rows, 2 * rows), lambda i: (pair_of(i), 0, half_of(i))),
+            pl.BlockSpec((PAIR, 2 * rows), lambda i: (pair_of(i), half_of(i))),
+        ],
+        scratch_shapes=[
+            pltpu.VMEM((rows, width), F32),
+            pltpu.VMEM((BANDS, rows, width), BF16),
+            pltpu.VMEM((pairs, rows, PAIR), BF16),
+            pltpu.VMEM((pairs, every, PAIR), BF16),
+            pltpu.VMEM((pairs, every, PAIR), BF16),
+            pltpu.VMEM((every, PAIR), BF16),
+            pltpu.VMEM((pairs, rows, PAIR), F32),
+            pltpu.VMEM((pairs, rows, PAIR), F32),
+            pltpu.VMEM((width, 3 * width), BF16),
+            pltpu.SemaphoreType.DMA((3,)),
+            pltpu.SemaphoreType.DMA((3,)),
+            pltpu.SemaphoreType.DMA((5,)),
+        ],
+        compiler_params=pltpu.CompilerParams(
+            vmem_limit_bytes=VMEM_LIMIT, collective_id=1, has_side_effects=True
+        ),
+        name="forward",
+    )(info, mask, patches, specials, token, gain, shift, query_bias, value_bias, weight)
+    return outs
+
+
+def forward_general(
+    info, mask, patches, specials, token, gain, shift, weight, query_bias, value_bias, rows
+):
+    slots, width = patches.shape
+    every, pairs = BANDS * rows, width // PAIR
+    shaped = jax.ShapeDtypeStruct
+    tokens, first = pl.pallas_call(
+        partial(first_kernel, slots),
+        out_shape=[shaped((rows, width), F32), shaped((rows, width), BF16)],
+        in_specs=[SMEM] + [VMEM] * 6,
+        compiler_params=params(),
+        name="first",
+    )(info, mask, patches, specials, token, gain, shift)
+    firsts = gather_blocks(first)
+    block = pl.BlockSpec((rows, width), lambda i: (i, 0))
+    pair_block = pl.BlockSpec((pairs, rows, PAIR), lambda i: (0, i, 0))
+    queries, keys, values = pl.pallas_call(
+        partial(project_kernel, slots),
+        grid=(BANDS,),
+        out_shape=[
+            shaped((pairs, rows, PAIR), BF16),
+            shaped((pairs, every, PAIR), BF16),
+            shaped((pairs, every, PAIR), BF16),
+        ],
+        in_specs=[SMEM, block, whole((width, 3 * width)), VMEM, VMEM],
+        out_specs=[whole((pairs, rows, PAIR)), pair_block, pair_block],
+        compiler_params=params(),
+        name="project",
+    )(info, firsts, weight, query_bias, value_bias)
+    own_pair = pl.BlockSpec((rows, PAIR), lambda i: (0, i))
+    all_pair = pl.BlockSpec((every, PAIR), lambda i: (0, i))
+    own_heads = pl.BlockSpec((1, rows, PAIR), lambda i: (i, 0, 0))
+    all_heads = pl.BlockSpec((1, every, PAIR), lambda i: (i, 0, 0))
+    attended, totals, weights, firsts_t = pl.pallas_call(
+        partial(attend_kernel, slots),
+        grid=(pairs,),
+        out_shape=[
+            shaped((rows, width), F32),
+            shaped((rows, width), F32),
+            shaped((pairs, 2 * rows, every), BF16),
+            shaped((width, every), BF16),
+        ],
+        in_specs=[SMEM, own_heads, all_heads, all_heads, all_pair],
+        out_specs=[
+            own_pair,
+            own_pair,
+            pl.BlockSpec((1, 2 * rows, every), lambda i: (i, 0, 0)),
+            pl.BlockSpec((PAIR, every), lambda i: (i, 0)),
+        ],
+        compiler_params=params(),
+        name="attend",
+    )(info, queries, keys, values, firsts)
+    return tokens, queries, keys, values, attended, totals, weights, firsts_t
 
 
 def body(
@@ -1249,8 +1530,6 @@
     owned = -(-special_count // BANDS)
     rows = round_up(slots + owned, 16)
     pad = rows - slots
-    every = BANDS * rows
-    pairs = width // PAIR
     band = lax.axis_index("band")
     relatives = [band ^ r for r in range(BANDS)]
     info = jnp.stack(
@@ -1263,47 +1542,20 @@
     cot_patches, cot_specials = cot_patches[0], cot_specials[0]
     shaped = jax.ShapeDtypeStruct
 
-    tokens, first = pl.pallas_call(
-        partial(first_kernel, slots),
-        out_shape=[shaped((rows, width), F32), shaped((rows, width), BF16)],
-        in_specs=[SMEM] + [VMEM] * 6,
-        compiler_params=params(),
-        name="first",
-    )(info, mask, patches, specials, mask_token, first_gain, first_shift)
-
-    firsts = gather_blocks(first)
-
-    block = pl.BlockSpec((rows, width), lambda i: (i, 0))
-    queries, keys, values = pl.pallas_call(
-        partial(project_kernel, slots),
-        grid=(BANDS,),
-        out_shape=[
-            shaped((rows, width), BF16),
-            shaped((every, width), BF16),
-            shaped((every, width), BF16),
-        ],
-        in_specs=[SMEM, block, whole((width, 3 * width)), VMEM, VMEM],
-        out_specs=[whole((rows, width)), block, block],
-        compiler_params=params(),
-        name="project",
-    )(info, firsts, joint_weight, query_bias, value_bias)
-
-    own_pair = pl.BlockSpec((rows, PAIR), lambda i: (0, i))
-    all_pair = pl.BlockSpec((every, PAIR), lambda i: (0, i))
-    kept = pl.BlockSpec((1, 2 * rows, every), lambda i: (i, 0, 0))
-    attended, totals, weights = pl.pallas_call(
-        partial(attend_kernel, slots),
-        grid=(pairs,),
-        out_shape=[
-            shaped((rows, width), F32),
-            shaped((rows, width), F32),
-            shaped((pairs, 2 * rows, every), BF16),
-        ],
-        in_specs=[SMEM, own_pair, all_pair, all_pair],
-        out_specs=[own_pair, own_pair, kept],
-        compiler_params=params(),
-        name="attend",
-    )(info, queries, keys, values)
+    forward = forward_fused if lax.axis_size("crop") == CROPS else forward_general
+    tokens, queries, keys, values, attended, totals, weights, firsts_t = forward(
+        info,
+        mask,
+        patches,
+        specials,
+        mask_token,
+        first_gain,
+        first_shift,
+        joint_weight,
+        query_bias,
+        value_bias,
+        rows,
+    )
 
     branch, middle, second, incoming, down_in, down_keep, down_send, down_bias_grad = pl.pallas_call(
         partial(middle_kernel, slots),
@@ -1433,7 +1685,7 @@
         down_got=down_got,
         out_keep=out_keep,
         out_send=out_send,
-        firsts=firsts,
+        firsts_t=firsts_t,
         joint_weight=joint_weight,
         tokens=tokens,
         middle_grad=middle_grad,

time: 211 us -> 172 us (0.82)
  Pallas kernels: 180 us -> 163 us
  waiting for transfers between devices: 14.9 us -> 0.01 us
  starting transfers between devices: 4.8 us -> 0.57 us
  local copies, waits for them, and re-layouts: 7.1 us -> 4.26 us
    pallas_call x4 -> x2, Pallas kernels: 143 us -> 126 us  [the longest x1 92.2 us: backward_fused(): pl.pallas_call(partial(backward_kernel, chunks, slots, pairs), grid=(2 *...]
    ppermute x5 -> x2, waiting for transfers between devices: 14.9 us -> 0.01 us  [swap(): return lax.ppermute(x, axis, [(i, i ^ distance) for i in range(size)])]
    ppermute x5 -> x2, starting transfers between devices: 4.8 us -> 0.57 us  [swap(): return lax.ppermute(x, axis, [(i, i ^ distance) for i in range(size)])]
    unnamed x10 -> x5, local copies, waits for them, and re-layouts: 5.04 us -> 2.24 us
  transfers between devices with their start and end apart: 5 -> 2, of which waited for: 2 -> 0; matrix products, arithmetic and copies ran while one was open for 1% -> 0% of each run, Pallas kernels for 4% -> 5%
where the time goes in v2:
time: 172 us
  Pallas kernels  163 us (95%)
  local copies, waits for them, and re-layouts  4.26 us (2%)
  between operations  3.42 us (2%)
    pallas_call x1, Pallas kernels, backward_fused(): pl.pallas_call(partial(backward_kernel, chunks, slots, pairs), grid=(2 *...  92.2 us
    pallas_call x1, Pallas kernels, forward_fused(): pl.pallas_call(partial(forward_kernel, slots, pairs), grid=(2 * pairs,),...  33.7 us
    pallas_call x1, Pallas kernels, body(): pl.pallas_call(mlp_kernel, grid=(steps,), out_shape=[shaped((rows, width)...  20.3 us
    pallas_call x1, Pallas kernels, body(): pl.pallas_call(partial(middle_back_kernel, slots), out_shape=[shaped((slo...  7.93 us
    pallas_call x1, Pallas kernels, body(): pl.pallas_call(partial(middle_kernel, slots), out_shape=[shaped((rows, wi...  5.79 us
    pallas_call x1, Pallas kernels, backward_fused(): pl.pallas_call(partial(finish_kernel, chunks, special_count), out_shape=[...  3.49 us
  transfers between devices with their start and end apart: 2, of which 0 were waited for; matrix products, arithmetic and copies ran while one was open for 0% of the time, Pallas kernels for 5%

profile of v2, /device:TPU:1, one launch (start us, length us, event | category | flops | bytes accessed | tf_op | source)
XLA Modules:
  0.0 171.7 jit_solution(4035994096897852671)
XLA Ops:
  0.7 1.4 fusion
  4.8 0.6 stack.27.info
  5.4 33.7 %forward.1 = (f32[448,768]{1,0:T(8,128)}, bf16[6,448,128]{2,1,0:T(8,128)(2,1)}, bf16[6,1792,128]{2,1,0:T(8,128)(2,1)}, bf16[6,1792,128]{2,1,0:T(8,128)(2,1)}, f3...) custom-call(s32[9]{0:T(128)} %stack.27.info, ...), custom_call_target="tpu_custom_call" | custom-call | tf_op jit(solution)/shard_map/forward/pallas_call | solution.py:1402
  39.1 5.8 %middle.1 = (f32[448,768]{1,0:T(8,128)}, f32[448,768]{1,0:T(8,128)}, bf16[448,768]{1,0:T(8,128)(2,1)}, f32[448,768]{1,0:T(8,128)}, bf16[448,768]{1,0:T(8,128)(2,...) custom-call(s32[9]{0:T(128)} %stack.27.info, f32[448,768]{1,0:T(8,128)} %get-tuple-element.72.attended, ...), custom_call_target="tpu_custom_call" | custom-call | tf_op jit(solution)/shard_map/middle/pallas_call | solution.py:1560
  44.9 20.3 %mlp.1 = (f32[448,768]{1,0:T(8,128)}, f32[448,768]{1,0:T(8,128)}, bf16[768,1536]{1,0:T(8,128)(2,1)}, bf16[768,1536]{1,0:T(8,128)(2,1)}, f32[1,3072]{1,0:T(1,128)...) custom-call(s32[9]{0:T(128)} %stack.27.info, bf16[448,768]{1,0:T(8,128)(2,1)} %get-tuple-element.76.second, ...), custom_call_target="tpu_custom_call" | custom-call | tf_op jit(solution)/shard_map/mlp/pallas_call | solution.py:1600
  65.2 0.1 collective-permute-start
  65.3 0.5 collective-permute-start.1
  65.8 7.9 %middle_back.1 = (bf16[444,768]{1,0:T(8,128)(2,1)}, f32[4,768]{1,0:T(4,128)}, f32[448,768]{1,0:T(8,128)}, f32[448,768]{1,0:T(8,128)}, bf16[768,384]{1,0:T(8,128)...) custom-call(s32[9]{0:T(128)} %stack.27.info, f32[448,768]{1,0:T(8,128)} %get-tuple-element.74.middle, ...), custom_call_target="tpu_custom_call" | custom-call | tf_op jit(solution)/shard_map/middle_back/pallas_call | solution.py:1637
  73.7 0.0 collective-permute-done
  73.7 0.0 copy-start
  73.7 0.0 collective-permute-done.1
  73.7 1.4 copy-done
  75.1 92.2 %backward.1 = (bf16[444,768]{1,0:T(8,128)(2,1)}, bf16[12,2,2,48,384]{4,3,2,1,0:T(8,128)(2,1)}, f32[16,128]{1,0:T(8,128)}, f32[4,8,768]{2,1,0:T(8,128)}) custom-call(s32[9]{0:T(128)} %stack.27.info, bf16[6,896,1792]{2,1,0:T(8,128)(2,1)} %get-tuple-element.84.weights, bf16[6,448,128]{2,1,0:T(8,128)(2,1)} %get-tuple-element.85.queries, ...), custom_call_target="tpu_custom_call" | custom-call | tf_op jit(solution)/shard_map/backward/pallas_call | solution.py:1303
  167.3 0.0 copy-start.1
  167.3 3.5 %finish.1 = (f32[96,3072]{1,0:T(8,128)}, f32[384,768]{1,0:T(8,128)}, f32[96,768]{1,0:T(8,128)}, f32[96,2304]{1,0:T(8,128)}, f32[384]{0:T(512)}, /*index=5*/bf16[...) custom-call(bf16[12,2,2,48,384]{4,3,2,1,0:T(8,128)(2,1)} %get-tuple-, ...), custom_call_target="tpu_custom_call" | custom-call | tf_op jit(solution)/shard_map/finish/pallas_call | solution.py:1372
  170.8 0.0 copy-done.1
  170.8 0.8 copy.43
Async XLA Ops:
  65.2 8.5 %collective-permute-start = (bf16[768,1536]{1,0:T(8,128)(2,1)}, bf16[768,1536]{1,0:T(8,128)(2,1)S(1)}, u32[]{:S(2)}, u32[]{:S(2)}) collective-permute-start(bf16[768,1536]{1,0:T(8,128)(2,1)} %get-tuple-element.95), channel_id=1, source_target_pairs={{0,8},{8,0},{16,24},{24,16},{1,9},{9,1},{17,25},{25,17},{2,10},{10... | collective-permute-start | bytes 7077896 | tf_op jit(solution)/shard_map/ppermute | solution.py:528
  65.3 8.4 %collective-permute-start.1 = (bf16[3072,384]{1,0:T(8,128)(2,1)}, bf16[3072,384]{1,0:T(8,128)(2,1)}, u32[]{:S(2)}, u32[]{:S(2)}) collective-permute-start(bf16[3072,384]{1,0:T(8,128)(2,1)} %get-tuple-element.97), channel_id=1, source_target_pairs={{0,8},{8,0},{16,24},{24,16},{1,9},{9,1},{17,25},{25,17},{2,10},{10... | collective-permute-start | bytes 7077896 | tf_op jit(solution)/shard_map/ppermute | solution.py:528
  73.7 1.4 copy-start
  167.3 3.5 %copy-start.1 = (bf16[444,768]{1,0:T(8,128)(2,1)S(1)}, bf16[444,768]{1,0:T(8,128)(2,1)}, u32[]{:S(2)}) copy-start(bf16[444,768]{1,0:T(8,128)(2,1)} %get-tuple-element.106) | copy-start | bytes 2045956

commit v3 on v2

--- a/solution.py
+++ b/solution.py
@@ -398,8 +398,8 @@
     out_keep,
     out_send,
     vectors,
+    between=lambda part: None,
 ):
-    rows = middle.shape[0]
     mid = middle[...]
     given = incoming[...]
     two = branch_two[...] + line(down_bias)
@@ -411,12 +411,15 @@
     grad = second_grad[...]
     back = given + normalize_back(grad * line(gain), hat, scale)
     middle_grad[...] = back
+    between(0)
     out_in = (back * line(first_scale)).astype(BF16)
     attended_grad[...] = dot_nt(out_in, weight[...])
+    between(1)
     keep, send = own_half(out_in, info[2 * BANDS])
     low = attended[...].astype(BF16)
     out_keep[...] = dot_tn(low, keep).astype(BF16)
     out_send[...] = dot_tn(low, send).astype(BF16)
+    between(2)
     vectors[...] = jnp.concatenate(
         [
             column_sum(given * two),
@@ -715,8 +718,8 @@
         special_count,
     )
     matrices = (
-        reduce_half(g["up_keep"], g["up_got"], half),
-        reduce_half(g["down_keep"], g["down_got"], half),
+        reduce_half(g["mlp_grads"]["up_keep"], g["mlp_grads"]["up_got"], half),
+        reduce_half(g["mlp_grads"]["down_keep"], g["mlp_grads"]["down_got"], half),
         reduce_half(g["out_keep"], swap(g["out_send"], "band", 1), half),
         joint_order(reduce_half(joint_keep, swap(joint_send, "band", 1), half)),
     )
@@ -725,7 +728,8 @@
 
 MESH = pl.DeviceIdType.MESH
 CROPS = 8
-X_FIRST = (0, 1, 3, 4, 9, 10)
+X_FIRST = (1, 3, 5, 7, 8, 9)
+DIRECT = (9, 10, 11)
 NEIGHBOURS = ("core", "x", "diagonal")
 PLACES = NEIGHBOURS + tuple(range(1, CROPS))
 
@@ -760,6 +764,7 @@
     def __init__(self, place, send_sems, recv_sems):
         self.place, self.send_sems, self.recv_sems = place, send_sems, recv_sems
         self.routes = {}
+        self.sent = []
 
     def add(self, key, source, target, name):
         self.routes[key] = (len(self.routes), source, target, name)
@@ -777,12 +782,17 @@
 
     def send(self, key):
         self.copy(key).start()
+        self.sent.append(key)
 
     def arrived(self, key):
         self.copy(key).wait_recv()
 
+    def left(self, key):
+        self.copy(key).wait_send()
+        self.sent.remove(key)
+
     def finish(self):
-        for key in self.routes:
+        for key in self.sent:
             self.copy(key).wait_send()
 
 
@@ -800,85 +810,87 @@
         pltpu.VMEM((count, 2, 2, 2) + unit, BF16),
         pltpu.VMEM((count, 2, 2) + unit, BF16),
         pltpu.VMEM((count, 2) + unit, BF16),
-        pltpu.VMEM((count, 2) + unit, BF16),
+        pltpu.VMEM((count, 3, 2) + unit, BF16),
     ]
 
 
 class ChunkSums:
     def __init__(self, place, sender, buffers, total, count):
-        p, self.sender = place, sender
+        p, self.sender, self.place, self.total = place, sender, place, total
         own, got_a, got_b, got_c, got_d = buffers
+        self.got_d = got_d
         self.table = {}
         for n in range(count):
+            both, half = total.at[n, p.core], total.at[n, p.core, p.x]
             if x_first(n):
-                half = total.at[n, p.core, p.x]
-                rows = [
-                    (None, None, own.at[n, 1 - p.x], got_a.at[n], "x"),
-                    (own.at[n, p.x], got_a.at[n], own.at[n, p.x, :, :, 1 - p.y], got_b.at[n], "y"),
-                    (
-                        own.at[n, p.x, :, :, p.y],
-                        got_b.at[n],
-                        own.at[n, p.x, :, 1 - p.near, p.y],
-                        got_c.at[n],
-                        "near",
-                    ),
-                    (
-                        own.at[n, p.x, :, p.near, p.y],
-                        got_c.at[n],
-                        own.at[n, p.x, 1 - p.far, p.near, p.y],
-                        got_d.at[n, 0],
-                        "far",
-                    ),
-                    (own.at[n, p.x, p.far, p.near, p.y], got_d.at[n, 0], half, half, "x"),
-                    (None, None, total.at[n, p.core], total.at[n, p.core], "core"),
+                kept = [
+                    own.at[n, p.x],
+                    own.at[n, p.x, :, :, p.y],
+                    own.at[n, p.x, :, p.near, p.y],
+                    own.at[n, p.x, p.far, p.near, p.y],
                 ]
-                last = half
+                got = [got_a.at[n], got_b.at[n], got_c.at[n], got_d.at[n, 0, 0]]
+                sent = [
+                    own.at[n, 1 - p.x],
+                    own.at[n, p.x, :, :, 1 - p.y],
+                    own.at[n, p.x, :, 1 - p.near, p.y],
+                    own.at[n, p.x, 1 - p.far, p.near, p.y],
+                ]
+                names = ("x", "y", "near", "far")
             else:
-                half = total.at[n, p.core]
-                rows = [
-                    (None, None, own.at[n, :, :, 1 - p.y], got_a.at[n], "y"),
-                    (
-                        own.at[n, :, :, p.y],
-                        got_a.at[n],
-                        own.at[n, :, 1 - p.near, p.y],
-                        got_b.at[n],
-                        "near",
-                    ),
-                    (
-                        own.at[n, :, p.near, p.y],
-                        got_b.at[n],
-                        own.at[n, 1 - p.far, p.near, p.y],
-                        got_c.at[n],
-                        "far",
-                    ),
-                    (
-                        own.at[n, p.far, p.near, p.y],
-                        got_c.at[n],
-                        own.at[n, p.far, p.near, p.y],
-                        got_d.at[n],
-                        "x",
-                    ),
-                    (own.at[n, p.far, p.near, p.y], got_d.at[n], half, half, "core"),
+                kept = [
+                    own.at[n, :, :, p.y],
+                    own.at[n, :, p.near, p.y],
+                    own.at[n, p.far, p.near, p.y],
                 ]
-                last = half
+                got = [got_a.at[n], got_b.at[n], got_c.at[n]]
+                sent = [
+                    own.at[n, :, :, 1 - p.y],
+                    own.at[n, :, 1 - p.near, p.y],
+                    own.at[n, 1 - p.far, p.near, p.y],
+                ]
+                names = ("y", "near", "far")
+            rows = [(None, None, None, [(sent[0], got[0], names[0])])]
+            for i in range(1, len(names)):
+                add = (kept[i - 1], kept[i - 1], got[i - 1])
+                rows.append(add + ([(sent[i], got[i], names[i])],))
+            end = (kept[-1], got[-1])
+            if direct(n):
+                targets = [half] * 3 if x_first(n) else [got_d.at[n, i] for i in range(3)]
+                last = half if x_first(n) else both
+                rows.append((last,) + end + ([(last, t, m) for t, m in zip(targets, NEIGHBOURS)],))
+            elif x_first(n):
+                rows.append((half,) + end + ([(half, half, "x")],))
+                rows.append((None, None, None, [(both, both, "core")]))
+            else:
+                rows.append((kept[-1],) + end + ([(kept[-1], got_d.at[n, 0], "x")],))
+                rows.append((both, kept[-1], got_d.at[n, 0], [(both, both, "core")]))
             self.table[n] = rows
-            for stage, (_, _, source, target, name) in enumerate(rows):
-                sender.add((n, stage + 1), source, target, name)
-            self.table[n, "last"] = last
+            for stage, row in enumerate(rows):
+                for i, (source, target, name) in enumerate(row[3]):
+                    sender.add((n, stage + 1, i), source, target, name)
 
     def steps(self, n):
         return len(self.table[n]) + 1
 
     def step(self, n, stage):
+        rows, sender = self.table[n], self.sender
         if stage > 0:
-            self.sender.arrived((n, stage))
-        if stage == len(self.table[n]):
+            for i in range(len(rows[stage - 1][3])):
+                sender.arrived((n, stage, i))
+        if stage == len(rows):
+            if direct(n) and not x_first(n):
+                for i in range(3):
+                    sender.left((n, stage, i))
+                p, total, got = self.place, self.total, self.got_d
+                total[n, p.core] = total[n, p.core] + got[n, 1]
+                total[n, 1 - p.core] = got[n, 0] + got[n, 2]
             return
-        into, got, source, target, _ = self.table[n][stage]
+        into, kept, got, sent = rows[stage]
         if into is not None:
-            place = self.table[n, "last"] if source is target else into
-            place[...] = into[...] + got[...]
-        self.sender.send((n, stage + 1))
+            into[...] = kept[...] + got[...]
+        for i in range(len(sent)):
+            sender.send((n, stage + 1, i))
 
 
 class VectorSums:
@@ -931,6 +943,10 @@
     return n in X_FIRST
 
 
+def direct(n):
+    return n in DIRECT
+
+
 def halves_of(n):
     return (0, 1) if x_first(n) else (None,)
 
@@ -946,20 +962,260 @@
     return ref if x_half is None else ref.at[x_half]
 
 
+def middle_all_kernel(
+    chunks,
+    slots,
+    parts,
+    info,
+    attended,
+    tokens,
+    out_weight,
+    out_bias,
+    first_scale,
+    gain,
+    shift,
+    second_scale,
+    cot_patches,
+    cot_specials,
+    down_bias,
+    up,
+    up_bias,
+    down,
+    out_patches,
+    out_specials,
+    middle_grad,
+    attended_grad,
+    out_keep,
+    out_send,
+    vectors,
+    down_bias_grad,
+    up_bias_grad,
+    kept_out,
+    sent_out,
+    *scratch,
+):
+    (
+        kept,
+        sent,
+        branch,
+        middle,
+        second,
+        second_t,
+        incoming,
+        down_in,
+        down_keep,
+        down_send,
+        branch_two,
+        second_grad,
+        active_t,
+        store_sems,
+    ) = scratch
+    step = pl.program_id(0)
+    width = tokens.shape[1]
+    count = kept.shape[0]
+    band = lax.axis_index("band")
+
+    def stores(n):
+        return [
+            pltpu.make_async_copy(kept.at[n], kept_out.at[n], store_sems.at[0, n]),
+            pltpu.make_async_copy(sent.at[n], sent_out.at[n], store_sems.at[1, n]),
+        ]
+
+    def made(n, value, x_halves):
+        shape = (2, 2, 2, 2, width // CROPS // 2, width // 2)
+        for half, target in zip(own_half(value, band), (kept.at[n], sent.at[n])):
+            half = half.reshape(shape)
+            if x_halves:
+                for h in range(2):
+                    target[h] = half[:, :, :, h]
+            else:
+                target[...] = half
+        for copy in stores(n):
+            copy.start()
+
+    @pl.when(step == 0)
+    def _():
+        middle_kernel(
+            slots,
+            info,
+            attended,
+            tokens,
+            out_weight,
+            out_bias,
+            first_scale,
+            gain,
+            shift,
+            second_scale,
+            cot_patches,
+            cot_specials,
+            branch,
+            middle,
+            second,
+            incoming,
+            down_in,
+            down_keep,
+            down_send,
+            down_bias_grad,
+        )
+        second_t[...] = second[...].astype(F32).T.astype(BF16)
+        branch_two[...] = jnp.zeros_like(branch_two)
+        second_grad[...] = jnp.zeros_like(second_grad)
+
+    @pl.when(step < parts)
+    def _():
+        hidden = dot(second[...], up[...]) + up_bias[...]
+        active, slope = gelu_and_slope(hidden)
+        active = active.astype(BF16)
+        span = pl.ds(pl.multiple_of(step * width, width), width)
+        active_t[span, :] = active.astype(F32).T.astype(BF16)
+        hidden_in = (slope * dot_nt(down_in[...], down[...])).astype(BF16)
+        made(2 * step + 1, dot(second_t[...], hidden_in).astype(BF16), True)
+        branch_two[...] += dot(active, down[...])
+        second_grad[...] += dot_nt(hidden_in, up[...])
+        up_bias_grad[...] = column_sum(hidden_in.astype(F32))
+
+    @pl.when((step >= parts) & (step < 2 * parts))
+    def _():
+        part = step - parts
+        own_rows = width // CROPS
+        starts = [
+            pl.multiple_of((crop * parts + part) * own_rows, own_rows) for crop in range(CROPS)
+        ]
+        rows = jnp.concatenate([active_t[pl.ds(i, own_rows), :] for i in starts], axis=0)
+        made(2 * part, dot(rows, down_in[...]).astype(BF16), False)
+
+    @pl.when(step == 2 * parts)
+    def _():
+        middle_back_kernel(
+            slots,
+            info,
+            middle,
+            branch,
+            branch_two,
+            second_grad,
+            incoming,
+            attended,
+            out_weight,
+            down_bias,
+            second_scale,
+            gain,
+            first_scale,
+            out_patches,
+            out_specials,
+            middle_grad,
+            attended_grad,
+            out_keep,
+            out_send,
+            vectors,
+        )
+        for n in range(count):
+            for copy in stores(n):
+                copy.wait()
+
+
+def middle_fused(
+    info,
+    attended,
+    tokens,
+    out_weight,
+    out_bias,
+    first_scale,
+    second_gain,
+    second_shift,
+    second_scale,
+    cot_patches,
+    cot_specials,
+    down_bias,
+    up_weight,
+    up_bias,
+    down_weight,
+):
+    rows, width = tokens.shape
+    slots = cot_patches.shape[0]
+    hidden_width = up_weight.shape[1]
+    parts = hidden_width // width
+    chunks = chunk_list(parts)
+    count = 2 * parts
+    unit_rows, half = width // CROPS // 2, width // 2
+    unit = (2, 2, 2, 2, unit_rows, half)
+    shaped = jax.ShapeDtypeStruct
+    last = parts - 1
+    outs = pl.pallas_call(
+        partial(middle_all_kernel, chunks, slots, parts),
+        grid=(2 * parts + 1,),
+        out_shape=[
+            shaped((slots, width), BF16),
+            shaped((rows - slots, width), F32),
+            shaped((rows, width), F32),
+            shaped((rows, width), F32),
+            shaped((width, half), BF16),
+            shaped((width, half), BF16),
+            shaped((8, width), F32),
+            shaped((1, width), F32),
+            shaped((1, hidden_width), F32),
+            shaped((count,) + unit, BF16),
+            shaped((count,) + unit, BF16),
+        ],
+        in_specs=[SMEM]
+        + [VMEM] * 11
+        + [
+            pl.BlockSpec((width, width), lambda i: (0, jnp.minimum(i, last))),
+            pl.BlockSpec((1, width), lambda i: (0, jnp.minimum(i, last))),
+            pl.BlockSpec((width, width), lambda i: (jnp.minimum(i, last), 0)),
+        ],
+        out_specs=[VMEM] * 8 + [pl.BlockSpec((1, width), lambda i: (0, jnp.minimum(i, last))), ANY, ANY],
+        scratch_shapes=[
+            pltpu.VMEM((count,) + unit, BF16),
+            pltpu.VMEM((count,) + unit, BF16),
+            pltpu.VMEM((rows, width), F32),
+            pltpu.VMEM((rows, width), F32),
+            pltpu.VMEM((rows, width), BF16),
+            pltpu.VMEM((width, rows), BF16),
+            pltpu.VMEM((rows, width), F32),
+            pltpu.VMEM((rows, width), BF16),
+            pltpu.VMEM((rows, half), BF16),
+            pltpu.VMEM((rows, half), BF16),
+            pltpu.VMEM((rows, width), F32),
+            pltpu.VMEM((rows, width), F32),
+            pltpu.VMEM((hidden_width, rows), BF16),
+            pltpu.SemaphoreType.DMA((2, count)),
+        ],
+        compiler_params=params(),
+        name="middle_all",
+    )(
+        info,
+        attended,
+        tokens,
+        out_weight,
+        out_bias,
+        first_scale,
+        second_gain,
+        second_shift,
+        second_scale,
+        cot_patches,
+        cot_specials,
+        down_bias,
+        up_weight,
+        up_bias,
+        down_weight,
+    )
+    return tuple(outs[:9]) + (outs[9:],)
+
+
 PLAN = (
-    (0, 0, 0), (0, 1, 0), (0, 2, 0), (0, 3, 0), (0, 5, 0), (0, 6, 0),
-    (7, 4, 0), (7, 7, 0), (9, 0, 1), (9, 2, 1), (16, 2, 2), (16, 1, 1),
-    (16, 5, 1), (18, 8, 0), (19, 2, 3), (19, 3, 1), (19, 6, 1), (22, 5, 2),
-    (24, 2, 4), (24, 6, 2), (24, 4, 1), (24, 7, 1), (26, 5, 3), (26, 0, 2),
-    (26, 9, 0), (27, 2, 5), (29, 6, 3), (29, 1, 2), (30, 7, 2), (32, 0, 3),
-    (33, 1, 3), (33, 8, 1), (33, 10, 0), (36, 7, 3), (36, 3, 2), (37, 0, 4),
-    (38, 4, 2), (38, 11, 0), (39, 8, 2), (40, 1, 4), (40, 5, 4), (40, 6, 4),
-    (40, 3, 3), (40, 4, 3), (40, 9, 1), (45, 8, 3), (45, 11, 1), (47, 5, 5),
-    (48, 3, 4), (49, 6, 5), (50, 10, 1), (51, 4, 4), (52, 9, 2), (53, 7, 4),
-    (54, 0, 5), (55, 1, 5), (56, 11, 2), (57, 7, 5), (58, 10, 2), (59, 8, 4),
-    (60, 9, 3), (61, 0, 6), (62, 3, 5), (63, 1, 6), (64, 4, 5), (65, 8, 5),
-    (66, 11, 3), (67, 3, 6), (68, 4, 6), (69, 10, 3), (70, 11, 4), (71, 9, 4),
-    (72, 10, 4), (73, 9, 5), (74, 11, 5), (75, 10, 5), (76, 9, 6), (77, 10, 6),
+    (2, 1, 0), (2, 0, 0), (3, 3, 0), (4, 2, 0), (9, 5, 0), (9, 4, 0),
+    (10, 1, 1), (10, 0, 1), (14, 7, 0), (16, 0, 2), (16, 3, 1), (16, 2, 1),
+    (18, 6, 0), (18, 8, 0), (18, 0, 3), (19, 5, 1), (19, 4, 1), (19, 2, 2),
+    (22, 1, 2), (24, 4, 2), (24, 7, 1), (24, 3, 2), (24, 2, 3), (25, 1, 3),
+    (26, 9, 0), (28, 8, 1), (28, 6, 1), (28, 3, 3), (28, 4, 3), (29, 0, 4),
+    (29, 1, 4), (30, 5, 2), (30, 0, 5), (31, 6, 2), (31, 7, 2), (31, 3, 4),
+    (32, 10, 0), (33, 5, 3), (33, 8, 2), (36, 6, 3), (36, 7, 3), (36, 5, 4),
+    (37, 8, 3), (38, 11, 0), (38, 10, 1), (39, 2, 4), (39, 7, 4), (40, 8, 4),
+    (40, 2, 5), (40, 10, 2), (40, 9, 1), (44, 4, 4), (44, 11, 1), (45, 1, 5),
+    (47, 3, 5), (48, 6, 4), (49, 4, 5), (50, 5, 5), (51, 10, 3), (52, 9, 2),
+    (53, 1, 6), (54, 7, 5), (55, 3, 6), (56, 8, 5), (57, 6, 5), (58, 11, 2),
+    (59, 5, 6), (60, 7, 6), (61, 9, 3), (62, 8, 6), (63, 10, 4), (64, 11, 3),
+    (65, 9, 4), (66, 11, 4), (67, 9, 5),
 )
 
 
@@ -981,10 +1237,8 @@
     down_bias,
     up_bias,
     out_own,
-    up_keep,
-    up_got,
-    down_keep,
-    down_got,
+    kept_in,
+    sent_in,
     out_keep,
     out_send,
     firsts_in,
@@ -1000,10 +1254,10 @@
     buffers, vector_buffers = scratch[:5], scratch[5:8]
     (
         total,
+        got,
         out_got,
         joint_got,
         joint_sent,
-        loaded,
         query_sum,
         query_grad,
         key_grad,
@@ -1030,23 +1284,14 @@
     sums = ChunkSums(place, sender, buffers, total, count)
     vector_sums = VectorSums(place, sender, vector_buffers, vector_total)
     own = buffers[0]
-    keeps = dict(up=up_keep, down=down_keep, out=out_keep)
-    gots = dict(up=up_got, down=down_got)
+    passed = kept_in.shape[0]
 
     def own_loads(n):
-        name, part = chunks[n]
+        if n < passed:
+            return [pltpu.make_async_copy(kept_in.at[n], own.at[n], load_sems.at[n, 0])]
         return [
             pltpu.make_async_copy(
-                part_of(keeps[name], name, part, columns, h), piece(own.at[n], h), load_sems.at[n, 0, i]
-            )
-            for i, h in enumerate(halves_of(n))
-        ]
-
-    def got_loads(n):
-        name, part = chunks[n]
-        return [
-            pltpu.make_async_copy(
-                part_of(gots[name], name, part, columns, h), piece(loaded.at[mlp.index(n) % 2], h), load_sems.at[n, 1, i]
+                part_of(out_keep, "out", 0, columns, h), piece(own.at[n], h), load_sems.at[n, i]
             )
             for i, h in enumerate(halves_of(n))
         ]
@@ -1058,10 +1303,11 @@
         ]
 
     early = [n for n, (name, _) in enumerate(chunks) if name != "joint"]
-    mlp = [n for _, n, stage in PLAN if stage == 0 and chunks[n][0] in gots]
     out_chunk = early[-1]
     late = [n for n, (name, _) in enumerate(chunks) if name == "joint"]
 
+    for n in range(passed):
+        sender.add((n, 0), sent_in.at[n], got.at[n], "core")
     for h in halves_of(out_chunk):
         source = part_of(out_send, "out", 0, columns, h)
         sender.add((out_chunk, 0, h), source, piece(out_got, h), "core")
@@ -1077,10 +1323,10 @@
         for n in early:
             for copy in own_loads(n):
                 copy.start()
-        for n in mlp[:2]:
-            for copy in got_loads(n):
-                copy.start()
         place.greet(PLACES)
+        for _, n, stage in PLAN:
+            if stage == 0 and n < passed:
+                sender.send((n, 0))
         for h in halves_of(out_chunk):
             sender.send((out_chunk, 0, h))
 
@@ -1088,18 +1334,13 @@
         if stage == 0:
             for copy in own_loads(n):
                 copy.wait()
-            if n in mlp:
-                for copy in got_loads(n):
-                    copy.wait()
-                index = mlp.index(n)
-                own[n] = own[n] + loaded[index % 2]
-                if index + 2 < len(mlp):
-                    for copy in got_loads(mlp[index + 2]):
-                        copy.start()
-            else:
+            if n == out_chunk:
                 for h in halves_of(n):
                     sender.arrived((n, 0, h))
                 own[n] = own[n] + out_got[...]
+            else:
+                sender.arrived((n, 0))
+                own[n] = own[n] + got[n]
         sums.step(n, stage)
 
     def late_stage(n, stage):
@@ -1298,8 +1539,6 @@
     own_heads = pl.BlockSpec((1, rows, PAIR), lambda i: (pair_of(i), 0, 0))
     half_heads = pl.BlockSpec((1, 2 * rows, PAIR), lambda i: (pair_of(i), far_first(i), 0))
     kept = pl.BlockSpec((1, 2 * rows, 2 * rows), lambda i: (pair_of(i), 0, far_first(i)))
-    up_shape = (2, 2, 2, 2, unit_rows, hidden_parts * columns)
-    down_shape = (2, 2, 2, hidden_parts, 2, unit_rows, columns)
     grad_patches, total, vector_total, specials = pl.pallas_call(
         partial(backward_kernel, chunks, slots, pairs),
         grid=(2 * pairs + 1,),
@@ -1311,16 +1550,16 @@
         ],
         in_specs=[SMEM, kept, own_heads, half_heads, half_heads, own_pair, own_pair, own_pair]
         + [VMEM] * 6
-        + [ANY] * 10,
+        + [ANY] * 8,
         out_specs=[VMEM, ANY, VMEM, VMEM],
         scratch_shapes=chunk_scratch(count, unit_rows, columns)
         + vector_scratch()
         + [
             pltpu.VMEM((count, 2, 2, unit_rows, columns), BF16),
+            pltpu.VMEM((2 * hidden_parts,) + unit, BF16),
             pltpu.VMEM(unit, BF16),
             pltpu.VMEM((3,) + unit, BF16),
             pltpu.VMEM((3,) + unit, BF16),
-            pltpu.VMEM((2,) + unit, BF16),
             pltpu.VMEM((pairs, rows, PAIR), F32),
             pltpu.VMEM((pairs, rows, PAIR), BF16),
             pltpu.VMEM((pairs, every, PAIR), BF16),
@@ -1335,7 +1574,7 @@
             pltpu.VMEM((BANDS, 8, width), F32),
             pltpu.SemaphoreType.DMA((10 * count,)),
             pltpu.SemaphoreType.DMA((10 * count,)),
-            pltpu.SemaphoreType.DMA((count, 2, 2)),
+            pltpu.SemaphoreType.DMA((count, 2)),
             pltpu.SemaphoreType.DMA((5,)),
         ],
         compiler_params=pltpu.CompilerParams(
@@ -1357,10 +1596,7 @@
         g["down_bias_grad"],
         g["up_bias_grad"],
         g["out_own"],
-        g["up_keep"].reshape(up_shape),
-        g["up_got"].reshape(up_shape),
-        g["down_keep"].reshape(down_shape),
-        g["down_got"].reshape(down_shape),
+        *g["mlp_grads"],
         g["out_keep"].reshape(unit),
         g["out_send"].reshape(unit),
         g["firsts_t"],
@@ -1498,6 +1734,140 @@
         name="attend",
     )(info, queries, keys, values, firsts)
     return tokens, queries, keys, values, attended, totals, weights, firsts_t
+
+
+def middle_general(
+    info,
+    attended,
+    tokens,
+    out_weight,
+    out_bias,
+    first_scale,
+    second_gain,
+    second_shift,
+    second_scale,
+    cot_patches,
+    cot_specials,
+    down_bias,
+    up_weight,
+    up_bias,
+    down_weight,
+):
+    rows, width = tokens.shape
+    slots = cot_patches.shape[0]
+    hidden_width = up_weight.shape[1]
+    pad = rows - slots
+    shaped = jax.ShapeDtypeStruct
+    branch, middle, second, incoming, down_in, down_keep, down_send, down_bias_grad = pl.pallas_call(
+        partial(middle_kernel, slots),
+        out_shape=[
+            shaped((rows, width), F32),
+            shaped((rows, width), F32),
+            shaped((rows, width), BF16),
+            shaped((rows, width), F32),
+            shaped((rows, width), BF16),
+            shaped((rows, width // 2), BF16),
+            shaped((rows, width // 2), BF16),
+            shaped((1, width), F32),
+        ],
+        in_specs=[SMEM] + [VMEM] * 10,
+        out_specs=[VMEM] * 8,
+        compiler_params=params(),
+        name="middle",
+    )(
+        info,
+        attended,
+        tokens,
+        out_weight,
+        out_bias,
+        first_scale,
+        second_gain,
+        second_shift,
+        second_scale,
+        cot_patches,
+        cot_specials,
+    )
+
+    steps = hidden_width // width
+    half = width // 2
+    (
+        branch_two,
+        second_grad,
+        up_keep,
+        up_send,
+        up_bias_grad,
+        down_grad_keep,
+        down_grad_send,
+    ) = pl.pallas_call(
+        mlp_kernel,
+        grid=(steps,),
+        out_shape=[
+            shaped((rows, width), F32),
+            shaped((rows, width), F32),
+            shaped((width, hidden_width // 2), BF16),
+            shaped((width, hidden_width // 2), BF16),
+            shaped((1, hidden_width), F32),
+            shaped((hidden_width, half), BF16),
+            shaped((hidden_width, half), BF16),
+        ],
+        in_specs=[
+            SMEM,
+            whole((rows, width)),
+            whole((rows, width)),
+            whole((rows, half)),
+            whole((rows, half)),
+            pl.BlockSpec((width, width), lambda i: (0, i)),
+            pl.BlockSpec((1, width), lambda i: (0, i)),
+            pl.BlockSpec((width, width), lambda i: (i, 0)),
+        ],
+        out_specs=[
+            whole((rows, width)),
+            whole((rows, width)),
+            pl.BlockSpec((width, half), lambda i: (0, i)),
+            pl.BlockSpec((width, half), lambda i: (0, i)),
+            pl.BlockSpec((1, width), lambda i: (0, i)),
+            pl.BlockSpec((width, half), lambda i: (i, 0)),
+            pl.BlockSpec((width, half), lambda i: (i, 0)),
+        ],
+        compiler_params=params(),
+        name="mlp",
+    )(info, second, down_in, down_keep, down_send, up_weight, up_bias, down_weight)
+    up_got = swap(up_send, "band", 1)
+    down_got = swap(down_grad_send, "band", 1)
+
+    out_patches, out_own, middle_grad, attended_grad, out_keep, out_send, vectors = pl.pallas_call(
+        partial(middle_back_kernel, slots),
+        out_shape=[
+            shaped((slots, width), BF16),
+            shaped((pad, width), F32),
+            shaped((rows, width), F32),
+            shaped((rows, width), F32),
+            shaped((width, half), BF16),
+            shaped((width, half), BF16),
+            shaped((8, width), F32),
+        ],
+        in_specs=[SMEM] + [VMEM] * 11,
+        out_specs=[VMEM] * 7,
+        compiler_params=params(),
+        name="middle_back",
+    )(
+        info,
+        middle,
+        branch,
+        branch_two,
+        second_grad,
+        incoming,
+        attended,
+        out_weight,
+        down_bias,
+        second_scale,
+        second_gain,
+        first_scale,
+    )
+
+    shared = (out_patches, out_own, middle_grad, attended_grad, out_keep, out_send, vectors)
+    halves = dict(up_keep=up_keep, up_got=up_got, down_keep=down_grad_keep, down_got=down_got)
+    return shared + (down_bias_grad, up_bias_grad, halves)
 
 
 def body(
@@ -1557,23 +1927,19 @@
         rows,
     )
 
-    branch, middle, second, incoming, down_in, down_keep, down_send, down_bias_grad = pl.pallas_call(
-        partial(middle_kernel, slots),
-        out_shape=[
-            shaped((rows, width), F32),
-            shaped((rows, width), F32),
-            shaped((rows, width), BF16),
-            shaped((rows, width), F32),
-            shaped((rows, width), BF16),
-            shaped((rows, width // 2), BF16),
-            shaped((rows, width // 2), BF16),
-            shaped((1, width), F32),
-        ],
-        in_specs=[SMEM] + [VMEM] * 10,
-        out_specs=[VMEM] * 8,
-        compiler_params=params(),
-        name="middle",
-    )(
+    middle = middle_fused if lax.axis_size("crop") == CROPS else middle_general
+    (
+        out_patches,
+        out_own,
+        middle_grad,
+        attended_grad,
+        out_keep,
+        out_send,
+        vectors,
+        down_bias_grad,
+        up_bias_grad,
+        mlp_grads,
+    ) = middle(
         info,
         attended,
         tokens,
@@ -1585,85 +1951,11 @@
         second_scale,
         cot_patches,
         cot_specials,
+        down_bias,
+        up_weight,
+        up_bias.reshape(1, -1),
+        down_weight,
     )
-
-    steps = hidden_width // width
-    half = width // 2
-    (
-        branch_two,
-        second_grad,
-        up_keep,
-        up_send,
-        up_bias_grad,
-        down_grad_keep,
-        down_grad_send,
-    ) = pl.pallas_call(
-        mlp_kernel,
-        grid=(steps,),
-        out_shape=[
-            shaped((rows, width), F32),
-            shaped((rows, width), F32),
-            shaped((width, hidden_width // 2), BF16),
-            shaped((width, hidden_width // 2), BF16),
-            shaped((1, hidden_width), F32),
-            shaped((hidden_width, half), BF16),
-            shaped((hidden_width, half), BF16),
-        ],
-        in_specs=[
-            SMEM,
-            whole((rows, width)),
-            whole((rows, width)),
-            whole((rows, half)),
-            whole((rows, half)),
-            pl.BlockSpec((width, width), lambda i: (0, i)),
-            pl.BlockSpec((1, width), lambda i: (0, i)),
-            pl.BlockSpec((width, width), lambda i: (i, 0)),
-        ],
-        out_specs=[
-            whole((rows, width)),
-            whole((rows, width)),
-            pl.BlockSpec((width, half), lambda i: (0, i)),
-            pl.BlockSpec((width, half), lambda i: (0, i)),
-            pl.BlockSpec((1, width), lambda i: (0, i)),
-            pl.BlockSpec((width, half), lambda i: (i, 0)),
-            pl.BlockSpec((width, half), lambda i: (i, 0)),
-        ],
-        compiler_params=params(),
-        name="mlp",
-    )(info, second, down_in, down_keep, down_send, up_weight, up_bias.reshape(1, -1), down_weight)
-    up_got = swap(up_send, "band", 1)
-    down_got = swap(down_grad_send, "band", 1)
-
-    out_patches, out_own, middle_grad, attended_grad, out_keep, out_send, vectors = pl.pallas_call(
-        partial(middle_back_kernel, slots),
-        out_shape=[
-            shaped((slots, width), BF16),
-            shaped((pad, width), F32),
-            shaped((rows, width), F32),
-            shaped((rows, width), F32),
-            shaped((width, half), BF16),
-            shaped((width, half), BF16),
-            shaped((8, width), F32),
-        ],
-        in_specs=[SMEM] + [VMEM] * 11,
-        out_specs=[VMEM] * 7,
-        compiler_params=params(),
-        name="middle_back",
-    )(
-        info,
-        middle,
-        branch,
-        branch_two,
-        second_grad,
-        incoming,
-        attended,
-        out_weight,
-        down_bias,
-        second_scale,
-        second_gain,
-        first_scale,
-    )
-
     given = dict(
         info=info,
         weights=weights,
@@ -1679,10 +1971,7 @@
         down_bias_grad=down_bias_grad,
         up_bias_grad=up_bias_grad,
         out_own=out_own,
-        up_keep=up_keep,
-        up_got=up_got,
-        down_keep=down_grad_keep,
-        down_got=down_got,
+        mlp_grads=mlp_grads,
         out_keep=out_keep,
         out_send=out_send,
         firsts_t=firsts_t,

time: 172 us -> 163 us (0.948)
  Pallas kernels: 163 us -> 155 us
    pallas_call x3 -> x1, Pallas kernels: 34 us -> 27 us  [middle_fused(): pl.pallas_call(partial(middle_all_kernel, chunks, slots, parts), grid=(2...]
  transfers between devices with their start and end apart: 2 -> 0, of which waited for: 0 -> 0; matrix products, arithmetic and copies ran while one was open for 0% -> 0% of each run, Pallas kernels for 5% -> 0%
where the time goes in v3:
time: 163 us
  Pallas kernels  155 us (95%)
  local copies, waits for them, and re-layouts  4.01 us (2%)
  between operations  3.38 us (2%)
    pallas_call x1, Pallas kernels, backward_fused(): pl.pallas_call(partial(backward_kernel, chunks, slots, pairs), grid=(2 *...  91 us
    pallas_call x1, Pallas kernels, forward_fused(): pl.pallas_call(partial(forward_kernel, slots, pairs), grid=(2 * pairs,),...  33.8 us
    pallas_call x1, Pallas kernels, middle_fused(): pl.pallas_call(partial(middle_all_kernel, chunks, slots, parts), grid=(2...  27 us
    pallas_call x1, Pallas kernels, backward_fused(): pl.pallas_call(partial(finish_kernel, chunks, special_count), out_shape=[...  3.43 us

profile of v3, /device:TPU:1, one launch (start us, length us, event | category | flops | bytes accessed | tf_op | source)
XLA Modules:
  0.0 162.6 jit_solution(8312291073558530197)
XLA Ops:
  0.7 1.4 fusion
  4.8 0.6 stack.27.info
  5.4 33.8 %forward.1 = (f32[448,768]{1,0:T(8,128)}, bf16[6,448,128]{2,1,0:T(8,128)(2,1)}, bf16[6,1792,128]{2,1,0:T(8,128)(2,1)}, bf16[6,1792,128]{2,1,0:T(8,128)(2,1)}, f3...) custom-call(s32[9]{0:T(128)} %stack.27.info, ...), custom_call_target="tpu_custom_call" | custom-call | tf_op jit(solution)/shard_map/forward/pallas_call | solution.py:1638
  39.2 27.0 %middle_all.1 = (bf16[444,768]{1,0:T(8,128)(2,1)}, f32[4,768]{1,0:T(4,128)}, f32[448,768]{1,0:T(8,128)}, f32[448,768]{1,0:T(8,128)}, bf16[768,384]{1,0:T(8,128)(...) custom-call(s32[9]{0:T(128)} %stack.27.info, ...), custom_call_target="tpu_custom_call" | custom-call | tf_op jit(solution)/shard_map/middle_all/pallas_call | solution.py:1143
  66.2 91.0 %backward.1 = (bf16[444,768]{1,0:T(8,128)(2,1)}, bf16[12,2,2,48,384]{4,3,2,1,0:T(8,128)(2,1)}, f32[16,128]{1,0:T(8,128)}, f32[4,8,768]{2,1,0:T(8,128)}) custom-call(s32[9]{0:T(128)} %stack.27.info, bf16[6,896,1792]{2,1,0:T(8,128)(2,1)} %get-tuple-element.64.weights, bf16[6,448,128]{2,1,0:T(8,128)(2,1)} %get-tuple-element.65.queries, ...), custom_call_target="tpu_custom_call" | custom-call | tf_op jit(solution)/shard_map/backward/pallas_call | solution.py:1542
  157.2 3.4 %finish.1 = (f32[96,3072]{1,0:T(8,128)}, f32[384,768]{1,0:T(8,128)}, f32[96,768]{1,0:T(8,128)}, f32[96,2304]{1,0:T(8,128)}, f32[384]{0:T(512)}, /*index=5*/bf16[...) custom-call(bf16[12,2,2,48,384]{4,3,2,1,0:T(8,128)(2,1)} %get-tuple-, ...), custom_call_target="tpu_custom_call" | custom-call | tf_op jit(solution)/shard_map/finish/pallas_call | solution.py:1608
  160.6 2.0 %copy.43 = bf16[1,444,768]{2,1,0:T(8,128)(2,1)} copy(bf16[1,444,768]{2,1,0:T(8,128)(2,1)} %bitcast.15) | data formatting | bytes 1363968

commit v4 on v3

--- a/solution.py
+++ b/solution.py
@@ -11,6 +11,8 @@
 GRID = 37
 PAIR = 2 * HEAD
 BANDS = 4
+SPECIALS = 5
+ROW_PART = 64
 KEY_PART = 256
 F32 = jnp.float32
 BF16 = jnp.bfloat16
@@ -85,11 +87,19 @@
     ref[slots:rows, :] = jnp.concatenate(extra, axis=0)
 
 
-def counted_rows(info_ref, relative, rows, slots, width):
+def block_counts(band_rows, relative):
+    band = lax.axis_index("band")
+    core, x = lax.rem(band, 2), lax.div(band, 2)
+    core = core + lax.rem(relative, 2) * (1 - 2 * core)
+    x = x + lax.div(relative, 2) * (1 - 2 * x)
+    owner = 2 * x + core
+    return band_rows[owner] * GRID, lax.div(SPECIALS - owner + BANDS - 1, BANDS)
+
+
+def counted_rows(band_rows, relative, rows, slots, width):
+    used, specials = block_counts(band_rows, relative)
     index = lax.broadcasted_iota(jnp.int32, (rows, width), 0)
-    used = index < info_ref[relative]
-    special = (index >= slots) & (index < slots + info_ref[BANDS + relative])
-    return used | special
+    return (index < used) | ((index >= slots) & (index < slots + specials))
 
 
 def stack_pair(rows):
@@ -111,7 +121,7 @@
 
 
 def first_kernel(slots, info, mask, patches, specials, token, gain, shift, tokens, first):
-    band = info[2 * BANDS]
+    band = lax.axis_index("band")
     filled = jnp.where(mask_column(mask), line(token), patches[...].astype(F32))
     place_rows(tokens, filled, specials[...].astype(F32), band)
     hat, _ = normalize(tokens[...])
@@ -307,7 +317,7 @@
     down_bias_grad,
 ):
     rows = tokens.shape[0]
-    band = info[2 * BANDS]
+    band = lax.axis_index("band")
     side = dot(attended[...].astype(BF16), weight[...]) + line(bias)
     branch[...] = side
     mid = tokens[...] + line(first_scale) * side
@@ -369,7 +379,7 @@
 
     branch_two[...] += dot(active, down[...])
     second_grad[...] += dot_nt(hidden_in, up[...])
-    keep, send = own_half(hidden_in, info[2 * BANDS])
+    keep, send = own_half(hidden_in, lax.axis_index("band"))
     up_grad_send[...] = dot_tn(low, send).astype(BF16)
     up_grad_keep[...] = dot_tn(low, keep).astype(BF16)
     down_grad_send[...] = dot_tn(active, down_send[...]).astype(BF16)
@@ -415,7 +425,7 @@
     out_in = (back * line(first_scale)).astype(BF16)
     attended_grad[...] = dot_nt(out_in, weight[...])
     between(1)
-    keep, send = own_half(out_in, info[2 * BANDS])
+    keep, send = own_half(out_in, lax.axis_index("band"))
     low = attended[...].astype(BF16)
     out_keep[...] = dot_tn(low, keep).astype(BF16)
     out_send[...] = dot_tn(low, send).astype(BF16)
@@ -433,7 +443,7 @@
     )
 
 
-def attend_back_pair(weights, queries, keys, values, attended, totals, attended_grad, outs, between):
+def attend_back_pair(weights, queries, keys, values, attended, totals, attended_grad, outs):
     key_grad, value_grad = outs
     queries, keys, values = queries.at[0], keys.at[0], values.at[0]
     rows = queries.shape[0]
@@ -446,7 +456,7 @@
     returned_t = returned.astype(F32).T.astype(BF16)
     total = jnp.zeros((2 * rows, PAIR), F32)
     start = 0
-    for part, size in enumerate(key_parts(keys.shape[0])):
+    for size in key_parts(keys.shape[0]):
         span = slice(start, start + size)
         start += size
         low = weights[0, :, span]
@@ -455,7 +465,6 @@
         total = total + dot(scores, keys[span, :])
         key_grad[span, :] = dot(stacked_t, scores).T.astype(BF16)
         value_grad[span, :] = dot(returned_t, low).T.astype(BF16)
-        between(part)
     return unstack_pair(total) * factor
 
 
@@ -497,20 +506,28 @@
     return results
 
 
-def first_back(slots, info, grad, tokens, middle_grad, mask, gain):
+def first_back(slots, info, grad, tokens, middle_grad, mask, gain, patches, between=lambda part: None):
     rows, width = tokens.shape
-    grad = jnp.where(counted_rows(info, 0, rows, slots, width), grad, 0.0)
-    hat, scale = normalize(tokens[...])
-    token_grad = middle_grad[...] + normalize_back(grad * line(gain), hat, scale)
     masked = mask_column(mask)
-    patch_grad = token_grad[:slots]
-    patches = jnp.where(masked, 0.0, patch_grad).astype(BF16)
-    vectors = [
-        column_sum(jnp.where(masked, patch_grad, 0.0)),
-        column_sum(grad * hat),
-        column_sum(grad),
-    ]
-    return patches, token_grad[slots:], vectors
+    counted = counted_rows(info, 0, rows, slots, width)
+    sums = None
+    for part, start in enumerate(range(0, rows, ROW_PART)):
+        at = slice(start, start + ROW_PART)
+        some = jnp.where(counted[at], grad[at], 0.0)
+        hat, scale = normalize(tokens[at, :])
+        token_grad = middle_grad[at, :] + normalize_back(some * line(gain), hat, scale)
+        end = min(start + ROW_PART, slots)
+        hidden = masked[start:end]
+        patch_grad = token_grad[: end - start]
+        patches[start:end, :] = jnp.where(hidden, 0.0, patch_grad).astype(BF16)
+        terms = [
+            column_sum(jnp.where(hidden, patch_grad, 0.0)),
+            column_sum(some * hat),
+            column_sum(some),
+        ]
+        sums = terms if sums is None else [x + y for x, y in zip(sums, terms)]
+        between(part)
+    return token_grad[slots - start :], sums
 
 
 def bias_sums(info, slots, rows, query_grad, value_grad):
@@ -596,7 +613,7 @@
     weights, queries, keys, values, attended, totals, attended_grad, query_grad, key_grad, value_grad
 ):
     inputs = (weights, queries, keys, values, attended, totals, attended_grad)
-    part = attend_back_pair(*inputs, (key_grad.at[0], value_grad.at[0]), lambda part: None)
+    part = attend_back_pair(*inputs, (key_grad.at[0], value_grad.at[0]))
     query_grad[0] = part.astype(BF16)
 
 
@@ -610,7 +627,7 @@
     third = 3 * PAIR
     for part in range(query_grad.shape[0] // 2):
         keep, send = joint_columns(
-            firsts_t, query_grad, key_grad, value_grad, own_pair_first(part, info[2 * BANDS])
+            firsts_t, query_grad, key_grad, value_grad, own_pair_first(part, lax.axis_index("band"))
         )
         joint_keep[:, part * third : (part + 1) * third] = keep
         joint_send[:, part * third : (part + 1) * third] = send
@@ -620,10 +637,9 @@
 def first_back_kernel(
     slots, info, first_grad, tokens, middle_grad, mask, gain, sums, patches, specials, vectors
 ):
-    grads, special_grad, rows = first_back(
-        slots, info, first_grad[...], tokens, middle_grad, mask, gain
+    special_grad, rows = first_back(
+        slots, info, first_grad[...], tokens, middle_grad, mask, gain, patches
     )
-    patches[...] = grads
     specials[...] = special_grad
     vectors[...] = jnp.concatenate(rows + [sums[0:5]], axis=0)
 
@@ -728,8 +744,8 @@
 
 MESH = pl.DeviceIdType.MESH
 CROPS = 8
-X_FIRST = (1, 3, 5, 7, 8, 9)
-DIRECT = (9, 10, 11)
+X_FIRST = (1, 3, 5, 7, 9, 10)
+DIRECT = (11,)
 NEIGHBOURS = ("core", "x", "diagonal")
 PLACES = NEIGHBOURS + tuple(range(1, CROPS))
 
@@ -1203,19 +1219,19 @@
 
 
 PLAN = (
-    (2, 1, 0), (2, 0, 0), (3, 3, 0), (4, 2, 0), (9, 5, 0), (9, 4, 0),
-    (10, 1, 1), (10, 0, 1), (14, 7, 0), (16, 0, 2), (16, 3, 1), (16, 2, 1),
-    (18, 6, 0), (18, 8, 0), (18, 0, 3), (19, 5, 1), (19, 4, 1), (19, 2, 2),
-    (22, 1, 2), (24, 4, 2), (24, 7, 1), (24, 3, 2), (24, 2, 3), (25, 1, 3),
-    (26, 9, 0), (28, 8, 1), (28, 6, 1), (28, 3, 3), (28, 4, 3), (29, 0, 4),
-    (29, 1, 4), (30, 5, 2), (30, 0, 5), (31, 6, 2), (31, 7, 2), (31, 3, 4),
-    (32, 10, 0), (33, 5, 3), (33, 8, 2), (36, 6, 3), (36, 7, 3), (36, 5, 4),
-    (37, 8, 3), (38, 11, 0), (38, 10, 1), (39, 2, 4), (39, 7, 4), (40, 8, 4),
-    (40, 2, 5), (40, 10, 2), (40, 9, 1), (44, 4, 4), (44, 11, 1), (45, 1, 5),
-    (47, 3, 5), (48, 6, 4), (49, 4, 5), (50, 5, 5), (51, 10, 3), (52, 9, 2),
-    (53, 1, 6), (54, 7, 5), (55, 3, 6), (56, 8, 5), (57, 6, 5), (58, 11, 2),
-    (59, 5, 6), (60, 7, 6), (61, 9, 3), (62, 8, 6), (63, 10, 4), (64, 11, 3),
-    (65, 9, 4), (66, 11, 4), (67, 9, 5),
+    (0, 1, 0), (0, 0, 0), (1, 3, 0), (1, 2, 0), (1, 5, 0), (1, 4, 0),
+    (2, 7, 0), (2, 6, 0), (3, 8, 0), (3, 1, 1), (3, 0, 1), (5, 0, 2),
+    (5, 3, 1), (5, 2, 1), (6, 0, 3), (7, 2, 2), (7, 5, 1), (7, 4, 1),
+    (8, 7, 1), (8, 2, 3), (8, 6, 1), (8, 9, 0), (9, 0, 4), (9, 4, 2),
+    (10, 6, 2), (10, 0, 5), (10, 8, 1), (10, 10, 0), (10, 4, 3), (11, 1, 2),
+    (12, 3, 2), (12, 6, 3), (13, 8, 2), (14, 5, 2), (14, 1, 3), (14, 11, 0),
+    (14, 3, 3), (14, 2, 4), (16, 7, 2), (17, 8, 3), (17, 2, 5), (17, 5, 3),
+    (18, 1, 4), (20, 3, 4), (20, 7, 3), (20, 9, 1), (21, 5, 4), (21, 11, 1),
+    (23, 7, 4), (24, 9, 2), (25, 10, 1), (26, 11, 2), (27, 4, 4), (28, 9, 3),
+    (29, 6, 4), (30, 4, 5), (31, 10, 2), (32, 8, 4), (33, 11, 3), (34, 1, 5),
+    (35, 6, 5), (36, 3, 5), (37, 9, 4), (38, 5, 5), (39, 8, 5), (40, 10, 3),
+    (41, 7, 5), (42, 1, 6), (43, 3, 6), (44, 5, 6), (45, 7, 6), (46, 10, 4),
+    (47, 11, 4), (48, 9, 5), (49, 10, 5), (50, 9, 6), (51, 10, 6),
 )
 
 
@@ -1374,15 +1390,15 @@
         sender.send((n, 0))
 
     half_rows = 2 * rows
-    per_step = len(key_parts(half_rows))
-
-    def between(part):
-        for index in range(2 * pairs):
-            if occupied(index * per_step + part):
-
-                @pl.when(step == index)
+    per_step = 1
+
+    def between(index):
+        for i in range(2 * pairs):
+            if occupied(i):
+
+                @pl.when(index == i)
                 def _():
-                    exchanges(index * per_step + part)
+                    exchanges(i)
 
     grads = (query_grad, key_grad, value_grad)
     last = 2 * pairs
@@ -1425,7 +1441,8 @@
         span = pl.ds(first_row, half_rows)
         outs = (key_grad.at[pair, span], value_grad.at[pair, span])
         inputs = (weights, queries, keys, values, attended, totals, attended_grad)
-        part = attend_back_pair(*inputs, outs, between)
+        part = attend_back_pair(*inputs, outs)
+        between(step)
 
         @pl.when(far_half)
         def _():
@@ -1445,25 +1462,36 @@
         first_grad = first_part(0, rows, *grads, weight)
         exchanges(after + 2)
         biases = bias_sums(info, slots, rows, query_grad, value_grad)
+        exchanges(after + 3)
         sender.arrived(("first", 0))
         sender.arrived("far")
         first_grad = first_grad + got_parts[0].astype(F32) + got_far[...].astype(F32)
-        exchanges(after + 3)
-        patches, special_grad, rows_of = first_back(
-            slots, info, first_grad, tokens, middle_grad, mask, gain
+        special_grad, rows_of = first_back(
+            slots,
+            info,
+            first_grad,
+            tokens,
+            middle_grad,
+            mask,
+            gain,
+            grad_patches,
+            lambda part: exchanges(after + 4 + part),
         )
-        grad_patches[...] = patches
         specials[place.band] = jnp.concatenate([out_own[0:4], special_grad[0:4]], axis=0)
         for name in NEIGHBOURS:
             sender.send(("special", name))
         packed = jnp.concatenate([vectors[0:5]] + rows_of + [biases[0:2], down_bias[...]], axis=0)
         pack_vectors(vector_sums.own, packed, up_bias, width // CROPS)
         vector_sums.spread()
-        for slot in range(after + 4, max(entry[0] for entry in PLAN) + 1):
+        ends = max(entry[0] for entry in PLAN) + 1
+        start = after + 4 + rows // ROW_PART
+        shared = min(start + 5, ends - 1)
+        closed = min(start + 12, ends - 1)
+        for slot in range(start, ends):
             exchanges(slot)
-            if slot == after + 7:
+            if slot == shared:
                 vector_sums.share()
-            if slot == after + 15:
+            if slot == closed:
                 vector_sums.close()
         for name in NEIGHBOURS:
             sender.arrived(("special", name))
@@ -1480,6 +1508,7 @@
     total,
     vector_total,
     specials,
+    grad_patches,
     up,
     down,
     out,
@@ -1487,8 +1516,10 @@
     up_bias,
     out_specials,
     grad_specials,
+    grad_patches_out,
     *vectors,
 ):
+    grad_patches_out[...] = grad_patches[...]
     _, _, _, rows, columns = total.shape
     refs = dict(up=up, down=down, out=out, joint=joint)
     for n, (name, part) in enumerate(chunks):
@@ -1615,15 +1646,16 @@
             shaped((hidden_width // CROPS,), F32),
             special,
             special,
+            shaped((slots, width), BF16),
         ]
         + [shaped((part,), F32)] * 11,
-        in_specs=[VMEM] * 3,
-        out_specs=[VMEM] * 18,
+        in_specs=[VMEM] * 4,
+        out_specs=[VMEM] * 19,
         compiler_params=params(),
         name="finish",
-    )(total, vector_total, specials)
-    up, down, out, joint, up_bias, out_specials, grad_specials = results[:7]
-    return grad_patches, up, down, out, joint, results[7:], up_bias, out_specials, grad_specials
+    )(total, vector_total, specials, grad_patches)
+    up, down, out, joint, up_bias, out_specials, grad_specials, grad_patches = results[:8]
+    return grad_patches, up, down, out, joint, results[8:], up_bias, out_specials, grad_specials
 
 
 def forward_fused(
@@ -1900,13 +1932,7 @@
     owned = -(-special_count // BANDS)
     rows = round_up(slots + owned, 16)
     pad = rows - slots
-    band = lax.axis_index("band")
-    relatives = [band ^ r for r in range(BANDS)]
-    info = jnp.stack(
-        [band_rows[b] * GRID for b in relatives]
-        + [(special_count - b + BANDS - 1) // BANDS for b in relatives]
-        + [band]
-    ).astype(jnp.int32)
+    info = band_rows
     mask = patch_mask
     patches, specials = patches[0], specials[0]
     cot_patches, cot_specials = cot_patches[0], cot_specials[0]

time: 163 us -> 154 us (0.945)
  local copies, waits for them, and re-layouts: 4.01 us -> 0 us
  between operations: 3.38 us -> 0.86 us
  Pallas kernels: 155 us -> 153 us
    pallas_call x1, Pallas kernels: 91 us -> 88.4 us  [backward_fused(): pl.pallas_call(partial(backward_kernel, chunks, slots, pairs), grid=(2 *...]
    unnamed x1 -> x0, local copies, waits for them, and re-layouts: 1.99 us -> none
where the time goes in v4:
time: 154 us
  Pallas kernels  153 us (99%)
    pallas_call x1, Pallas kernels, backward_fused(): pl.pallas_call(partial(backward_kernel, chunks, slots, pairs), grid=(2 *...  88.4 us
    pallas_call x1, Pallas kernels, forward_fused(): pl.pallas_call(partial(forward_kernel, slots, pairs), grid=(2 * pairs,),...  33.8 us
    pallas_call x1, Pallas kernels, middle_fused(): pl.pallas_call(partial(middle_all_kernel, chunks, slots, parts), grid=(2...  27 us
    pallas_call x1, Pallas kernels, backward_fused(): pl.pallas_call(partial(finish_kernel, chunks, special_count), out_shape=[...  3.84 us

profile of v4, /device:TPU:1, one launch (start us, length us, event | category | flops | bytes accessed | tf_op | source)
XLA Modules:
  0.0 153.9 jit_solution(17692439389639446519)
XLA Ops:
  0.7 33.8 %forward.1 = (f32[448,768]{1,0:T(8,128)}, bf16[6,448,128]{2,1,0:T(8,128)(2,1)}, bf16[6,1792,128]{2,1,0:T(8,128)(2,1)}, bf16[6,1792,128]{2,1,0:T(8,128)(2,1)}, f3...) custom-call(s32[4]{0:T(128)} %info.5, s32[1,444]{1,0:T(1,128)} %mask.3, ...), custom_call_target="tpu_custom_call" | custom-call | tf_op jit(solution)/shard_map/forward/pallas_call | solution.py:1670
  34.5 27.0 %middle_all.1 = (bf16[444,768]{1,0:T(8,128)(2,1)}, f32[4,768]{1,0:T(4,128)}, f32[448,768]{1,0:T(8,128)}, f32[448,768]{1,0:T(8,128)}, bf16[768,384]{1,0:T(8,128)(...) custom-call(s32[4]{0:T(128)} %info.5, ...), custom_call_target="tpu_custom_call" | custom-call | tf_op jit(solution)/shard_map/middle_all/pallas_call | solution.py:1159
  61.5 88.4 %backward.1 = (bf16[444,768]{1,0:T(8,128)(2,1)}, bf16[12,2,2,48,384]{4,3,2,1,0:T(8,128)(2,1)}, f32[16,128]{1,0:T(8,128)}, f32[4,8,768]{2,1,0:T(8,128)}) custom-call(s32[4]{0:T(128)} %info.5, bf16[6,896,1792]{2,1,0:T(8,128)(2,1)} %get-tuple-element.65.weights, bf16[6,448,128]{2,1,0:T(8,128)(2,1)} %get-tuple-element.66.queries, ...), custom_call_target="tpu_custom_call" | custom-call | tf_op jit(solution)/shard_map/backward/pallas_call | solution.py:1573
  149.9 3.8 %finish.1 = (f32[96,3072]{1,0:T(8,128)}, f32[384,768]{1,0:T(8,128)}, f32[96,768]{1,0:T(8,128)}, f32[96,2304]{1,0:T(8,128)}, f32[384]{0:T(512)}, /*index=5*/bf16[...) custom-call(bf16[12,2,2,48,384]{4,3,2,1,0:T(8,128)(2,1)} %get-tuple-, ...), custom_call_target="tpu_custom_call" | custom-call | tf_op jit(solution)/shard_map/finish/pallas_call | solution.py:1639

commit v5 on v4

--- a/solution.py
+++ b/solution.py
@@ -744,7 +744,7 @@
 
 MESH = pl.DeviceIdType.MESH
 CROPS = 8
-X_FIRST = (1, 3, 5, 7, 9, 10)
+X_FIRST = (1, 3, 5, 7, 11)
 DIRECT = (11,)
 NEIGHBOURS = ("core", "x", "diagonal")
 PLACES = NEIGHBOURS + tuple(range(1, CROPS))
@@ -1220,18 +1220,18 @@
 
 PLAN = (
     (0, 1, 0), (0, 0, 0), (1, 3, 0), (1, 2, 0), (1, 5, 0), (1, 4, 0),
-    (2, 7, 0), (2, 6, 0), (3, 8, 0), (3, 1, 1), (3, 0, 1), (5, 0, 2),
-    (5, 3, 1), (5, 2, 1), (6, 0, 3), (7, 2, 2), (7, 5, 1), (7, 4, 1),
-    (8, 7, 1), (8, 2, 3), (8, 6, 1), (8, 9, 0), (9, 0, 4), (9, 4, 2),
-    (10, 6, 2), (10, 0, 5), (10, 8, 1), (10, 10, 0), (10, 4, 3), (11, 1, 2),
-    (12, 3, 2), (12, 6, 3), (13, 8, 2), (14, 5, 2), (14, 1, 3), (14, 11, 0),
-    (14, 3, 3), (14, 2, 4), (16, 7, 2), (17, 8, 3), (17, 2, 5), (17, 5, 3),
-    (18, 1, 4), (20, 3, 4), (20, 7, 3), (20, 9, 1), (21, 5, 4), (21, 11, 1),
-    (23, 7, 4), (24, 9, 2), (25, 10, 1), (26, 11, 2), (27, 4, 4), (28, 9, 3),
-    (29, 6, 4), (30, 4, 5), (31, 10, 2), (32, 8, 4), (33, 11, 3), (34, 1, 5),
-    (35, 6, 5), (36, 3, 5), (37, 9, 4), (38, 5, 5), (39, 8, 5), (40, 10, 3),
-    (41, 7, 5), (42, 1, 6), (43, 3, 6), (44, 5, 6), (45, 7, 6), (46, 10, 4),
-    (47, 11, 4), (48, 9, 5), (49, 10, 5), (50, 9, 6), (51, 10, 6),
+    (3, 7, 0), (3, 6, 0), (3, 1, 1), (3, 0, 1), (5, 0, 2), (6, 8, 0),
+    (6, 3, 1), (6, 2, 1), (6, 0, 3), (7, 5, 1), (7, 4, 1), (8, 2, 2),
+    (8, 7, 1), (8, 9, 0), (8, 6, 1), (8, 4, 2), (9, 0, 4), (9, 1, 2),
+    (10, 2, 3), (10, 0, 5), (10, 6, 2), (10, 4, 3), (10, 10, 0), (11, 1, 3),
+    (11, 8, 1), (12, 3, 2), (12, 6, 3), (13, 1, 4), (14, 5, 2), (14, 11, 0),
+    (14, 8, 2), (14, 2, 4), (15, 3, 3), (16, 7, 2), (16, 4, 4), (17, 5, 3),
+    (17, 2, 5), (17, 6, 4), (17, 1, 5), (18, 8, 3), (18, 4, 5), (19, 3, 4),
+    (19, 6, 5), (19, 7, 3), (19, 1, 6), (20, 9, 1), (20, 5, 4), (22, 7, 4),
+    (22, 11, 1), (23, 8, 4), (24, 3, 5), (25, 9, 2), (26, 5, 5), (27, 10, 1),
+    (28, 7, 5), (29, 8, 5), (30, 3, 6), (31, 5, 6), (32, 7, 6), (33, 11, 2),
+    (34, 9, 3), (35, 10, 2), (36, 9, 4), (37, 11, 3), (38, 9, 5), (39, 10, 3),
+    (40, 11, 4), (41, 10, 4), (42, 11, 5), (43, 10, 5),
 )
 
 

time: 154 us -> 154 us (level)
  no operation moved by 1% of the time
where the time goes in v5:
time: 154 us; the launch traced here: 153 us
  Pallas kernels  153 us (99%)
    pallas_call x1, Pallas kernels, backward_fused(): pl.pallas_call(partial(backward_kernel, chunks, slots, pairs), grid=(2 *...  87.9 us
    pallas_call x1, Pallas kernels, forward_fused(): pl.pallas_call(partial(forward_kernel, slots, pairs), grid=(2 * pairs,),...  33.8 us
    pallas_call x1, Pallas kernels, middle_fused(): pl.pallas_call(partial(middle_all_kernel, chunks, slots, parts), grid=(2...  27 us
    pallas_call x1, Pallas kernels, backward_fused(): pl.pallas_call(partial(finish_kernel, chunks, special_count), out_shape=[...  3.84 us

profile of v5, /device:TPU:1, one launch (start us, length us, event | category | flops | bytes accessed | tf_op | source)
XLA Modules:
  0.0 153.4 jit_solution(14482557230136984889)
XLA Ops:
  0.7 33.8 %forward.1 = (f32[448,768]{1,0:T(8,128)}, bf16[6,448,128]{2,1,0:T(8,128)(2,1)}, bf16[6,1792,128]{2,1,0:T(8,128)(2,1)}, bf16[6,1792,128]{2,1,0:T(8,128)(2,1)}, f3...) custom-call(s32[4]{0:T(128)} %info.5, s32[1,444]{1,0:T(1,128)} %mask.3, ...), custom_call_target="tpu_custom_call" | custom-call | tf_op jit(solution)/shard_map/forward/pallas_call | solution.py:1670
  34.5 27.0 %middle_all.1 = (bf16[444,768]{1,0:T(8,128)(2,1)}, f32[4,768]{1,0:T(4,128)}, f32[448,768]{1,0:T(8,128)}, f32[448,768]{1,0:T(8,128)}, bf16[768,384]{1,0:T(8,128)(...) custom-call(s32[4]{0:T(128)} %info.5, ...), custom_call_target="tpu_custom_call" | custom-call | tf_op jit(solution)/shard_map/middle_all/pallas_call | solution.py:1159
  61.5 87.9 %backward.1 = (bf16[444,768]{1,0:T(8,128)(2,1)}, bf16[12,2,2,48,384]{4,3,2,1,0:T(8,128)(2,1)}, f32[16,128]{1,0:T(8,128)}, f32[4,8,768]{2,1,0:T(8,128)}) custom-call(s32[4]{0:T(128)} %info.5, bf16[6,896,1792]{2,1,0:T(8,128)(2,1)} %get-tuple-element.65.weights, bf16[6,448,128]{2,1,0:T(8,128)(2,1)} %get-tuple-element.66.queries, ...), custom_call_target="tpu_custom_call" | custom-call | tf_op jit(solution)/shard_map/backward/pallas_call | solution.py:1573
  149.4 3.8 %finish.1 = (f32[96,3072]{1,0:T(8,128)}, f32[384,768]{1,0:T(8,128)}, f32[96,768]{1,0:T(8,128)}, f32[96,2304]{1,0:T(8,128)}, f32[384]{0:T(512)}, /*index=5*/bf16[...) custom-call(bf16[12,2,2,48,384]{4,3,2,1,0:T(8,128)(2,1)} %get-tuple-, ...), custom_call_target="tpu_custom_call" | custom-call | tf_op jit(solution)/shard_map/finish/pallas_call | solution.py:1639
